TPU v7x, 256 devices: a whole 4x4x8 slice. The times are simulated.
256 devices in a mesh: tm: 32 (over z, x), ctx: 8 (over y, core).
Axes of the slice: x: 4, y: 4, z: 8, core: 2. Of those that a mesh axis runs over, the one named last changes fastest.
Arguments:
- frames: bfloat16 [4096, 1024], P('tm'), may hold values from -6 to 6
- value_weight: bfloat16 [1024, 1024], P(None, 'ctx'), may hold values from -0.1875 to 0.1875
- gate_weight: bfloat16 [1024, 1024], P(None, 'ctx'), may hold values from -0.1875 to 0.1875
- conv_taps: float32 [31, 1024], P(None, 'ctx'), may hold values from -1 to 1
- out_weight: bfloat16 [1024, 1024], P('ctx'), may hold values from -1 to 1
- adapter: bfloat16 [1024, 8192], P('tm', 'ctx'), may hold values from -0.1875 to 0.1875
- audio_pos: int32 [4096], replicated, may hold values from 0 to 16383, as said below
- text_rows: bfloat16 [16384, 8192], P('tm', 'ctx'), may hold values from -6 to 6
- value_proj: bfloat16 [8192, 4096], P('ctx', 'tm'), may hold values from -0.0625 to 0.0625
- queries: bfloat16 [16384, 4096], P(('tm', 'ctx')), may hold values from -12 to 12
- keys: bfloat16 [16384, 4096], P(('tm', 'ctx')), may hold values from -4 to 4
- grad_out: bfloat16 [16384, 4096], P(('tm', 'ctx')), may hold values from -6 to 6
- window_low: int32 [16384], P('tm'), may hold values from 0 to 16383, as said below
Outputs:
- d_keys: bfloat16 [16384, 4096], P('tm', 'ctx')
- d_hidden: bfloat16 [16384, 8192], P('tm', 'ctx')
Inputs may be any that keep to these rules, and one draw needn't show every extreme that they name: `audio_pos`: the positions are distinct. Of the audio rows r = t * 128 .. (t + 1) * 128 - 1 of one time block t, at most 8 land in one block of 512 consecutive positions, and exactly 8 land in some block. The audio rows that land in one block of 512 positions occupy consecutive positions, in the order of r. window_low[i] <= i - 1 for i >= 1, window_low[0] = 0, and i - window_low[i] <= 512, with equality for some i.
All inputs are finite; a program needn't handle non-finite values.
Results may differ from a plain program's by a relative error of at most 0.023.
Values may be sent and summed in bfloat16 or wider, within the bound.
A program may use at most 128 MiB of HBM per device.

v0:
```python
import math

import jax
import jax.numpy as jnp
from jax import lax
from jax.sharding import PartitionSpec as P

DH = 128


NORM_EPS = 1e-05
MASK_FILL = -1e30


def extended(value, sides, width):
    for axis, dim in sides:
        size, length = (lax.axis_size(axis), value.shape[dim])
        up = [(i, (i + 1) % size) for i in range(size - 1)]
        down = [(j, i) for i, j in up]
        last = lax.slice_in_dim(value, length - width, length, axis=dim)
        leading = lax.slice_in_dim(value, 0, width, axis=dim)
        before = lax.ppermute(last, axis, up)
        after = lax.ppermute(leading, axis, down)
        value = jnp.concatenate([before, value, after], axis=dim)
    return value


def passed_along(value, axis, by):
    size = lax.axis_size(axis)
    pairs = [(i, i + by) for i in range(size) if 0 <= i + by < size]
    return lax.ppermute(value, axis, pairs)


def encode_frames(frames, value_weight, gate_weight, conv_taps, out_weight):
    frame_rows = frames.shape[0]
    rows_float = frames.astype(jnp.float32)
    centre = jnp.mean(rows_float, axis=1, keepdims=True)
    offsets = rows_float - centre
    spread = jnp.mean(offsets * offsets, axis=1, keepdims=True)
    normed = (offsets * lax.rsqrt(spread + NORM_EPS)).astype(jnp.bfloat16)
    value_part = jnp.dot(normed, value_weight, preferred_element_type=jnp.float32)
    gate_part = jnp.dot(normed, gate_weight, preferred_element_type=jnp.float32)
    glu_rows = (value_part * jax.nn.sigmoid(gate_part)).astype(jnp.bfloat16)
    rim_width = (conv_taps.shape[0] - 1) // 2
    padded = extended(glu_rows, (("tm", 0),), rim_width).astype(jnp.float32)
    smooth = jnp.zeros(glu_rows.shape, jnp.float32)
    for offset in range(conv_taps.shape[0]):
        smooth = smooth + conv_taps[offset][None, :] * padded[offset : offset + frame_rows]
    action = (smooth * jax.nn.sigmoid(smooth)).astype(jnp.bfloat16)
    partial_mix = jnp.dot(action, out_weight, preferred_element_type=jnp.float32)
    mixed_sum = lax.psum(partial_mix, "ctx")
    return (rows_float + mixed_sum).astype(jnp.bfloat16)


def sender_matrix(own_pos, block_rows, block_count, capacity):
    target = own_pos // block_rows
    hit_table = (target[:, None] == jnp.arange(block_count, dtype=jnp.int32)[None, :]).astype(
        jnp.int32
    )
    rank_rows = jnp.sum((jnp.cumsum(hit_table, axis=0) - hit_table) * hit_table, axis=1)
    slot_ids = target * capacity + rank_rows
    every_slot = jnp.arange(block_count * capacity, dtype=jnp.int32)
    return (slot_ids[None, :] == every_slot[:, None]).astype(jnp.bfloat16)


def landing_rows(audio_pos, block_count, frame_rows, block_rows, capacity, target):
    pos_table = audio_pos.reshape(block_count, frame_rows)
    landing = (pos_table // block_rows == target).astype(jnp.int32)
    rank_rows = jnp.cumsum(landing, axis=1) - landing
    local_pos = pos_table - target * block_rows + 1
    slot_ids = jnp.arange(capacity, dtype=jnp.int32)
    hit_table = landing[:, None, :] * (rank_rows[:, None, :] == slot_ids[None, :, None]).astype(
        jnp.int32
    )
    return jnp.sum(hit_table * local_pos[:, None, :], axis=2).reshape(-1) - 1


def body(
    frames,
    value_weight,
    gate_weight,
    conv_taps,
    out_weight,
    adapter,
    audio_pos,
    text_rows,
    value_proj,
    queries,
    keys,
    grad_out,
    window_low,
):
    tm_count = lax.axis_size("tm")
    ctx_count = lax.axis_size("ctx")
    tm_place = lax.axis_index("tm")
    frame_rows = frames.shape[0]
    block_rows = text_rows.shape[0]
    capacity = 2 * frame_rows // tm_count
    score_scale = 1.0 / math.sqrt(DH)
    encoded = encode_frames(frames, value_weight, gate_weight, conv_taps, out_weight)
    adapted = jnp.dot(
        encoded,
        lax.all_gather(adapter, "tm", axis=0, tiled=True),
        preferred_element_type=jnp.float32,
    ).astype(jnp.bfloat16)
    own_pos = lax.dynamic_slice_in_dim(audio_pos, tm_place * frame_rows, frame_rows)
    picker = sender_matrix(own_pos, block_rows, tm_count, capacity)
    outgoing = jnp.dot(picker, adapted, preferred_element_type=jnp.float32).astype(jnp.bfloat16)
    outgoing = outgoing.reshape(tm_count, capacity, adapted.shape[1])
    incoming = lax.all_to_all(outgoing, "tm", split_axis=0, concat_axis=0, tiled=True)
    landing = landing_rows(audio_pos, tm_count, frame_rows, block_rows, capacity, tm_place)
    placer = landing[None, :] == jnp.arange(block_rows, dtype=jnp.int32)[:, None]
    placed = jnp.dot(
        placer.astype(jnp.bfloat16),
        incoming.reshape(-1, adapted.shape[1]),
        preferred_element_type=jnp.float32,
    )
    is_audio = jnp.any(placer, axis=1)
    hidden = jnp.where(is_audio[:, None], placed.astype(jnp.bfloat16), text_rows)
    full_proj = lax.all_gather(value_proj, "tm", axis=1, tiled=True)
    head_cols = full_proj.shape[1] // ctx_count
    heads_here = head_cols // DH
    values_t = lax.psum_scatter(
        lax.dot_general(
            full_proj, hidden, (((0,), (1,)), ((), ())), preferred_element_type=jnp.float32
        ).astype(jnp.bfloat16),
        "ctx",
        scatter_dimension=0,
        tiled=True,
    )
    q_here, k_here, g_here = (
        lax.all_to_all(queries, "ctx", split_axis=1, concat_axis=0, tiled=True),
        lax.all_to_all(keys, "ctx", split_axis=1, concat_axis=0, tiled=True),
        lax.all_to_all(grad_out, "ctx", split_axis=1, concat_axis=0, tiled=True),
    )
    prior_keys, prior_values = passed_along((k_here, values_t), "tm", 1)
    query_rows = q_here.reshape(block_rows, heads_here, DH)
    grad_rows = g_here.reshape(block_rows, heads_here, DH)
    key_all = jnp.concatenate([prior_keys, k_here], axis=0).reshape(2 * block_rows, heads_here, DH)
    value_all = jnp.concatenate([prior_values, values_t], axis=1).reshape(
        heads_here, DH, 2 * block_rows
    )
    query_pos = tm_place * block_rows + jnp.arange(block_rows, dtype=jnp.int32)
    key_pos = (tm_place - 1) * block_rows + jnp.arange(2 * block_rows, dtype=jnp.int32)
    allowed = (key_pos[None, :] <= query_pos[:, None]) & (key_pos[None, :] >= window_low[:, None])
    scores = (
        jnp.einsum("ihd,jhd->hij", query_rows, key_all, preferred_element_type=jnp.float32)
        * score_scale
    )
    masked = jnp.where(allowed[None], scores, MASK_FILL)
    row_peak = jnp.max(masked, axis=2)
    raw_scores = jnp.where(allowed[None], jnp.exp(masked - row_peak[:, :, None]), 0.0)
    row_total = jnp.sum(raw_scores, axis=2)
    probs_full = raw_scores / row_total[:, :, None]
    weights_low = probs_full.astype(jnp.bfloat16)
    attended = jnp.einsum(
        "hij,hdj->ihd", weights_low, value_all, preferred_element_type=jnp.float32
    )
    row_delta = jnp.einsum("ihd,ihd->hi", grad_rows.astype(jnp.float32), attended)
    grad_scores = jnp.einsum(
        "ihd,hdj->hij", grad_rows, value_all, preferred_element_type=jnp.float32
    )
    slopes = (probs_full * (grad_scores - row_delta[:, :, None])).astype(jnp.bfloat16)
    value_terms_all = jnp.einsum(
        "hij,ihd->jhd", weights_low, grad_rows, preferred_element_type=jnp.float32
    )
    key_terms_all = (
        jnp.einsum("hij,ihd->jhd", slopes, query_rows, preferred_element_type=jnp.float32)
        * score_scale
    )
    back_value, back_key = passed_along(
        (value_terms_all[:block_rows], key_terms_all[:block_rows]), "tm", -1
    )
    own_value = value_terms_all[block_rows:] + back_value
    own_key = key_terms_all[block_rows:] + back_key
    value_grad = own_value.reshape(block_rows, head_cols).astype(jnp.bfloat16)
    d_keys = own_key.reshape(block_rows, head_cols).astype(jnp.bfloat16)
    hidden_grad = lax.dot_general(
        lax.all_gather(value_grad, "ctx", axis=1, tiled=True),
        full_proj,
        (((1,), (1,)), ((), ())),
        preferred_element_type=jnp.float32,
    )
    return (d_keys, hidden_grad.astype(jnp.bfloat16))


def solution(mesh):
    return jax.shard_map(
        body,
        mesh=mesh,
        in_specs=(
            P("tm", None),
            P(None, "ctx"),
            P(None, "ctx"),
            P(None, "ctx"),
            P("ctx", None),
            P("tm", "ctx"),
            P(),
            P("tm", "ctx"),
            P("ctx", "tm"),
            P(("tm", "ctx"), None),
            P(("tm", "ctx"), None),
            P(("tm", "ctx"), None),
            P("tm"),
        ),
        out_specs=(P("tm", "ctx"), P("tm", "ctx")),
        check_vma=False,
    )
```

profile of v0, /device:TPU:9, one launch (start us, length us, event | category | flops | bytes accessed | tf_op | source)
XLA Modules:
  0.0 376.5 jit_solution(12934297166976858519)
XLA Ops:
  8.1 1.1 convert_reduce_fusion
  9.2 1.2 fusion.30
  10.4 1.3 fusion.19
  11.7 1.3 fusion.20
  13.1 3.1 collective-permute-start.1
  16.2 1.3 collective-permute-start.2
  17.5 1.0 slice_bitcast_fusion.30
  18.5 1.0 slice_bitcast_fusion.29
  19.5 1.1 collective-permute-done.2
  20.6 1.2 fusion.72
  21.9 0.5 all-gather.4.cloned.1.call-update
  22.4 0.5 all-gather.6.cloned.1.call-update
  23.2 0.2 reduce_window_sum.23
  23.3 0.2 select_reduce_fusion
  23.6 67.4 %all-reduce.2.cloned.1.call-done = f32[128,1024]{1,0:T(8,128)} async-done(((f32[128,1024]{1,0:T(8,128)}), f32[128,1024]{1,0:T(8,128)}) %all-reduce.2.cloned.1.call-update) | async-done | bytes 524304 | tf_op jit(solution)/shard_map/psum | solution.py:51
  91.0 13.8 %all-gather.4.cloned.1.call-done = bf16[1024,1024]{1,0:T(8,128)(2,1)} async-done(((bf16[32,1024]{1,0:T(8,128)(2,1)}), bf16[1024,1024]{1,0:T(8,128)(2,1)}) %all-gather.4.cloned.1.call-update) | async-done | bytes 2097168 | tf_op jit(solution)/shard_map/all_gather | solution.py:103
  104.8 3.2 fusion.16
  108.1 5.9 %all-to-all-start.2 = ((bf16[32,8,1024]{2,1,0:T(8,128)(2,1)}), bf16[32,8,1024]{2,1,0:T(8,128)(2,1)S(1)}, u32[]{:S(2)}, u32[]{:S(2)}) async-start(bf16[32,8,1024]{2,1,0:T(8,128)(2,1)} %fusion.16), calls=%async_computation.2 | async-start | bytes 1048576 | tf_op jit(solution)/shard_map/all_to_all | solution.py:110
  114.1 0.3 reduce_window_sum.22
  114.4 0.6 multiply_reduce_fusion.1
  115.1 0.2 fusion.35
  115.3 11.5 %all-to-all-done.2 = bf16[32,8,1024]{2,1,0:T(8,128)(2,1)S(1)} async-done(((bf16[32,8,1024]{2,1,0:T(8,128)(2,1)}), bf16[32,8,1024]{2,1,0:T(8,128)(2,1)S(1)}, u32[]{:S(2)}, u32[]{:S(2)}) %all-to-all-start.2) | async-done | bytes 524320 | tf_op jit(solution)/shard_map/all_to_all | solution.py:110
  126.8 84.5 %all-gather.6.cloned.1.call-done = bf16[1024,4096]{1,0:T(8,128)(2,1)} async-done(((bf16[1024,128]{1,0:T(8,128)(2,1)}), bf16[1024,4096]{1,0:T(8,128)(2,1)}) %all-gather.6.cloned.1.call-update) | async-done | bytes 8388624 | tf_op jit(solution)/shard_map/all_gather | solution.py:120
  211.3 8.9 %fusion.3 = bf16[4096,512]{0,1:T(8,128)(2,1)} fusion(bf16[1024,4096]{1,0:T(8,128)(2,1)} %all-gather.6.cloned.1.call-done, bf16[512,1024]{1,0:T(8,128)(2,1)S(1)} %copy-done.12, pred[512]{0:T(512)(128)(4,1)S(1)} %fusion.35, bf16[32,8,1024]{2,1,0:T(8,128)(2,1)S(1)} %all-to-all-done.2, s32[256]{0:T(256)S(1)} %sub.76), kind=kOutput, calls=%fused_computation.7 | convolution fusion | flops 4566679552 | bytes 14157312 | tf_op jit(solution)/shard_map/dot_general | solution.py:124
  220.2 1.0 copy-done.7
  221.2 0.8 copy.99
  222.1 8.4 %all-to-all-start = ((bf16[64,8,512]{2,0,1:T(8,128)(2,1)}), bf16[64,8,512]{2,0,1:T(8,128)(2,1)S(1)}, u32[]{:S(2)}, u32[]{:S(2)}) async-start(bf16[64,8,512]{2,0,1:T(8,128)(2,1)} %bitcast.156), calls=%async_computation | async-start | bytes 1048576 | tf_op jit(solution)/shard_map/all_to_all | solution.py:133
  230.4 0.8 copy.98
  231.3 8.6 %all-to-all-done = bf16[64,8,512]{2,0,1:T(8,128)(2,1)S(1)} async-done(((bf16[64,8,512]{2,0,1:T(8,128)(2,1)}), bf16[64,8,512]{2,0,1:T(8,128)(2,1)S(1)}, u32[]{:S(2)}, u32[]{:S(2)}) %all-to-all-start) | async-done | bytes 524320 | tf_op jit(solution)/shard_map/all_to_all | solution.py:133
  239.9 6.1 %all-to-all-start.1 = ((bf16[64,8,512]{2,0,1:T(8,128)(2,1)}), bf16[64,8,512]{2,0,1:T(8,128)(2,1)S(1)}, u32[]{:S(2)}, u32[]{:S(2)}) async-start(bf16[64,8,512]{2,0,1:T(8,128)(2,1)} %bitcast.155), calls=%async_computation.1 | async-start | bytes 1048576 | tf_op jit(solution)/shard_map/all_to_all | solution.py:132
  246.0 2.1 collective-permute-start
  248.1 0.9 copy.97
  249.0 8.3 %all-to-all-done.1 = bf16[64,8,512]{2,0,1:T(8,128)(2,1)S(1)} async-done(((bf16[64,8,512]{2,0,1:T(8,128)(2,1)}), bf16[64,8,512]{2,0,1:T(8,128)(2,1)S(1)}, u32[]{:S(2)}, u32[]{:S(2)}) %all-to-all-start.1) | async-done | bytes 524320 | tf_op jit(solution)/shard_map/all_to_all | solution.py:132
  257.3 5.4 %all-to-all-start.3 = ((bf16[64,8,512]{2,0,1:T(8,128)(2,1)}), bf16[64,8,512]{2,0,1:T(8,128)(2,1)S(1)}, u32[]{:S(2)}, u32[]{:S(2)}) async-start(bf16[64,8,512]{2,0,1:T(8,128)(2,1)} %bitcast.154), calls=%async_computation.4 | async-start | bytes 1048576 | tf_op jit(solution)/shard_map/all_to_all | solution.py:134
  262.7 1.3 compare_and_fusion
  264.2 0.1 reshape.210
  264.3 0.3 copy.76
  264.7 7.4 %all-to-all-done.3 = bf16[64,8,512]{2,0,1:T(8,128)(2,1)S(1)} async-done(((bf16[64,8,512]{2,0,1:T(8,128)(2,1)}), bf16[64,8,512]{2,0,1:T(8,128)(2,1)S(1)}, u32[]{:S(2)}, u32[]{:S(2)}) %all-to-all-start.3) | async-done | bytes 524320 | tf_op jit(solution)/shard_map/all_to_all | solution.py:134
  272.2 1.2 copy.78
  273.3 1.3 copy.65
  274.6 0.3 copy.66
  274.9 1.2 fusion.23
  276.1 5.7 %fusion.86 = (f32[4,512]{1,0:T(4,128)S(1)}, f32[4,512,1024]{1,2,0:T(8,128)S(1)}) fusion(f32[4,1024,512]{2,1,0:T(8,128)S(1)} %fusion.23, pred[512,1024]{0,1:T(8,128)(4,1)} %compare_and_fusion), kind=kOutput, calls=%fused_computation.188 | output fusion | flops 14681087 | bytes 17309696 | tf_op jit(solution)/shard_map/sub | solution.py:152
  281.8 1.3 fusion.12
  283.2 1.9 copy-done.3
  285.1 1.5 convolution_bitcast_fusion
  286.6 0.4 copy-done.2
  287.0 1.3 collective-permute-start.5
  288.3 24.7 %collective-permute-done.5 = f32[512,4,128]{0,2,1:T(8,128)S(1)} collective-permute-done((f32[512,4,128]{0,2,1:T(8,128)S(1)}, f32[512,4,128]{0,2,1:T(8,128)S(1)}, u32[]{:S(2)}, u32[]{:S(2)}) %collective-permute-start.5) | collective-permute-done | bytes 1048608 | tf_op jit(solution)/shard_map/ppermute | solution.py:31
  313.0 1.0 fusion.21
  314.0 2.6 collective-permute-start.3
  316.6 10.2 %collective-permute-done.3 = bf16[512,512]{0,1:T(8,128)(2,1)S(1)} collective-permute-done((bf16[512,512]{0,1:T(8,128)(2,1)}, bf16[512,512]{0,1:T(8,128)(2,1)S(1)}, u32[]{:S(2)}, u32[]{:S(2)}) %collective-permute-start.3) | collective-permute-done | bytes 524320 | tf_op jit(solution)/shard_map/ppermute | solution.py:31
  326.9 1.1 pad_maximum_fusion
  328.0 0.5 copy.90
  328.5 2.9 convolution_bitcast_fusion.1
  331.5 1.3 copy.86
  332.8 1.9 multiply_reduce_fusion
  334.8 6.6 %multiply_bitcast_fusion = f32[1024,4,128]{0,2,1:T(8,128)S(1)} fusion(bf16[512,4,128]{0,2,1:T(8,128)(2,1)} %copy-done.5, f32[4,512]{1,0:T(4,128)S(1)} %copy.87, bf16[4,128,1024]{2,1,0:T(8,128)(2,1)S(1)} %bitcast.158, bf16[512,4,128]{0,2,1:T(8,128)(2,1)} %copy.78, f32[4,512,1024]{1,2,0:T(8,128)} %copy-done.3, f32[4,512]{1,0:T(4,128)S(1)} %get-tuple-element.45), kind=kOutput, calls=%fused_computation.16 | convolution fusion | flops 1082654720 | bytes 12599296 | tf_op jit(solution)/shard_map/hij,ihd->jhd/dot_general | solution.py:168
  341.5 1.5 collective-permute-start.4
  343.1 5.2 %all-gather.8.cloned.1.call-done = bf16[512,4096]{0,1:T(8,128)(2,1)} async-done(((bf16[512,512]{0,1:T(8,128)(2,1)}), bf16[512,4096]{0,1:T(8,128)(2,1)}) %all-gather.8.cloned.1.call-update) | async-done | bytes 4194320 | tf_op jit(solution)/shard_map/all_gather | solution.py:179
  348.3 10.2 %convolution_convert_fusion.1 = bf16[512,1024]{1,0:T(8,128)(2,1)} fusion(bf16[512,4096]{0,1:T(8,128)(2,1)} %all-gather.8.cloned.1.call-done, bf16[1024,4096]{1,0:T(8,128)(2,1)} %all-gather.6.cloned.1.call-done), kind=kOutput, calls=%fused_computation.19 | convolution fusion | flops 4295491584 | bytes 13631488 | tf_op jit(solution)/shard_map/dot_general | solution.py:178
  358.5 8.4 %collective-permute-done.4 = f32[512,4,128]{0,2,1:T(8,128)} collective-permute-done((f32[512,4,128]{0,2,1:T(8,128)S(1)}, f32[512,4,128]{0,2,1:T(8,128)}, u32[]{:S(2)}, u32[]{:S(2)}) %collective-permute-start.4) | collective-permute-done | bytes 1048608 | tf_op jit(solution)/shard_map/ppermute | solution.py:31
  366.9 1.4 fusion.22
  368.3 1.0 copy.79
  (54 shorter events, 1.3 us)
Async XLA Ops:
  8.0 12.5 %copy-start = (bf16[128,1024]{1,0:T(8,128)(2,1)S(1)}, bf16[128,1024]{1,0:T(8,128)(2,1)}, u32[]{:S(2)}) copy-start(bf16[128,1024]{1,0:T(8,128)(2,1)} %param.17) | copy-start | bytes 786436
  8.0 96.8 %copy-start.4 = (bf16[128,1024]{1,0:T(8,128)(2,1)S(1)}, bf16[128,1024]{1,0:T(8,128)(2,1)}, u32[]{:S(2)}) copy-start(bf16[128,1024]{1,0:T(8,128)(2,1)} %param.13) | copy-start | bytes 786436
  8.0 15.0 %copy-start.10 = (s32[4096]{0:T(1024)S(1)}, s32[4096]{0:T(1024)}, u32[]{:S(2)}) copy-start(s32[4096]{0:T(1024)} %param.19) | copy-start | bytes 49156
  8.0 83.0 %all-reduce.2.cloned.1.call-start = ((), (), s32[]{:S(2)}) async-start(), calls=%async_computation.5 | async-start | bytes 1048576 | tf_op jit(solution)/shard_map/psum | solution.py:51
  13.1 6.4 %collective-permute-start.1 = (bf16[15,128]{1,0:T(8,128)(2,1)S(1)}, bf16[15,128]{1,0:T(8,128)(2,1)S(1)}, u32[]{:S(2)}, u32[]{:S(2)}) collective-permute-start(bf16[15,128]{1,0:T(8,128)(2,1)S(1)} %get-tuple-element.12), channel_id=1, source_target_pairs={{0,8},{8,16},{16,24},{24,32},{32,40},{40,48},{48,56},{56,64},{64,7... | collective-permute-start | bytes 11528 | tf_op jit(solution)/shard_map/ppermute | solution.py:22
  16.2 4.4 %collective-permute-start.2 = (bf16[15,128]{1,0:T(8,128)(2,1)S(1)}, bf16[15,128]{1,0:T(8,128)(2,1)S(1)}, u32[]{:S(2)}, u32[]{:S(2)}) collective-permute-start(bf16[15,128]{1,0:T(8,128)(2,1)S(1)} %get-tuple-element.13), channel_id=1, source_target_pairs={{8,0},{16,8},{24,16},{32,24},{40,32},{48,40},{56,48},{64,56},{72,6... | collective-permute-start | bytes 11528 | tf_op jit(solution)/shard_map/ppermute | solution.py:23
  20.5 190.8 %copy-start.12 = (bf16[512,1024]{1,0:T(8,128)(2,1)S(1)}, bf16[512,1024]{1,0:T(8,128)(2,1)}, u32[]{:S(2)}) copy-start(bf16[512,1024]{1,0:T(8,128)(2,1)} %param.20) | copy-start | bytes 3145732
  21.8 83.0 %all-gather.4.cloned.1.call-start = ((), (), s32[]{:S(2)}) async-start(), calls=%async_computation.6 | async-start | bytes 2162688 | tf_op jit(solution)/shard_map/all_gather | solution.py:103
  22.4 188.9 %all-gather.6.cloned.1.call-start = ((), (), s32[]{:S(2)}) async-start(), calls=%async_computation.7 | async-start | bytes 8650752 | tf_op jit(solution)/shard_map/all_gather | solution.py:120
  108.1 18.8 %all-to-all-start.2 = ((bf16[32,8,1024]{2,1,0:T(8,128)(2,1)}), bf16[32,8,1024]{2,1,0:T(8,128)(2,1)S(1)}, u32[]{:S(2)}, u32[]{:S(2)}) async-start(bf16[32,8,1024]{2,1,0:T(8,128)(2,1)} %fusion.16), calls=%async_computation.2 | async-start | bytes 1048576 | tf_op jit(solution)/shard_map/all_to_all | solution.py:110
  114.0 200.0 %reduce-scatter.2.cloned.1.call-start = ((), (), s32[]{:S(2)}) async-start(), calls=%async_computation.8 | async-start | bytes 4718592 | tf_op jit(solution)/shard_map/reduce_scatter | solution.py:123
  220.2 1.0 copy-start.7
  220.2 10.2 %copy-start.8 = (bf16[64,4096]{1,0:T(8,128)(2,1)S(1)}, bf16[64,4096]{1,0:T(8,128)(2,1)}, u32[]{:S(2)}) copy-start(bf16[64,4096]{1,0:T(8,128)(2,1)} %param.22) | copy-start | bytes 1572868
  220.2 27.9 %copy-start.9 = (bf16[64,4096]{1,0:T(8,128)(2,1)S(1)}, bf16[64,4096]{1,0:T(8,128)(2,1)}, u32[]{:S(2)}) copy-start(bf16[64,4096]{1,0:T(8,128)(2,1)} %param.24) | copy-start | bytes 1572868
  220.2 42.5 %copy-start.11 = (s32[512]{0:T(512)S(1)}, s32[512]{0:T(512)}, u32[]{:S(2)}) copy-start(s32[512]{0:T(512)} %param.25) | copy-start | bytes 6148
  222.1 17.8 %all-to-all-start = ((bf16[64,8,512]{2,0,1:T(8,128)(2,1)}), bf16[64,8,512]{2,0,1:T(8,128)(2,1)S(1)}, u32[]{:S(2)}, u32[]{:S(2)}) async-start(bf16[64,8,512]{2,0,1:T(8,128)(2,1)} %bitcast.156), calls=%async_computation | async-start | bytes 1048576 | tf_op jit(solution)/shard_map/all_to_all | solution.py:133
  239.9 17.4 %all-to-all-start.1 = ((bf16[64,8,512]{2,0,1:T(8,128)(2,1)}), bf16[64,8,512]{2,0,1:T(8,128)(2,1)S(1)}, u32[]{:S(2)}, u32[]{:S(2)}) async-start(bf16[64,8,512]{2,0,1:T(8,128)(2,1)} %bitcast.155), calls=%async_computation.1 | async-start | bytes 1048576 | tf_op jit(solution)/shard_map/all_to_all | solution.py:132
  246.0 27.3 %collective-permute-start = (bf16[512,512]{1,0:T(8,128)(2,1)S(1)}, bf16[512,512]{1,0:T(8,128)(2,1)}, u32[]{:S(2)}, u32[]{:S(2)}) collective-permute-start(bf16[512,512]{1,0:T(8,128)(2,1)S(1)} %bitcast.161), channel_id=1, source_target_pairs={{0,8},{8,16},{16,24},{24,32},{32,40},{40,48},{48,56},{56,64},{64,7... | collective-permute-start | bytes 1572872 | tf_op jit(solution)/shard_map/ppermute | solution.py:31
  257.3 14.7 %all-to-all-start.3 = ((bf16[64,8,512]{2,0,1:T(8,128)(2,1)}), bf16[64,8,512]{2,0,1:T(8,128)(2,1)S(1)}, u32[]{:S(2)}, u32[]{:S(2)}) async-start(bf16[64,8,512]{2,0,1:T(8,128)(2,1)} %bitcast.154), calls=%async_computation.4 | async-start | bytes 1048576 | tf_op jit(solution)/shard_map/all_to_all | solution.py:134
  262.7 85.6 %all-gather.8.cloned.1.call-start = ((), (), s32[]{:S(2)}) async-start(), calls=%async_computation.9 | async-start | bytes 4718592 | tf_op jit(solution)/shard_map/all_gather | solution.py:179
  264.7 10.2 %copy-start.5 = (bf16[512,4,128]{0,2,1:T(8,128)(2,1)}, bf16[512,4,128]{0,2,1:T(8,128)(2,1)S(1)}, u32[]{:S(2)}) copy-start(bf16[512,4,128]{0,2,1:T(8,128)(2,1)S(1)} %copy.76) | copy-start | bytes 1572868
  281.8 3.2 copy-start.3
  281.8 3.2 copy-start.6
  285.1 2.0 copy-start.2
  287.0 25.9 %collective-permute-start.5 = (f32[512,4,128]{0,2,1:T(8,128)S(1)}, f32[512,4,128]{0,2,1:T(8,128)S(1)}, u32[]{:S(2)}, u32[]{:S(2)}) collective-permute-start(f32[512,4,128]{0,2,1:T(8,128)S(1)} %slice.308), channel_id=1, source_target_pairs={{8,0},{16,8},{24,16},{32,24},{40,32},{48,40},{56,48},{64,56},{72,6... | collective-permute-start | bytes 3145736 | tf_op jit(solution)/shard_map/ppermute | solution.py:31
  314.0 12.9 %collective-permute-start.3 = (bf16[512,512]{0,1:T(8,128)(2,1)}, bf16[512,512]{0,1:T(8,128)(2,1)S(1)}, u32[]{:S(2)}, u32[]{:S(2)}) collective-permute-start(bf16[512,512]{0,1:T(8,128)(2,1)} %reduce-scatter.2.cloned.1.call-done), channel_id=1, source_target_pairs={{0,8},{8,16},{16,24},{24,32},{32,40},{40,48},{48,56},{56,64},{64,7... | collective-permute-start | bytes 1572872 | tf_op jit(solution)/shard_map/ppermute | solution.py:31
  341.5 25.4 %collective-permute-start.4 = (f32[512,4,128]{0,2,1:T(8,128)S(1)}, f32[512,4,128]{0,2,1:T(8,128)}, u32[]{:S(2)}, u32[]{:S(2)}) collective-permute-start(f32[512,4,128]{0,2,1:T(8,128)S(1)} %slice.306), channel_id=1, source_target_pairs={{8,0},{16,8},{24,16},{32,24},{40,32},{48,40},{56,48},{64,56},{72,6... | collective-permute-start | bytes 3145736 | tf_op jit(solution)/shard_map/ppermute | solution.py:31
  348.3 21.0 %copy-start.1 = (bf16[128,1024]{1,0:T(8,128)(2,1)S(1)}, bf16[128,1024]{1,0:T(8,128)(2,1)}, u32[]{:S(2)}) copy-start(bf16[128,1024]{1,0:T(8,128)(2,1)} %param.17) | copy-start | bytes 786436
Sparse Core Ops, SparseCore 0:
  21.9 69.0 all-reduce.1
  220.3 47.0 reduce-scatter.1
  314.1 34.1 all-gather.7
Sparse Core Ops, SparseCore 1:
  25.2 79.6 all-gather.3
  107.5 103.8 all-gather.5
where the time goes:
time: 384 us; the launch traced here: 376 us
  waiting for transfers between devices  252 us (66%)
  matrix products  38.4 us (10%)
  starting transfers between devices  37.8 us (10%)
  other arithmetic  17.7 us (5%)
  between operations  15.6 us (4%)
  local copies, waits for them, and re-layouts  14.5 us (4%)
    all_gather x1, waiting for transfers between devices, body(): full_proj = lax.all_gather(value_proj, 'tm', axis=1, tiled=True)  84.5 us
    psum x1, waiting for transfers between devices, encode_frames(): mixed_sum = lax.psum(partial_mix, 'ctx')  67.4 us
    ppermute x4, waiting for transfers between devices, passed_along(): return lax.ppermute(value, axis, pairs)  43.3 us
    all_gather x1, waiting for transfers between devices, body(): lax.all_gather(adapter, 'tm', axis=0, tiled=True)  13.8 us
    all_to_all x1, waiting for transfers between devices, body(): lax.all_to_all(outgoing, 'tm', split_axis=0, concat_axis=0, tiled=True)  11.5 us
    dot_general x1, matrix products, body(): lax.dot_general(lax.all_gather(value_grad, 'ctx', axis=1, tiled=True), fu...  10.2 us
    dot_general x1, matrix products, body(): lax.dot_general(full_proj, hidden, (((0,), (1,)), ((), ())), preferred_el...  8.86 us
    all_to_all x1, waiting for transfers between devices, body(): lax.all_to_all(keys, 'ctx', split_axis=1, concat_axis=0, tiled=True)  8.64 us
  transfers between devices with their start and end apart: 15, of which 12 were waited for; matrix products, arithmetic and copies ran while one was open for 13% of the time, Pallas kernels for 0%

commit v1 on v0

v1 whole, which is shorter than its diff:
```python
import math

import jax
import jax.numpy as jnp
from jax import lax
from jax.experimental import pallas as pl
from jax.experimental.pallas import tpu as pltpu
from jax.sharding import PartitionSpec as P

DH = 128
NORM_EPS = 1e-05
MASK_FILL = -1e30
MESH = pl.DeviceIdType.MESH
F32 = jnp.float32
BF16 = jnp.bfloat16

NT = 32
NC = 8
NX = 4
NZ = 8
TOK = 512
AUD = 128
DE = 1024
COLS = 1024
HC = 512
HH = HC // DH
HALF = TOK // 2
SLOT = 8
TILES = ((0, 0, 0, 256), (0, 256, 0, 512), (1, 0, 0, 512), (1, 256, 256, 256))
N_SEMS = 128


def dot(a, b):
    return jnp.dot(a, b, preferred_element_type=F32)


def dot_t(a, b):
    return lax.dot_general(a, b, (((1,), (1,)), ((), ())), preferred_element_type=F32)


def iota(shape, dim):
    return lax.broadcasted_iota(jnp.int32, shape, dim)


def kernel(
    frames, vw, gw, taps, ow, text, low8, slot8, land_lo, land_hi, adapter, vp, q, k, g,
    dk_out, dh_out,
    W, AD, qs, gs, ks, lown, ext, glu_s, mixs, mixr, enc, adp, pick, inc, hid,
    e_ref, gv_ref, st_own, st_nxt, st_fp, st_fn, dl_own, dl_nxt, dl_fp, dl_fn,
    VG, psend, pown, precv, rsend, rrecv, vbuf, acc,
    ssem, rsem, lsem, aus, aur, rss, rsr,
):
    t = lax.axis_index("tm")
    c = lax.axis_index("ctx")
    x = lax.rem(t, NX)
    z = lax.div(t, NX)
    core = lax.rem(c, 2)
    yy = lax.div(c, 2)
    up = (lax.rem(z + 1, NZ) * NX + x, c)
    dn = (lax.rem(z + NZ - 1, NZ) * NX + x, c)
    nxt = (lax.rem(t + 1, NT), c)
    prv = (lax.rem(t + NT - 1, NT), c)
    mate = (t, c + 1 - 2 * core)

    def ctx_peer(d):
        return (t, lax.rem(c + d, NC))

    def x_peer(d):
        return (z * NX + lax.rem(x + d, NX), c)

    def zat(d):
        return lax.rem(z + d + NZ, NZ)

    def al(v, m):
        return pl.multiple_of(v, m)

    sends = []

    def send(src, dst, dev):
        i = len(sends)
        copy = pltpu.make_async_remote_copy(
            src_ref=src, dst_ref=dst, send_sem=ssem.at[i], recv_sem=rsem.at[i],
            device_id=dev, device_id_type=MESH,
        )
        copy.start()
        sends.append(copy)
        return copy

    def arrived(copies):
        for copy in copies:
            copy.wait_recv()

    locals_ = []

    def local(src, dst):
        copy = pltpu.make_async_copy(src, dst, lsem.at[len(locals_)])
        copy.start()
        locals_.append(copy)
        return copy

    bar = pltpu.get_barrier_semaphore()

    def greet(d, carry):
        pl.semaphore_signal(bar, inc=1, device_id=(lax.rem(t + d, NT), c), device_id_type=MESH)
        return carry

    lax.fori_loop(1, NT, greet, 0)
    for d in range(1, NC):
        pl.semaphore_signal(bar, inc=1, device_id=ctx_peer(d), device_id_type=MESH)

    own_vp = local(vp, W.at[t])
    own_ad = local(adapter, AD.at[pl.ds(al(t * 32, 32), 32)])
    own_rows = pl.ds(al(c * 64, 64), 64)
    own_cols = pl.ds(al(c * HC, HC), HC)
    own_qkg = [
        local(k.at[:, own_cols], ks.at[own_rows]),
        local(q.at[:, own_cols], qs.at[0, own_rows]),
        local(g.at[:, own_cols], gs.at[0, own_rows]),
    ]
    pl.semaphore_wait(bar, NT - 1 + NC - 1)

    halo = [
        send(frames.at[pl.ds(AUD - 16, 16)], ext.at[pl.ds(0, 16)], nxt),
        send(frames.at[pl.ds(0, 16)], ext.at[pl.ds(AUD + 16, 16)], prv),
    ]
    low_copy = send(low8, lown, prv)
    ad_x = [send(adapter, AD.at[pl.ds(al(t * 32, 32), 32)], x_peer(d)) for d in (1, 3, 2)]
    bz = {}
    az = {}
    dz = {}
    bx = {}

    def ring(s, ref_of, part_of, table):
        if s < NZ // 2 - 1:
            u, v = ref_of(zat(-s)), ref_of(zat(s))
        else:
            u, v = part_of(zat(-s), 0), part_of(zat(s), 1)
        table[s] = [send(u, u, up), send(v, v, dn)]

    def b_ref(zz):
        return W.at[zz * NX + x, pl.ds(512, 512)]

    def b_part(zz, p):
        return W.at[zz * NX + x, pl.ds(512 + 256 * p, 256)]

    def a_ref(zz):
        return W.at[pl.ds(zz * NX, NX), pl.ds(0, 512)]

    def a_part(zz, p):
        return W.at[pl.ds(zz * NX + 2 * p, 2), pl.ds(0, 512)]

    def d_ref(zz):
        return AD.at[pl.ds(al(zz * 128, 128), 128)]

    def d_part(zz, p):
        return AD.at[pl.ds(al(zz * 128 + 64 * p, 64), 64)]

    def b_spread(s):
        offsets = (0,) if s < 0 else ((-1 - s, 1 + s) if s < 3 else (4,))
        bx[s] = [send(b_ref(zat(o)), b_ref(zat(o)), x_peer(d)) for o in offsets for d in (1, 3, 2)]

    def a_step(s):
        ring(s, a_ref, a_part, az)

    def b_step(s):
        ring(s, b_ref, b_part, bz)

    def d_step(s):
        ring(s, d_ref, d_part, dz)

    own_vp.wait()
    a_x = [
        send(vp.at[pl.ds(0, 512)], W.at[t, pl.ds(0, 512)], x_peer(d)) for d in (1, 3, 2)
    ]
    b_step(0)
    qkg = []
    for src, dst in ((k, ks), (q, qs.at[0]), (g, gs.at[0])):
        for d in (1, 7, 2, 6, 3, 5, 4):
            peer = lax.rem(c + d, NC)
            qkg.append(send(src.at[:, pl.ds(al(peer * HC, HC), HC)], dst.at[own_rows], (t, peer)))
    b_spread(-1)

    ext[pl.ds(16, AUD), :] = frames[...]
    arrived(halo)
    rows = ext[...].astype(F32)
    centre = jnp.mean(rows, axis=1, keepdims=True)
    off = rows - centre
    spread = jnp.mean(off * off, axis=1, keepdims=True)
    normed = (off * lax.rsqrt(spread + NORM_EPS)).astype(BF16)
    value_part = dot(normed, vw[...])
    gate_part = dot(normed, gw[...])
    glu = (value_part * jax.nn.sigmoid(gate_part)).astype(BF16).astype(F32)
    row = iota(glu.shape, 0)
    first = jnp.where(t == 0, 16, 0)
    last = jnp.where(t == NT - 1, AUD + 16, AUD + 32)
    glu_s[...] = jnp.where((row >= first) & (row < last), glu, 0.0)

    own_ad.wait()
    arrived(ad_x)
    d_step(0)
    arrived(a_x)
    a_step(0)

    smooth = jnp.zeros((AUD, DH), F32)
    for j in range(taps.shape[0]):
        smooth = smooth + taps[pl.ds(j, 1), :] * glu_s[pl.ds(1 + j, AUD), :]
    action = (smooth * jax.nn.sigmoid(smooth)).astype(BF16)
    mixs[...] = dot(action, ow[...]).astype(BF16)
    mix = [
        send(mixs.at[pl.ds(al(lax.rem(c + d, NC) * 16, 16), 16)], mixr.at[d], ctx_peer(d))
        for d in (4, 2, 6, 3, 5, 1, 7)
    ]
    arrived(bz[0])
    b_step(1)
    b_spread(0)
    arrived(mix)
    mine = pl.ds(al(c * 16, 16), 16)
    total = frames[mine, :].astype(F32) + mixs[mine, :].astype(F32)
    for d in range(1, NC):
        total = total + mixr[d].astype(F32)
    enc[mine, :] = total.astype(BF16)
    enc_copies = [send(enc.at[mine], enc.at[mine], ctx_peer(d)) for d in (4, 2, 6, 3, 5, 1, 7)]

    arrived(dz[0])
    d_step(1)
    for copy in own_qkg:
        copy.wait()
    arrived(qkg)
    halo_qg = [send(qs.at[0], qs.at[1], prv), send(gs.at[0], gs.at[1], prv)]
    arrived(bz[1])
    b_step(2)
    b_spread(1)
    arrived(dz[1])
    d_step(2)

    scale = 1.0 / math.sqrt(DH)
    base = t * TOK
    row8 = iota((8, HALF), 0)

    def head_cols(h):
        return pl.ds(al(h * DH, DH), DH)

    def score_tiles(block, lows, limit, stats):
        def one_head(h, carry):
            hs = head_cols(h)
            for b, i0, j0, jn in TILES:
                if b != block:
                    continue
                qi = pl.ds(i0, HALF)
                s = dot_t(ks[pl.ds(j0, jn), hs], qs[b, qi, hs]) * scale
                jj = iota((jn, HALF), 0) + j0
                ok = jj >= lows[pl.ds(0, 1), qi] - base
                if block == 0:
                    ok = ok & (jj <= iota((jn, HALF), 1) + i0)
                else:
                    ok = ok & (jj < limit)
                s = jnp.where(ok, s, MASK_FILL)
                m = jnp.max(s, axis=0, keepdims=True)
                e = jnp.where(ok, jnp.exp(s - m), 0.0)
                n = jnp.sum(e, axis=0, keepdims=True)
                e_ref[b, h, pl.ds(j0, jn), qi] = e
                stats[h, :, qi] = jnp.where(row8 == 0, m, n)
            return carry

        lax.fori_loop(0, HH, one_head, 0)

    score_tiles(0, low8, TOK, st_own)
    stats_a = send(st_own, st_fn, prv)
    arrived(dz[2])
    d_step(3)
    arrived(az[0])
    a_step(1)
    arrived(bz[2])
    b_step(3)
    b_spread(2)

    arrived([low_copy])
    arrived(halo_qg)
    score_tiles(1, lown, jnp.where(t == NT - 1, 0, TOK), st_nxt)
    stats_b = send(st_nxt, st_fp, nxt)

    arrived(dz[3])
    arrived(enc_copies)
    for n in range(4):
        cols = pl.ds(256 * n, 256)
        adp[:, cols] = dot(enc[...], AD[:, cols]).astype(BF16)
    slot_row = iota((NT * 16, AUD), 0)
    picker = ((slot_row // 16) * SLOT + slot_row % SLOT == slot8[pl.ds(0, 1), :]).astype(F32)
    picker = picker.astype(BF16)
    low_half = dot(picker, adp[:, pl.ds(0, 512)])
    high_half = dot(picker, adp[:, pl.ds(512, 512)])
    upper = iota((NT * 16, 512), 0) % 16 < SLOT
    pick[...] = jnp.where(upper, low_half, high_half).astype(BF16)
    my_slot = pl.ds(al(t * 16, 16), 16)

    def audio_copy(d):
        peer = lax.rem(t + d, NT)
        return pltpu.make_async_remote_copy(
            src_ref=pick.at[pl.ds(al(peer * 16, 16), 16)], dst_ref=inc.at[my_slot],
            send_sem=aus.at[d], recv_sem=aur.at[d], device_id=(peer, c), device_id_type=MESH,
        )

    def audio_start(d, carry):
        audio_copy(d).start()
        return carry

    lax.fori_loop(1, NT, audio_start, 0)
    inc[my_slot, :] = pick[my_slot, :]
    arrived(bz[3])
    b_spread(3)

    arrived([stats_a, stats_b])

    def factor(mine_st, other_st, h):
        m1, s1 = mine_st[h, pl.ds(0, 1), :], mine_st[h, pl.ds(1, 1), :]
        m2, s2 = other_st[h, pl.ds(0, 1), :], other_st[h, pl.ds(1, 1), :]
        m = jnp.maximum(m1, m2)
        a1 = jnp.exp(m1 - m)
        return a1 / (s1 * a1 + s2 * jnp.exp(m2 - m))

    def gather_terms(tiles, other, h):
        hs = head_cols(h)
        top = dot(tiles[0], other[0, pl.ds(0, 256), hs]) + dot(tiles[1][:256], other[0, pl.ds(256, 256), hs])
        top = top + dot(tiles[2][:256], other[1, pl.ds(0, 256), hs])
        low = dot(tiles[1][256:], other[0, pl.ds(256, 256), hs])
        low = low + dot(tiles[2][256:], other[1, pl.ds(0, 256), hs])
        low = low + dot(tiles[3], other[1, pl.ds(256, 256), hs])
        return top, low

    def prob_head(h, carry):
        f = (factor(st_own, st_fp, h), factor(st_nxt, st_fn, h))
        tiles = []
        for b, i0, j0, jn in TILES:
            p = e_ref[b, h, pl.ds(j0, jn), pl.ds(i0, HALF)] * f[b][:, i0 : i0 + HALF]
            e_ref[b, h, pl.ds(j0, jn), pl.ds(i0, HALF)] = p
            tiles.append(p.astype(BF16))
        top, low = gather_terms(tiles, gs, h)
        hs = head_cols(h)
        VG[c, pl.ds(0, 256), hs] = top.astype(BF16)
        VG[c, pl.ds(256, 256), hs] = low.astype(BF16)
        return carry

    lax.fori_loop(0, HH, prob_head, 0)
    vg_y = [send(VG.at[c], VG.at[c], ctx_peer(2 * d)) for d in (1, 3, 2)]
    vg_mate = [send(VG.at[c], VG.at[c], mate)]
    arrived(az[1])
    a_step(2)

    def audio_arrived(d, carry):
        audio_copy(d).wait_recv()
        return carry

    lax.fori_loop(1, NT, audio_arrived, 0)
    for land, cols in ((land_lo, pl.ds(0, 512)), (land_hi, pl.ds(512, 512))):
        place = (iota((TOK, NT * 16), 0) == land[pl.ds(0, 1), :]).astype(F32)
        there = jnp.sum(place, axis=1, keepdims=True) > 0.5
        rows_in = dot(place.astype(BF16), inc[...])
        hid[:, cols] = jnp.where(there, rows_in, text[:, cols].astype(F32)).astype(BF16)

    offsets = (0, -1, 1, -2, 2, -3, 3, 4)
    mate_rows = pl.ds(al((1 - core) * HALF, HALF), HALF)
    my_rows = pl.ds(al(core * HALF, HALF), HALF)

    def weights_of(cp):
        return jnp.concatenate([W[cp * HH + j] for j in range(HH)], axis=1)

    pair = []

    def terms(i):
        cp = zat(offsets[i])
        psend[i] = dot(hid[mate_rows, :], weights_of(cp)).astype(BF16)
        pair.append(send(psend.at[i], precv.at[i], mate))
        pown[i] = dot(hid[my_rows, :], weights_of(cp)).astype(BF16)

    def group_copy(d, i):
        return pltpu.make_async_remote_copy(
            src_ref=rsend.at[i], dst_ref=rrecv.at[yy, my_rows],
            send_sem=rss.at[d], recv_sem=rsr.at[d],
            device_id=(t, lax.rem(c + d, NC)), device_id_type=MESH,
        )

    def chip_sum(i):
        cp = zat(offsets[i])
        d = lax.rem(cp - c + NC, NC)
        arrived([pair[i]])
        total = pown[i].astype(F32) + precv[i].astype(F32)
        rsend[i] = total.astype(BF16)

        @pl.when(d != 0)
        def _():
            group_copy(d, i).start()

        @pl.when(d == 0)
        def _():
            rrecv[yy, my_rows, :] = rsend[i]

    arrived(bx[-1])
    terms(0)
    arrived(az[2])
    a_step(3)
    arrived(bx[0])
    terms(1)
    chip_sum(0)
    terms(2)
    chip_sum(1)
    arrived(bx[1])
    terms(3)
    chip_sum(2)
    terms(4)
    chip_sum(3)
    arrived(vg_y)
    for d in (1, 3, 2):
        src = lax.rem(c + NC - 2 * d, NC)
        vg_mate.append(send(VG.at[src], VG.at[src], mate))
    arrived(bx[2])
    terms(5)
    chip_sum(4)
    terms(6)
    chip_sum(5)
    arrived(az[3])
    arrived(bx[3])
    terms(7)
    chip_sum(6)
    chip_sum(7)

    arrived(vg_mate)

    def hidden_grad(n, carry):
        rows_n = pl.ds(al(n * 256, 256), 256)

        def chunk(cc, carry2):
            w = jnp.concatenate([W[cc * HH + j, rows_n, :] for j in range(HH)], axis=1)
            acc[...] += dot_t(VG[cc], w)
            return carry2

        acc[...] = jnp.zeros(acc.shape, F32)
        lax.fori_loop(0, NC, chunk, 0)
        dh_out[:, rows_n] = acc[...].astype(BF16)
        return carry

    lax.fori_loop(0, COLS // 256, hidden_grad, 0)

    for d in range(1, NC):
        group_copy(d, 0).wait_recv()
    total = rrecv[0].astype(F32)
    for y in range(1, NC // 2):
        total = total + rrecv[y].astype(F32)
    vbuf[...] = total.astype(BF16)

    def delta_head(h, carry):
        hs = head_cols(h)
        for b, i0, j0, jn in TILES:
            qi = pl.ds(i0, HALF)
            gv = dot_t(vbuf[pl.ds(j0, jn), hs], gs[b, qi, hs])
            gv_ref[b, h, pl.ds(j0, jn), qi] = gv
            w = e_ref[b, h, pl.ds(j0, jn), qi].astype(BF16).astype(F32)
            part = jnp.sum(w * gv, axis=0, keepdims=True)
            table = dl_own if b == 0 else dl_nxt
            table[h, :, qi] = jnp.where(row8 == 0, part, 0.0)
        return carry

    lax.fori_loop(0, HH, delta_head, 0)
    arrived([send(dl_own, dl_fn, prv), send(dl_nxt, dl_fp, nxt)])

    def key_head(h, carry):
        delta = (
            dl_own[h, pl.ds(0, 1), :] + dl_fp[h, pl.ds(0, 1), :],
            dl_nxt[h, pl.ds(0, 1), :] + dl_fn[h, pl.ds(0, 1), :],
        )
        tiles = []
        for b, i0, j0, jn in TILES:
            qi = pl.ds(i0, HALF)
            p = e_ref[b, h, pl.ds(j0, jn), qi]
            gv = gv_ref[b, h, pl.ds(j0, jn), qi]
            tiles.append((p * (gv - delta[b][:, i0 : i0 + HALF])).astype(BF16))
        top, low = gather_terms(tiles, qs, h)
        hs = head_cols(h)
        dk_out[pl.ds(0, 256), hs] = (top * scale).astype(BF16)
        dk_out[pl.ds(256, 256), hs] = (low * scale).astype(BF16)
        return carry

    lax.fori_loop(0, HH, key_head, 0)

    def audio_sent(d, carry):
        audio_copy(d).wait_send()
        return carry

    lax.fori_loop(1, NT, audio_sent, 0)
    for d in range(1, NC):
        group_copy(d, 0).wait_send()
    for copy in sends:
        copy.wait_send()


def positions(audio_pos):
    t = lax.axis_index("tm")
    order = jnp.arange(AUD, dtype=jnp.int32)
    own = lax.dynamic_slice_in_dim(audio_pos, t * AUD, AUD)
    target = own // TOK
    same = (target[:, None] == target[None, :]) & (order[:, None] < order[None, :])
    slot = target * SLOT + jnp.sum(same.astype(jnp.int32), axis=0)
    table = audio_pos.reshape(NT, AUD)
    here = table // TOK == t
    before = (order[:, None] < order[None, :]).astype(BF16)
    rank = jnp.dot(here.astype(BF16), before, preferred_element_type=F32).astype(jnp.int32)
    slots = jnp.arange(SLOT, dtype=jnp.int32)
    hit = here[:, None, :] & (rank[:, None, :] == slots[None, :, None])
    place = jnp.sum(jnp.where(hit, table[:, None, :] - t * TOK + 1, 0), axis=2) - 1
    none = jnp.full_like(place, -1)
    land_lo = jnp.concatenate([place, none], axis=1).reshape(1, NT * 16)
    land_hi = jnp.concatenate([none, place], axis=1).reshape(1, NT * 16)
    eight = lambda a: jnp.broadcast_to(a, (8, a.shape[-1]))
    return eight(slot[None]), eight(land_lo), eight(land_hi)


def body(
    frames, value_weight, gate_weight, conv_taps, out_weight, adapter, audio_pos, text_rows,
    value_proj, queries, keys, grad_out, window_low,
):
    slot8, land_lo, land_hi = positions(audio_pos)
    low8 = jnp.broadcast_to(window_low[None], (8, TOK))
    vm = pl.BlockSpec(memory_space=pltpu.VMEM)
    hbm = pl.BlockSpec(memory_space=pl.ANY)
    vmem = pltpu.VMEM
    dma = pltpu.SemaphoreType.DMA
    return pl.pallas_call(
        kernel,
        out_shape=(
            jax.ShapeDtypeStruct((TOK, HC), BF16),
            jax.ShapeDtypeStruct((TOK, COLS), BF16),
        ),
        in_specs=[vm] * 10 + [hbm] * 5,
        out_specs=(vm, vm),
        scratch_shapes=[
            vmem((NT, COLS, DH), BF16),
            vmem((DE, COLS), BF16),
            vmem((2, TOK, HC), BF16),
            vmem((2, TOK, HC), BF16),
            vmem((TOK, HC), BF16),
            vmem((8, TOK), jnp.int32),
            vmem((AUD + 32, DE), BF16),
            vmem((AUD + 32, DH), F32),
            vmem((AUD, DE), BF16),
            vmem((NC, 16, DE), BF16),
            vmem((AUD, DE), BF16),
            vmem((AUD, COLS), BF16),
            vmem((NT * 16, 512), BF16),
            vmem((NT * 16, 512), BF16),
            vmem((TOK, COLS), BF16),
            vmem((2, HH, TOK, TOK), F32),
            vmem((2, HH, TOK, TOK), F32),
        ]
        + [vmem((HH, 8, TOK), F32)] * 8
        + [
            vmem((NC, TOK, HC), BF16),
            vmem((NC, HALF, HC), BF16),
            vmem((NC, HALF, HC), BF16),
            vmem((NC, HALF, HC), BF16),
            vmem((NC, HALF, HC), BF16),
            vmem((NC // 2, TOK, HC), BF16),
            vmem((TOK, HC), BF16),
            vmem((TOK, 256), F32),
            dma((N_SEMS,)),
            dma((N_SEMS,)),
            dma((8,)),
            dma((NT,)),
            dma((NT,)),
            dma((NC,)),
            dma((NC,)),
        ],
        compiler_params=pltpu.CompilerParams(
            collective_id=0, has_side_effects=True, vmem_limit_bytes=60 * 1024 * 1024
        ),
        cost_estimate=pl.CostEstimate(flops=13_000_000_000, bytes_accessed=8_000_000, transcendentals=4_000_000),
    )(
        frames, value_weight, gate_weight, conv_taps, out_weight, text_rows, low8, slot8,
        land_lo, land_hi, adapter, value_proj, queries, keys, grad_out,
    )


def solution(mesh):
    return jax.shard_map(
        body,
        mesh=mesh,
        in_specs=(
            P("tm", None),
            P(None, "ctx"),
            P(None, "ctx"),
            P(None, "ctx"),
            P("ctx", None),
            P("tm", "ctx"),
            P(),
            P("tm", "ctx"),
            P("ctx", "tm"),
            P(("tm", "ctx"), None),
            P(("tm", "ctx"), None),
            P(("tm", "ctx"), None),
            P("tm"),
        ),
        out_specs=(P("tm", "ctx"), P("tm", "ctx")),
        check_vma=False,
    )
```

time: 384 us -> 165 us (0.43); the launches traced: 376 us -> 162 us
  waiting for transfers between devices: 252 us -> 0 us
  Pallas kernels: 0 us -> 153 us
  matrix products: 38.4 us -> 0.14 us
  starting transfers between devices: 37.8 us -> 0 us
  other arithmetic: 17.7 us -> 0.92 us
  between operations: 15.6 us -> 0.69 us
  local copies, waits for them, and re-layouts: 14.5 us -> 6.96 us
    pallas_call x0 -> x1, Pallas kernels: none -> 153 us  [body(): pl.pallas_call(kernel, out_shape=(jax.ShapeDtypeStruct((TOK, HC), BF16),...]
    all_gather x3 -> x0, waiting for transfers between devices: 104 us -> none  [the longest x1 84.5 us: body(): full_proj = lax.all_gather(value_proj, 'tm', axis=1, tiled=True)]
    psum x1 -> x0, waiting for transfers between devices: 67.4 us -> none  [encode_frames(): mixed_sum = lax.psum(partial_mix, 'ctx')]
    ppermute x6 -> x0, waiting for transfers between devices: 44.4 us -> none  [the longest x4 43.3 us: passed_along(): return lax.ppermute(value, axis, pairs)]
    dot_general x10 -> x1, matrix products: 38.4 us -> 0.14 us  [positions(): jnp.dot(here.astype(BF16), before, preferred_element_type=F32)]
    all_to_all x4 -> x0, waiting for transfers between devices: 35.8 us -> none  [the longest x1 11.5 us: body(): lax.all_to_all(outgoing, 'tm', split_axis=0, concat_axis=0, tiled=True)]
    all_to_all x4 -> x0, starting transfers between devices: 25.7 us -> none  [the longest x1 8.36 us: body(): lax.all_to_all(keys, 'ctx', split_axis=1, concat_axis=0, tiled=True)]
    ppermute x6 -> x0, starting transfers between devices: 11.9 us -> none  [the longest x4 7.54 us: passed_along(): return lax.ppermute(value, axis, pairs)]
  transfers between devices with their start and end apart: 15 -> 0, of which waited for: 12 -> 0; matrix products, arithmetic and copies ran while one was open for 13% -> 0% of each run, Pallas kernels for 0% -> 0%
where the time goes in v1:
time: 165 us; the launch traced here: 162 us
  Pallas kernels  153 us (93%)
  local copies, waits for them, and re-layouts  6.96 us (4%)
    pallas_call x1, Pallas kernels, body(): pl.pallas_call(kernel, out_shape=(jax.ShapeDtypeStruct((TOK, HC), BF16),...  153 us
    unnamed x8, local copies, waits for them, and re-layouts  4.3 us

profile of v1, /device:TPU:9, one launch (start us, length us, event | category | flops | bytes accessed | tf_op | source)
XLA Modules:
  0.0 162.0 jit_solution(2272270987909393282)
XLA Ops:
  0.6 0.0 copy-start.1
  0.6 0.7 copy-done.1
  1.3 0.1 and_select_fusion
  1.4 0.1 convert_reduce_fusion
  1.5 0.1 multiply_add_fusion
  1.6 0.6 broadcast_in_dim.25.slot8
  2.2 0.1 convolution_convert_fusion
  2.4 0.6 select_reduce_fusion
  3.0 0.0 copy-start.2
  3.0 0.7 copy-done.2
  3.7 0.6 broadcast_in_dim.24.low8
  4.3 0.1 fusion.7
  4.4 0.1 broadcast_in_dim.30
  4.5 0.1 broadcast_in_dim.28
  4.5 0.6 broadcast_in_dim.29.land_lo
  5.2 0.6 broadcast_in_dim.31.land_hi
  5.8 153.3 %shard_map.140 = (bf16[512,512]{1,0:T(8,128)(2,1)}, bf16[512,1024]{1,0:T(8,128)(2,1)}) custom-call(bf16[128,1024]{1,0:T(8,128)(2,1)} %frames.1, bf16[1024,128]{1,0:T(8,128)(2,1)} %vw.1, bf16[1024,128]{1,0:T(8,128)(2,1)} %gw.1, f32[31,128]{1,0:T(8,128)} %taps.1, bf16[128,1024]{1,0:T(8,128)(2,1)} %ow.1, bf16[512,1024]{1,0:T(8,128)(2,1)} %text.1, ...), custom_call_target="tpu_custom_call" | custom-call | flops 12999999488 | bytes 8000000 | tf_op jit(solution)/shard_map/pallas_call | solution.py:526
  159.0 0.0 copy-start
  159.0 2.0 %copy.17 = bf16[512,512]{1,0:T(8,128)(2,1)} copy(bf16[512,512]{1,0:T(8,128)(2,1)} %get-tuple-element.6) | data formatting | bytes 1048576
  161.0 0.0 copy-done
  161.0 1.0 copy.18
  (3 shorter events, 0.0 us)
Async XLA Ops:
  0.6 0.7 copy-start.1
  3.0 0.7 copy-start.2
  159.0 2.0 %copy-start = (bf16[512,1024]{1,0:T(8,128)(2,1)S(1)}, bf16[512,1024]{1,0:T(8,128)(2,1)}, u32[]{:S(2)}) copy-start(bf16[512,1024]{1,0:T(8,128)(2,1)} %get-tuple-element.7) | copy-start | bytes 3145732

commit v2 on v1

v2 whole, which is shorter than its diff:
```python
import math

import jax
import jax.numpy as jnp
from jax import lax
from jax.experimental import pallas as pl
from jax.experimental.pallas import tpu as pltpu
from jax.sharding import PartitionSpec as P

DH = 128
NORM_EPS = 1e-05
MASK_FILL = -1e30
MESH = pl.DeviceIdType.MESH
F32 = jnp.float32
BF16 = jnp.bfloat16

NT = 32
NC = 8
NX = 4
NZ = 8
TOK = 512
AUD = 128
DE = 1024
COLS = 1024
HC = 512
HH = HC // DH
HALF = TOK // 2
SLOT = 8
TILES = ((0, 0, 0, 256), (0, 256, 0, 512), (1, 0, 0, 512), (1, 256, 256, 256))
N_SEMS = 160
ROWS_A = 384
ROWS_B = COLS - ROWS_A
OFFSETS = (0, -1, 1, -2, 2, -3, 3, 4)
ORDER = (
    "issue", "i_b0", "i_k", "i_q", "mm", "pos", "LN", "d_s0", "i_bm", "p0", "m0", "conv",
    "d_s1", "b_s1", "i_ax", "hq", "rm", "sc0", "i_g", "enc", "b_s2", "p1", "d_s2", "r0", "hg",
    "p2", "d_s3", "b_s3", "a_s0", "sc1", "m3", "adapt", "r1", "m1", "m2", "prob", "a_s1", "r2",
    "vgr", "place", "t0", "t1", "t2", "rs0", "rs1", "a_s2", "t3", "vgf", "p3", "rs2", "t4",
    "rs3", "dh0", "rs4", "dh1", "r3", "dh2", "dh3", "dh4", "a_s3", "t5", "t6", "dh5", "dh6",
    "rs5", "rs6", "t7", "dh7", "rs7", "delta", "key",
)


def dot(a, b):
    return jnp.dot(a, b, preferred_element_type=F32)


def dot_t(a, b):
    return lax.dot_general(a, b, (((1,), (1,)), ((), ())), preferred_element_type=F32)


def iota(shape, dim):
    return lax.broadcasted_iota(jnp.int32, shape, dim)


def kernel(
    frames, vw, gw, taps, ow, text, low, aud, adapter, vp, q, k, g,
    dk_out, dh_out,
    W, AD, qs, gs, ks, low_s, lown, frames_s, vw_s, gw_s, taps_s, ow_s, text_s,
    slot_s, land_s, ext, glu_s, mixs, mixr, enc, adp, pick, inc, hid,
    e_ref, gv_ref, st_own, st_nxt, st_fp, st_fn, dl_own, dl_nxt, dl_fp, dl_fn,
    VG, psend, pown, precv, rsend, rrecv, vbuf, acc,
    ssem, rsem, lsem, aus, aur, rss, rsr,
):
    t = lax.axis_index("tm")
    c = lax.axis_index("ctx")
    x = lax.rem(t, NX)
    z = lax.div(t, NX)
    core = lax.rem(c, 2)
    yy = lax.div(c, 2)
    up = (lax.rem(z + 1, NZ) * NX + x, c)
    dn = (lax.rem(z + NZ - 1, NZ) * NX + x, c)
    nxt = (lax.rem(t + 1, NT), c)
    prv = (lax.rem(t + NT - 1, NT), c)
    mate = (t, c + 1 - 2 * core)

    def ctx_peer(d):
        return (t, lax.rem(c + d, NC))

    def x_peer(d):
        return (z * NX + lax.rem(x + d, NX), c)

    def zat(d):
        return lax.rem(z + d + NZ, NZ)

    def al(v, m):
        return pl.multiple_of(v, m)

    sends = []
    groups = {}
    waited = set()

    def send(name, src, dst, dev):
        i = len(sends)
        copy = pltpu.make_async_remote_copy(
            src_ref=src, dst_ref=dst, send_sem=ssem.at[i], recv_sem=rsem.at[i],
            device_id=dev, device_id_type=MESH,
        )
        copy.start()
        sends.append(copy)
        groups.setdefault(name, []).append(copy)

    def need(*names):
        for name in names:
            if name not in waited:
                waited.add(name)
                for copy in groups[name]:
                    if name in here:
                        copy.wait()
                    else:
                        copy.wait_recv()

    here = set()

    def local(name, src, dst):
        copy = pltpu.make_async_copy(src, dst, lsem.at[len(here)])
        copy.start()
        here.add(name)
        groups[name] = [copy]

    own_rows = pl.ds(al(c * 64, 64), 64)
    own_cols = pl.ds(al(c * HC, HC), HC)
    ad_rows = pl.ds(al(t * 32, 32), 32)
    rows_a = pl.ds(0, ROWS_A)
    rows_b = pl.ds(ROWS_A, ROWS_B)

    def issue():
        bar = pltpu.get_barrier_semaphore()

        def greet(d, carry):
            pl.semaphore_signal(bar, inc=1, device_id=(lax.rem(t + d, NT), c), device_id_type=MESH)
            return carry

        lax.fori_loop(1, NT, greet, 0)
        for d in range(1, NC):
            pl.semaphore_signal(bar, inc=1, device_id=ctx_peer(d), device_id_type=MESH)
        local("frames", frames, frames_s)
        local("vw", vw, vw_s)
        local("gw", gw, gw_s)
        local("vp", vp, W.at[t])
        local("ad", adapter, AD.at[ad_rows])
        local("taps", taps, taps_s)
        local("ow", ow, ow_s)
        local("k0", k.at[:, own_cols], ks.at[own_rows])
        local("q0", q.at[:, own_cols], qs.at[0, own_rows])
        local("g0", g.at[:, own_cols], gs.at[0, own_rows])
        local("text", text, text_s)
        low_s[...] = jnp.broadcast_to(low[...], low_s.shape)
        pl.semaphore_wait(bar, NT - 1 + NC - 1)
        send("fh", frames.at[pl.ds(AUD - 16, 16)], ext.at[pl.ds(0, 16)], nxt)
        send("fh", frames.at[pl.ds(0, 16)], ext.at[pl.ds(AUD + 16, 16)], prv)
        for d in (1, 3, 2):
            send("adx", adapter, AD.at[ad_rows], x_peer(d))
        send("low", low_s, lown, prv)

    def b_ref(zz, xx=x):
        return W.at[zz * NX + xx, rows_b]

    def b_part(zz, p):
        return W.at[zz * NX + x, pl.ds(ROWS_A + ROWS_B // 2 * p, ROWS_B // 2)]

    def a_ref(zz):
        return W.at[pl.ds(zz * NX, NX), rows_a]

    def a_part(zz, p):
        return W.at[pl.ds(zz * NX + 2 * p, 2), rows_a]

    def d_ref(zz):
        return AD.at[pl.ds(al(zz * 128, 128), 128)]

    def d_part(zz, p):
        return AD.at[pl.ds(al(zz * 128 + 64 * p, 64), 64)]

    def ring(name, s, ref_of, part_of):
        if s < NZ // 2 - 1:
            u, v = ref_of(zat(-s)), ref_of(zat(s))
        else:
            u, v = part_of(zat(-s), 0), part_of(zat(s), 1)
        send(f"{name}{s}", u, u, up)
        send(f"{name}{s}", v, v, dn)

    def a_step(s):
        need(*([f"a{s - 1}"] if s else ["ax", "vp"]))
        ring("a", s, a_ref, a_part)

    def b_step(s):
        need(*([f"b{s - 1}"] if s else ["vp"]))
        ring("b", s, b_ref, b_part)

    def d_step(s):
        need(*([f"d{s - 1}"] if s else ["adx", "ad"]))
        ring("d", s, d_ref, d_part)

    def reached(s):
        return (0,) if s < 0 else ((-1 - s, 1 + s) if s < 3 else (4,))

    def spread(s, d, kind):
        need(f"b{s}" if s >= 0 else "vp")
        for o in reached(s):
            send(f"{kind}{s}", b_ref(zat(o)), b_ref(zat(o)), x_peer(d))

    def relay(s):
        need(f"p{s}")
        behind = lax.rem(x + NX - 1, NX)
        for o in reached(s):
            send(f"r{s}", b_ref(zat(o), behind), b_ref(zat(o), behind), x_peer(1))

    def issue_ax():
        for d in (1, 3, 2):
            send("ax", vp.at[rows_a], W.at[t, rows_a], x_peer(d))

    def regroup(name, src, dst):
        for d in (1, 7, 2, 6, 3, 5, 4):
            peer = lax.rem(c + d, NC)
            send(name, src.at[:, pl.ds(al(peer * HC, HC), HC)], dst.at[own_rows], (t, peer))

    def positions():
        order = (iota((AUD, AUD), 0) < iota((AUD, AUD), 1)).astype(F32).astype(BF16)
        own = aud[pl.ds(t, 1), :]
        target = own // TOK
        hit = (iota((NT, AUD), 0) == target).astype(F32)
        rank = jnp.sum(dot(hit.astype(BF16), order) * hit, axis=0, keepdims=True)
        slot = target * SLOT + rank.astype(jnp.int32)
        slot_s[...] = jnp.broadcast_to(slot, slot_s.shape)
        table = aud[...]
        landing = table // TOK == t
        landing_rank = dot(landing.astype(F32).astype(BF16), order)
        spot = jnp.where(landing, table - t * TOK + 1, 0)
        n = NT * 16
        grow = (iota((n, NT), 0) // 16 == iota((n, NT), 1)).astype(F32).astype(BF16)
        spot_hi = dot(grow, (spot // 16).astype(F32).astype(BF16))
        spot_lo = dot(grow, (spot % 16).astype(F32).astype(BF16))
        ranks = dot(grow, jnp.where(landing, landing_rank, 64.0).astype(BF16))
        place = spot_hi * 16.0 + spot_lo
        r = (iota((n, AUD), 0) % 16).astype(F32)
        eye = iota((n, n), 0) == iota((n, n), 1)
        for half in range(2):
            col = jnp.sum(jnp.where(ranks == r - 8.0 * half, place, 0.0), axis=1, keepdims=True) - 1.0
            line = jnp.sum(jnp.where(eye, col, 0.0), axis=0, keepdims=True)
            land_s[half] = jnp.broadcast_to(line, (8, n)).astype(jnp.int32)

    def norm_glu():
        need("frames", "vw", "gw")
        ext[pl.ds(16, AUD), :] = frames_s[...]
        need("fh")
        rows = ext[...].astype(F32)
        centre = jnp.mean(rows, axis=1, keepdims=True)
        off = rows - centre
        spread_ = jnp.mean(off * off, axis=1, keepdims=True)
        normed = (off * lax.rsqrt(spread_ + NORM_EPS)).astype(BF16)
        value_part = dot(normed, vw_s[...])
        gate_part = dot(normed, gw_s[...])
        glu = (value_part * jax.nn.sigmoid(gate_part)).astype(BF16).astype(F32)
        row = iota(glu.shape, 0)
        first = jnp.where(t == 0, 16, 0)
        last = jnp.where(t == NT - 1, AUD + 16, AUD + 32)
        glu_s[...] = jnp.where((row >= first) & (row < last), glu, 0.0)

    def conv():
        need("taps", "ow")
        smooth = jnp.zeros((AUD, DH), F32)
        for j in range(taps_s.shape[0]):
            smooth = smooth + taps_s[pl.ds(j, 1), :] * glu_s[pl.ds(1 + j, AUD), :]
        action = (smooth * jax.nn.sigmoid(smooth)).astype(BF16)
        mixs[...] = dot(action, ow_s[...]).astype(BF16)
        for d in (4, 2, 6, 3, 5, 1, 7):
            rows_d = pl.ds(al(lax.rem(c + d, NC) * 16, 16), 16)
            send("mix", mixs.at[rows_d], mixr.at[d], ctx_peer(d))

    def encode():
        need("mix")
        mine = pl.ds(al(c * 16, 16), 16)
        total = frames_s[mine, :].astype(F32) + mixs[mine, :].astype(F32)
        for d in range(1, NC):
            total = total + mixr[d].astype(F32)
        enc[mine, :] = total.astype(BF16)
        for d in (4, 2, 6, 3, 5, 1, 7):
            send("enc", enc.at[mine], enc.at[mine], ctx_peer(d))

    def halo(name):
        part = qs if name == "q" else gs
        need(name, name + "0")
        send("h" + name, part.at[0], part.at[1], prv)

    scale = 1.0 / math.sqrt(DH)
    base = t * TOK
    row8 = iota((8, HALF), 0)

    def head_cols(h):
        return pl.ds(al(h * DH, DH), DH)

    def score_tiles(block, lows, limit, stats):
        def one_head(h, carry):
            hs = head_cols(h)
            for b, i0, j0, jn in TILES:
                if b != block:
                    continue
                qi = pl.ds(i0, HALF)
                s = dot_t(ks[pl.ds(j0, jn), hs], qs[b, qi, hs]) * scale
                jj = iota((jn, HALF), 0) + j0
                ok = jj >= lows[pl.ds(0, 1), qi] - base
                if block == 0:
                    ok = ok & (jj <= iota((jn, HALF), 1) + i0)
                else:
                    ok = ok & (jj < limit)
                s = jnp.where(ok, s, MASK_FILL)
                m = jnp.max(s, axis=0, keepdims=True)
                e = jnp.where(ok, jnp.exp(s - m), 0.0)
                n = jnp.sum(e, axis=0, keepdims=True)
                e_ref[b, h, pl.ds(j0, jn), qi] = e
                stats[h, :, qi] = jnp.where(row8 == 0, m, n)
            return carry

        lax.fori_loop(0, HH, one_head, 0)

    def score_own():
        need("k", "k0", "q", "q0")
        score_tiles(0, low_s, TOK, st_own)
        send("sta", st_own, st_fn, prv)

    def score_next():
        need("k", "k0", "hq", "low")
        score_tiles(1, lown, jnp.where(t == NT - 1, 0, TOK), st_nxt)
        send("stb", st_nxt, st_fp, nxt)

    my_slot = pl.ds(al(t * 16, 16), 16)

    def audio_copy(d):
        peer = lax.rem(t + d, NT)
        return pltpu.make_async_remote_copy(
            src_ref=pick.at[pl.ds(al(peer * 16, 16), 16)], dst_ref=inc.at[my_slot],
            send_sem=aus.at[d], recv_sem=aur.at[d], device_id=(peer, c), device_id_type=MESH,
        )

    def adapt():
        need("d3", "enc")
        for n in range(4):
            cols = pl.ds(256 * n, 256)
            adp[:, cols] = dot(enc[...], AD[:, cols]).astype(BF16)
        slot_row = iota((NT * 16, AUD), 0)
        picker = ((slot_row // 16) * SLOT + slot_row % SLOT == slot_s[pl.ds(0, 1), :]).astype(F32)
        picker = picker.astype(BF16)
        low_half = dot(picker, adp[:, pl.ds(0, 512)])
        high_half = dot(picker, adp[:, pl.ds(512, 512)])
        upper = iota((NT * 16, 512), 0) % 16 < SLOT
        pick[...] = jnp.where(upper, low_half, high_half).astype(BF16)

        def audio_start(d, carry):
            audio_copy(d).start()
            return carry

        lax.fori_loop(1, NT, audio_start, 0)
        inc[my_slot, :] = pick[my_slot, :]

    def factor(mine_st, other_st, h):
        m1, s1 = mine_st[h, pl.ds(0, 1), :], mine_st[h, pl.ds(1, 1), :]
        m2, s2 = other_st[h, pl.ds(0, 1), :], other_st[h, pl.ds(1, 1), :]
        m = jnp.maximum(m1, m2)
        a1 = jnp.exp(m1 - m)
        return a1 / (s1 * a1 + s2 * jnp.exp(m2 - m))

    def gather_terms(tiles, other, h):
        hs = head_cols(h)
        first, second = pl.ds(0, 256), pl.ds(256, 256)
        top = dot(tiles[0], other[0, first, hs]) + dot(tiles[1][:256], other[0, second, hs])
        top = top + dot(tiles[2][:256], other[1, first, hs])
        bottom = dot(tiles[1][256:], other[0, second, hs])
        bottom = bottom + dot(tiles[2][256:], other[1, first, hs])
        bottom = bottom + dot(tiles[3], other[1, second, hs])
        return top, bottom

    def prob():
        need("sta", "stb", "g", "g0", "hg")

        def prob_head(h, carry):
            f = (factor(st_own, st_fp, h), factor(st_nxt, st_fn, h))
            tiles = []
            for b, i0, j0, jn in TILES:
                p = e_ref[b, h, pl.ds(j0, jn), pl.ds(i0, HALF)] * f[b][:, i0 : i0 + HALF]
                e_ref[b, h, pl.ds(j0, jn), pl.ds(i0, HALF)] = p
                tiles.append(p.astype(BF16))
            top, bottom = gather_terms(tiles, gs, h)
            hs = head_cols(h)
            VG[c, pl.ds(0, 256), hs] = top.astype(BF16)
            VG[c, pl.ds(256, 256), hs] = bottom.astype(BF16)
            return carry

        lax.fori_loop(0, HH, prob_head, 0)
        send("vg1", VG.at[c], VG.at[c], ctx_peer(2))
        send("vg3", VG.at[c], VG.at[c], ctx_peer(6))
        send("vgc", VG.at[c], VG.at[c], mate)

    below, above, across = [lax.rem(c + d, NC) for d in (6, 2, 4)]

    def vg_relay():
        need("vg1", "vg3")
        one, two = VG.at[below, pl.ds(0, 256)], VG.at[above, pl.ds(256, 256)]
        send("vg2", one, one, ctx_peer(2))
        send("vg2", two, two, ctx_peer(6))
        send("vgc", VG.at[below], VG.at[below], mate)
        send("vgc", VG.at[above], VG.at[above], mate)

    def vg_last():
        need("vg2")
        send("vgc", VG.at[across], VG.at[across], mate)

    def place():
        need("text")

        def audio_arrived(d, carry):
            audio_copy(d).wait_recv()
            return carry

        lax.fori_loop(1, NT, audio_arrived, 0)
        for half in range(2):
            cols = pl.ds(512 * half, 512)
            hits = (iota((TOK, NT * 16), 0) == land_s[half, pl.ds(0, 1), :]).astype(F32)
            there = jnp.sum(hits, axis=1, keepdims=True) > 0.5
            rows_in = dot(hits.astype(BF16), inc[...])
            hid[:, cols] = jnp.where(there, rows_in, text_s[:, cols].astype(F32)).astype(BF16)

    mate_rows = pl.ds(al((1 - core) * HALF, HALF), HALF)
    my_rows = pl.ds(al(core * HALF, HALF), HALF)

    def weights_ready(i):
        s = (i - 1) // 2
        need(f"m{s}", f"p{s}", f"r{s}")
        need(*([f"a{s}", f"b{s}"] if i else ["ax", "vp"]))

    def terms(i):
        weights_ready(i)
        cp = zat(OFFSETS[i])
        w = jnp.concatenate([W[cp * HH + j] for j in range(HH)], axis=1)
        psend[i] = dot(hid[mate_rows, :], w).astype(BF16)
        send(f"pair{i}", psend.at[i], precv.at[i], mate)
        w = jnp.concatenate([W[cp * HH + j] for j in range(HH)], axis=1)
        pown[i] = dot(hid[my_rows, :], w).astype(BF16)

    def group_copy(d, i):
        return pltpu.make_async_remote_copy(
            src_ref=rsend.at[i], dst_ref=rrecv.at[yy, my_rows],
            send_sem=rss.at[d], recv_sem=rsr.at[d],
            device_id=(t, lax.rem(c + d, NC)), device_id_type=MESH,
        )

    def chip_sum(i):
        cp = zat(OFFSETS[i])
        d = lax.rem(cp - c + NC, NC)
        need(f"pair{i}")
        total = pown[i].astype(F32) + precv[i].astype(F32)
        rsend[i] = total.astype(BF16)

        @pl.when(d != 0)
        def _():
            group_copy(d, i).start()

        @pl.when(d == 0)
        def _():
            rrecv[yy, my_rows, :] = rsend[i]

    added = []

    def hidden_grad(i):
        weights_ready(i)
        need("vgc")
        cp = zat(OFFSETS[i])
        added.append(i)
        first, last = len(added) == 1, len(added) == NC

        def part(n, carry):
            rows_n = pl.ds(al(n * 256, 256), 256)
            w = jnp.concatenate([W[cp * HH + j, rows_n, :] for j in range(HH)], axis=1)
            term = dot_t(VG[cp], w)
            if not first:
                term = term + acc[n]
            if last:
                dh_out[:, rows_n] = term.astype(BF16)
            else:
                acc[n] = term
            return carry

        lax.fori_loop(0, COLS // 256, part, 0)

    def delta():
        for d in range(1, NC):
            group_copy(d, 0).wait_recv()
        total = rrecv[0].astype(F32)
        for y in range(1, NC // 2):
            total = total + rrecv[y].astype(F32)
        vbuf[...] = total.astype(BF16)

        def delta_head(h, carry):
            hs = head_cols(h)
            for b, i0, j0, jn in TILES:
                qi = pl.ds(i0, HALF)
                gv = dot_t(vbuf[pl.ds(j0, jn), hs], gs[b, qi, hs])
                gv_ref[b, h, pl.ds(j0, jn), qi] = gv
                w = e_ref[b, h, pl.ds(j0, jn), qi].astype(BF16).astype(F32)
                part = jnp.sum(w * gv, axis=0, keepdims=True)
                table = dl_own if b == 0 else dl_nxt
                table[h, :, qi] = jnp.where(row8 == 0, part, 0.0)
            return carry

        lax.fori_loop(0, HH, delta_head, 0)
        send("dl", dl_own, dl_fn, prv)
        send("dl", dl_nxt, dl_fp, nxt)

    def key():
        need("dl")

        def key_head(h, carry):
            deltas = (
                dl_own[h, pl.ds(0, 1), :] + dl_fp[h, pl.ds(0, 1), :],
                dl_nxt[h, pl.ds(0, 1), :] + dl_fn[h, pl.ds(0, 1), :],
            )
            tiles = []
            for b, i0, j0, jn in TILES:
                qi = pl.ds(i0, HALF)
                p = e_ref[b, h, pl.ds(j0, jn), qi]
                gv = gv_ref[b, h, pl.ds(j0, jn), qi]
                tiles.append((p * (gv - deltas[b][:, i0 : i0 + HALF])).astype(BF16))
            top, bottom = gather_terms(tiles, qs, h)
            hs = head_cols(h)
            dk_out[pl.ds(0, 256), hs] = (top * scale).astype(BF16)
            dk_out[pl.ds(256, 256), hs] = (bottom * scale).astype(BF16)
            return carry

        lax.fori_loop(0, HH, key_head, 0)

    steps = {
        "issue": issue, "i_ax": issue_ax,
        "i_b0": lambda: b_step(0), "i_bm": lambda: spread(-1, 1, "p"), "mm": lambda: spread(-1, 3, "m"),
        "i_k": lambda: regroup("k", k, ks),
        "i_q": lambda: regroup("q", q, qs.at[0]),
        "i_g": lambda: regroup("g", g, gs.at[0]),
        "pos": positions, "LN": norm_glu, "conv": conv, "enc": encode, "adapt": adapt, "place": place,
        "hq": lambda: halo("q"), "hg": lambda: halo("g"),
        "sc0": score_own, "sc1": score_next, "prob": prob, "vgr": vg_relay, "vgf": vg_last,
        "rm": lambda: relay(-1), "delta": delta, "key": key,
    }
    for s in range(4):
        steps[f"a_s{s}"] = lambda s=s: a_step(s)
        steps[f"b_s{s}"] = lambda s=s: b_step(s)
        steps[f"d_s{s}"] = lambda s=s: d_step(s)
        steps[f"p{s}"] = lambda s=s: spread(s, 1, "p")
        steps[f"m{s}"] = lambda s=s: spread(s, 3, "m")
        steps[f"r{s}"] = lambda s=s: relay(s)
    for i in range(NC):
        steps[f"t{i}"] = lambda i=i: terms(i)
        steps[f"rs{i}"] = lambda i=i: chip_sum(i)
        steps[f"dh{i}"] = lambda i=i: hidden_grad(i)
    for name in ORDER:
        steps[name]()

    def audio_sent(d, carry):
        audio_copy(d).wait_send()
        return carry

    lax.fori_loop(1, NT, audio_sent, 0)
    for d in range(1, NC):
        group_copy(d, 0).wait_send()
    for name in groups:
        need(name)
    for copy in sends:
        copy.wait_send()


def body(
    frames, value_weight, gate_weight, conv_taps, out_weight, adapter, audio_pos, text_rows,
    value_proj, queries, keys, grad_out, window_low,
):
    vm = pl.BlockSpec(memory_space=pltpu.VMEM)
    hbm = pl.BlockSpec(memory_space=pl.ANY)
    vmem = pltpu.VMEM
    dma = pltpu.SemaphoreType.DMA
    return pl.pallas_call(
        kernel,
        out_shape=(
            jax.ShapeDtypeStruct((TOK, HC), BF16),
            jax.ShapeDtypeStruct((TOK, COLS), BF16),
        ),
        in_specs=[hbm] * 6 + [vm] * 2 + [hbm] * 5,
        out_specs=(vm, vm),
        scratch_shapes=[
            vmem((NT, COLS, DH), BF16),
            vmem((DE, COLS), BF16),
            vmem((2, TOK, HC), BF16),
            vmem((2, TOK, HC), BF16),
            vmem((TOK, HC), BF16),
            vmem((8, TOK), jnp.int32),
            vmem((8, TOK), jnp.int32),
            vmem((AUD, DE), BF16),
            vmem((DE, DH), BF16),
            vmem((DE, DH), BF16),
            vmem(conv_taps.shape, F32),
            vmem((DH, DE), BF16),
            vmem((TOK, COLS), BF16),
            vmem((8, AUD), jnp.int32),
            vmem((2, 8, NT * 16), jnp.int32),
            vmem((AUD + 32, DE), BF16),
            vmem((AUD + 32, DH), F32),
            vmem((AUD, DE), BF16),
            vmem((NC, 16, DE), BF16),
            vmem((AUD, DE), BF16),
            vmem((AUD, COLS), BF16),
            vmem((NT * 16, 512), BF16),
            vmem((NT * 16, 512), BF16),
            vmem((TOK, COLS), BF16),
            vmem((2, HH, TOK, TOK), F32),
            vmem((2, HH, TOK, TOK), F32),
        ]
        + [vmem((HH, 8, TOK), F32)] * 8
        + [
            vmem((NC, TOK, HC), BF16),
            vmem((NC, HALF, HC), BF16),
            vmem((NC, HALF, HC), BF16),
            vmem((NC, HALF, HC), BF16),
            vmem((NC, HALF, HC), BF16),
            vmem((NC // 2, TOK, HC), BF16),
            vmem((TOK, HC), BF16),
            vmem((COLS // 256, TOK, 256), F32),
            dma((N_SEMS,)),
            dma((N_SEMS,)),
            dma((16,)),
            dma((NT,)),
            dma((NT,)),
            dma((NC,)),
            dma((NC,)),
        ],
        compiler_params=pltpu.CompilerParams(
            collective_id=0, has_side_effects=True, vmem_limit_bytes=60 * 1024 * 1024
        ),
        cost_estimate=pl.CostEstimate(flops=13_000_000_000, bytes_accessed=8_000_000, transcendentals=4_000_000),
    )(
        frames, value_weight, gate_weight, conv_taps, out_weight, text_rows,
        window_low.reshape(1, TOK), audio_pos.reshape(NT, AUD),
        adapter, value_proj, queries, keys, grad_out,
    )


def solution(mesh):
    return jax.shard_map(
        body,
        mesh=mesh,
        in_specs=(
            P("tm", None),
            P(None, "ctx"),
            P(None, "ctx"),
            P(None, "ctx"),
            P("ctx", None),
            P("tm", "ctx"),
            P(),
            P("tm", "ctx"),
            P("ctx", "tm"),
            P(("tm", "ctx"), None),
            P(("tm", "ctx"), None),
            P(("tm", "ctx"), None),
            P("tm"),
        ),
        out_specs=(P("tm", "ctx"), P("tm", "ctx")),
        check_vma=False,
    )
```

time: 165 us -> 153 us (0.927); the launches traced: 162 us -> 153 us
  local copies, waits for them, and re-layouts: 6.96 us -> 2.93 us
  Pallas kernels: 153 us -> 150 us
    pallas_call x1, Pallas kernels: 153 us -> 150 us  [body(): pl.pallas_call(kernel, out_shape=(jax.ShapeDtypeStruct((TOK, HC), BF16),...]
    broadcast_in_dim x6 -> x0, local copies, waits for them, and re-layouts: 2.58 us -> none  [the longest x5 1.97 us: positions(): eight = lambda a: jnp.broadcast_to(a, (8, a.shape[-1]))]
    unnamed x8 -> x4, local copies, waits for them, and re-layouts: 4.3 us -> 2.93 us
where the time goes in v2:
time: 153 us
  Pallas kernels  150 us (98%)
  local copies, waits for them, and re-layouts  2.93 us (2%)
    pallas_call x1, Pallas kernels, body(): pl.pallas_call(kernel, out_shape=(jax.ShapeDtypeStruct((TOK, HC), BF16),...  150 us

profile of v2, /device:TPU:9, one launch (start us, length us, event | category | flops | bytes accessed | tf_op | source)
XLA Modules:
  0.0 153.3 jit_solution(9527180804876216885)
XLA Ops:
  0.6 149.7 %shard_map.140 = (bf16[512,512]{1,0:T(8,128)(2,1)}, bf16[512,1024]{1,0:T(8,128)(2,1)}) custom-call(bf16[128,1024]{1,0:T(8,128)(2,1)} %frames.1, bf16[1024,128]{1,0:T(8,128)(2,1)} %vw.1, bf16[1024,128]{1,0:T(8,128)(2,1)} %gw.1, f32[31,128]{1,0:T(8,128)} %taps.1, bf16[128,1024]{1,0:T(8,128)(2,1)} %ow.1, bf16[512,1024]{1,0:T(8,128)(2,1)} %text.1, ...), custom_call_target="tpu_custom_call" | custom-call | flops 12999999488 | bytes 8000000 | tf_op jit(solution)/shard_map/pallas_call | solution.py:576
  150.3 0.0 copy-start
  150.3 2.0 %copy.17 = bf16[512,512]{1,0:T(8,128)(2,1)} copy(bf16[512,512]{1,0:T(8,128)(2,1)} %get-tuple-element.4) | data formatting | bytes 1048576
  152.3 0.0 copy-done
  152.3 1.0 copy.18
Async XLA Ops:
  150.3 2.0 %copy-start = (bf16[512,1024]{1,0:T(8,128)(2,1)S(1)}, bf16[512,1024]{1,0:T(8,128)(2,1)}, u32[]{:S(2)}) copy-start(bf16[512,1024]{1,0:T(8,128)(2,1)} %get-tuple-element.5) | copy-start | bytes 3145732

commit v3 on v2

--- a/solution.py
+++ b/solution.py
@@ -28,16 +28,17 @@
 SLOT = 8
 TILES = ((0, 0, 0, 256), (0, 256, 0, 512), (1, 0, 0, 512), (1, 256, 256, 256))
 N_SEMS = 160
-ROWS_A = 384
+ROWS_A = 352
 ROWS_B = COLS - ROWS_A
 OFFSETS = (0, -1, 1, -2, 2, -3, 3, 4)
 ORDER = (
-    "issue", "i_b0", "i_k", "i_q", "mm", "pos", "LN", "d_s0", "i_bm", "p0", "m0", "conv",
-    "d_s1", "b_s1", "i_ax", "hq", "rm", "sc0", "i_g", "enc", "b_s2", "p1", "d_s2", "r0", "hg",
-    "p2", "d_s3", "b_s3", "a_s0", "sc1", "m3", "adapt", "r1", "m1", "m2", "prob", "a_s1", "r2",
-    "vgr", "place", "t0", "t1", "t2", "rs0", "rs1", "a_s2", "t3", "vgf", "p3", "rs2", "t4",
-    "rs3", "dh0", "rs4", "dh1", "r3", "dh2", "dh3", "dh4", "a_s3", "t5", "t6", "dh5", "dh6",
-    "rs5", "rs6", "t7", "dh7", "rs7", "delta", "key",
+    "issue", "i_b0", "i_k", "i_q", "i_ax", "mm", "b_s1", "p0", "m0", "LN", "fk", "fq", "conv",
+    "i_g", "d_s0", "b_s2", "i_bm", "rm", "hq", "sc0", "b_s3", "pos", "enc", "fg", "d_s1", "r0",
+    "p3", "hg", "d_s2", "d_s3", "a_s0", "p1", "sc1", "adapt", "m1", "p2", "m2", "m3", "prob",
+    "r1", "a_s1", "r3", "vgr", "place", "t0", "t1", "r2", "vgf", "t2", "rs0", "a_s2", "t3",
+    "rs1", "t4", "rs2", "ad0", "dh0", "rs3", "dh1", "ad1", "rs4", "dh2", "dh3", "dh4", "ad2",
+    "a_s3", "t5", "ad3", "t6", "ad4", "dh5", "rs5", "dh6", "rs6", "t7", "dh7", "ad5", "ad6",
+    "rs7", "ad7", "delta", "key",
 )
 
 
@@ -59,7 +60,7 @@
     W, AD, qs, gs, ks, low_s, lown, frames_s, vw_s, gw_s, taps_s, ow_s, text_s,
     slot_s, land_s, ext, glu_s, mixs, mixr, enc, adp, pick, inc, hid,
     e_ref, gv_ref, st_own, st_nxt, st_fp, st_fn, dl_own, dl_nxt, dl_fp, dl_fn,
-    VG, psend, pown, precv, rsend, rrecv, vbuf, acc,
+    VG, psend, pown, precv, rsend, radd, rrecv, vbuf, acc, stage,
     ssem, rsem, lsem, aus, aur, rss, rsr,
 ):
     t = lax.axis_index("tm")
@@ -200,19 +201,35 @@
             send(f"{kind}{s}", b_ref(zat(o)), b_ref(zat(o)), x_peer(d))
 
     def relay(s):
-        need(f"p{s}")
-        behind = lax.rem(x + NX - 1, NX)
+        turn = 3 if s in (-1, 3) else 1
+        need(f"p{s}" if turn == 1 else f"m{s}")
+        origin = lax.rem(x + NX - turn, NX)
         for o in reached(s):
-            send(f"r{s}", b_ref(zat(o), behind), b_ref(zat(o), behind), x_peer(1))
+            send(f"r{s}", b_ref(zat(o), origin), b_ref(zat(o), origin), x_peer(turn))
 
     def issue_ax():
         for d in (1, 3, 2):
             send("ax", vp.at[rows_a], W.at[t, rows_a], x_peer(d))
 
-    def regroup(name, src, dst):
-        for d in (1, 7, 2, 6, 3, 5, 4):
-            peer = lax.rem(c + d, NC)
-            send(name, src.at[:, pl.ds(al(peer * HC, HC), HC)], dst.at[own_rows], (t, peer))
+    def beside(cc):
+        return cc + 1 - 2 * core
+
+    def regroup(name, src, dst, stage):
+        y_up, y_dn, far = [lax.rem(c + d, NC) for d in (2, 6, 4)]
+
+        def piece(peer):
+            return src.at[:, pl.ds(al(peer * HC, HC), HC)]
+
+        send(name + "s", piece(far), stage.at[0], (t, y_up))
+        send(name + "s", piece(beside(far)), stage.at[1], (t, y_dn))
+        for peer in (y_up, y_dn, beside(y_up), beside(y_dn), beside(c)):
+            send(name, piece(peer), dst.at[own_rows], (t, peer))
+
+    def regroup_relay(name, dst, stage):
+        need(name + "s")
+        y_up, y_dn = [lax.rem(c + d, NC) for d in (2, 6)]
+        send(name + "2", stage.at[0], dst.at[pl.ds(al(y_dn * 64, 64), 64)], (t, y_up))
+        send(name + "2", stage.at[1], dst.at[pl.ds(al(y_up * 64, 64), 64)], (t, beside(y_dn)))
 
     def positions():
         order = (iota((AUD, AUD), 0) < iota((AUD, AUD), 1)).astype(F32).astype(BF16)
@@ -279,7 +296,7 @@
 
     def halo(name):
         part = qs if name == "q" else gs
-        need(name, name + "0")
+        need(name, name + "2", name + "0")
         send("h" + name, part.at[0], part.at[1], prv)
 
     scale = 1.0 / math.sqrt(DH)
@@ -314,12 +331,12 @@
         lax.fori_loop(0, HH, one_head, 0)
 
     def score_own():
-        need("k", "k0", "q", "q0")
+        need("k", "k2", "k0", "q", "q2", "q0")
         score_tiles(0, low_s, TOK, st_own)
         send("sta", st_own, st_fn, prv)
 
     def score_next():
-        need("k", "k0", "hq", "low")
+        need("k", "k2", "k0", "hq", "low")
         score_tiles(1, lown, jnp.where(t == NT - 1, 0, TOK), st_nxt)
         send("stb", st_nxt, st_fp, nxt)
 
@@ -370,7 +387,7 @@
         return top, bottom
 
     def prob():
-        need("sta", "stb", "g", "g0", "hg")
+        need("sta", "stb", "g", "g2", "g0", "hg")
 
         def prob_head(h, carry):
             f = (factor(st_own, st_fp, h), factor(st_nxt, st_fn, h))
@@ -436,27 +453,62 @@
         w = jnp.concatenate([W[cp * HH + j] for j in range(HH)], axis=1)
         pown[i] = dot(hid[my_rows, :], w).astype(BF16)
 
-    def group_copy(d, i):
+    def owner_copy(side, kd, i):
+        owner = lax.rem(yy + 1 + 2 * side, NC // 2) * 2 + kd
         return pltpu.make_async_remote_copy(
-            src_ref=rsend.at[i], dst_ref=rrecv.at[yy, my_rows],
-            send_sem=rss.at[d], recv_sem=rsr.at[d],
-            device_id=(t, lax.rem(c + d, NC)), device_id_type=MESH,
+            src_ref=rsend.at[i], dst_ref=rrecv.at[1 + side, my_rows],
+            send_sem=rss.at[2 * side + kd], recv_sem=rsr.at[2 * side + core],
+            device_id=(t, owner), device_id_type=MESH,
         )
 
+    def add_copy(kd, i):
+        return pltpu.make_async_remote_copy(
+            src_ref=rsend.at[i], dst_ref=radd.at[kd],
+            send_sem=rss.at[4 + kd], recv_sem=rsr.at[4 + kd],
+            device_id=(t, lax.rem(c + 2 + 4 * core, NC)), device_id_type=MESH,
+        )
+
+    def mate_copy(i):
+        return pltpu.make_async_remote_copy(
+            src_ref=rsend.at[i], dst_ref=rrecv.at[0, my_rows],
+            send_sem=rss.at[6], recv_sem=rsr.at[6], device_id=mate, device_id_type=MESH,
+        )
+
+    def owner_of(i):
+        cp = zat(OFFSETS[i])
+        return lax.rem(lax.div(cp, 2) - yy + NC // 2, NC // 2), lax.rem(cp, 2)
+
     def chip_sum(i):
-        cp = zat(OFFSETS[i])
-        d = lax.rem(cp - c + NC, NC)
+        e, kd = owner_of(i)
         need(f"pair{i}")
         total = pown[i].astype(F32) + precv[i].astype(F32)
         rsend[i] = total.astype(BF16)
 
-        @pl.when(d != 0)
+        @pl.when(e == 2)
         def _():
-            group_copy(d, i).start()
-
-        @pl.when(d == 0)
+            add_copy(kd, i).start()
+
+        @pl.when(e == 3 - 2 * core)
         def _():
-            rrecv[yy, my_rows, :] = rsend[i]
+            owner_copy(lax.div(e, 2), kd, i).start()
+
+        @pl.when((e == 0) & (kd != core))
+        def _():
+            mate_copy(i).start()
+
+        @pl.when((e == 0) & (kd == core))
+        def _():
+            rrecv[0, my_rows, :] = rsend[i]
+
+    def added_sum(i):
+        e, kd = owner_of(i)
+
+        @pl.when(e == 1 + 2 * core)
+        def _():
+            add_copy(kd, i).wait_recv()
+            total = rsend[i].astype(F32) + radd[kd].astype(F32)
+            rsend[i] = total.astype(BF16)
+            owner_copy(lax.div(e, 2), kd, i).start()
 
     added = []
 
@@ -482,11 +534,12 @@
         lax.fori_loop(0, COLS // 256, part, 0)
 
     def delta():
-        for d in range(1, NC):
-            group_copy(d, 0).wait_recv()
-        total = rrecv[0].astype(F32)
-        for y in range(1, NC // 2):
-            total = total + rrecv[y].astype(F32)
+        for n in (0, 1, 2, 3, 6):
+            pltpu.make_async_remote_copy(
+                src_ref=rsend.at[0], dst_ref=rrecv.at[0, my_rows], send_sem=rss.at[n],
+                recv_sem=rsr.at[n], device_id=mate, device_id_type=MESH,
+            ).wait_recv()
+        total = rrecv[0].astype(F32) + rrecv[1].astype(F32) + rrecv[2].astype(F32)
         vbuf[...] = total.astype(BF16)
 
         def delta_head(h, carry):
@@ -530,9 +583,12 @@
     steps = {
         "issue": issue, "i_ax": issue_ax,
         "i_b0": lambda: b_step(0), "i_bm": lambda: spread(-1, 1, "p"), "mm": lambda: spread(-1, 3, "m"),
-        "i_k": lambda: regroup("k", k, ks),
-        "i_q": lambda: regroup("q", q, qs.at[0]),
-        "i_g": lambda: regroup("g", g, gs.at[0]),
+        "i_k": lambda: regroup("k", k, ks, stage.at[0]),
+        "i_q": lambda: regroup("q", q, qs.at[0], stage.at[1]),
+        "i_g": lambda: regroup("g", g, gs.at[0], stage.at[2]),
+        "fk": lambda: regroup_relay("k", ks, stage.at[0]),
+        "fq": lambda: regroup_relay("q", qs.at[0], stage.at[1]),
+        "fg": lambda: regroup_relay("g", gs.at[0], stage.at[2]),
         "pos": positions, "LN": norm_glu, "conv": conv, "enc": encode, "adapt": adapt, "place": place,
         "hq": lambda: halo("q"), "hg": lambda: halo("g"),
         "sc0": score_own, "sc1": score_next, "prob": prob, "vgr": vg_relay, "vgf": vg_last,
@@ -548,6 +604,7 @@
     for i in range(NC):
         steps[f"t{i}"] = lambda i=i: terms(i)
         steps[f"rs{i}"] = lambda i=i: chip_sum(i)
+        steps[f"ad{i}"] = lambda i=i: added_sum(i)
         steps[f"dh{i}"] = lambda i=i: hidden_grad(i)
     for name in ORDER:
         steps[name]()
@@ -557,8 +614,11 @@
         return carry
 
     lax.fori_loop(1, NT, audio_sent, 0)
-    for d in range(1, NC):
-        group_copy(d, 0).wait_send()
+    for n in range(7):
+        pltpu.make_async_remote_copy(
+            src_ref=rsend.at[0], dst_ref=rrecv.at[0, my_rows], send_sem=rss.at[n],
+            recv_sem=rsr.at[n], device_id=mate, device_id_type=MESH,
+        ).wait_send()
     for name in groups:
         need(name)
     for copy in sends:
@@ -616,9 +676,11 @@
             vmem((NC, HALF, HC), BF16),
             vmem((NC, HALF, HC), BF16),
             vmem((NC, HALF, HC), BF16),
-            vmem((NC // 2, TOK, HC), BF16),
+            vmem((2, HALF, HC), BF16),
+            vmem((3, TOK, HC), BF16),
             vmem((TOK, HC), BF16),
             vmem((COLS // 256, TOK, 256), F32),
+            vmem((3, 2, 64, HC), BF16),
             dma((N_SEMS,)),
             dma((N_SEMS,)),
             dma((16,)),

time: 153 us -> 158 us (1.033)
  Pallas kernels: 150 us -> 154 us
    pallas_call x1, Pallas kernels: 150 us -> 154 us  [body(): pl.pallas_call(kernel, out_shape=(jax.ShapeDtypeStruct((TOK, HC), BF16),...]
where the time goes in v3:
time: 158 us
  Pallas kernels  154 us (97%)
  local copies, waits for them, and re-layouts  2.93 us (2%)
    pallas_call x1, Pallas kernels, body(): pl.pallas_call(kernel, out_shape=(jax.ShapeDtypeStruct((TOK, HC), BF16),...  154 us

profile of v3, /device:TPU:9, one launch (start us, length us, event | category | flops | bytes accessed | tf_op | source)
XLA Modules:
  0.0 157.7 jit_solution(5175929025362224542)
XLA Ops:
  0.6 154.1 %shard_map.140 = (bf16[512,512]{1,0:T(8,128)(2,1)}, bf16[512,1024]{1,0:T(8,128)(2,1)}) custom-call(bf16[128,1024]{1,0:T(8,128)(2,1)} %frames.1, bf16[1024,128]{1,0:T(8,128)(2,1)} %vw.1, bf16[1024,128]{1,0:T(8,128)(2,1)} %gw.1, f32[31,128]{1,0:T(8,128)} %taps.1, bf16[128,1024]{1,0:T(8,128)(2,1)} %ow.1, bf16[512,1024]{1,0:T(8,128)(2,1)} %text.1, ...), custom_call_target="tpu_custom_call" | custom-call | flops 12999999488 | bytes 8000000 | tf_op jit(solution)/shard_map/pallas_call | solution.py:636
  154.7 0.0 copy-start
  154.7 2.0 %copy.17 = bf16[512,512]{1,0:T(8,128)(2,1)} copy(bf16[512,512]{1,0:T(8,128)(2,1)} %get-tuple-element.4) | data formatting | bytes 1048576
  156.7 0.0 copy-done
  156.7 1.0 copy.18
Async XLA Ops:
  154.7 2.0 %copy-start = (bf16[512,1024]{1,0:T(8,128)(2,1)S(1)}, bf16[512,1024]{1,0:T(8,128)(2,1)}, u32[]{:S(2)}) copy-start(bf16[512,1024]{1,0:T(8,128)(2,1)} %get-tuple-element.5) | copy-start | bytes 3145732

commit v4 on v0

v4 whole, which is shorter than its diff:
```python
import math

import jax
import jax.numpy as jnp
from jax import lax
from jax.experimental import pallas as pl
from jax.experimental.pallas import tpu as pltpu
from jax.sharding import PartitionSpec as P

DH = 128
NORM_EPS = 1e-05
MASK_FILL = -1e30
MESH = pl.DeviceIdType.MESH
F32 = jnp.float32
BF16 = jnp.bfloat16

NT = 32
NC = 8
NX = 4
NZ = 8
TOK = 512
AUD = 128
DE = 1024
COLS = 1024
HC = 512
HH = HC // DH
HALF = TOK // 2
SLOT = 8
TILES = ((0, 0, 0, 256), (0, 256, 0, 512), (1, 0, 0, 512), (1, 256, 256, 256))


def dot(a, b):
    return jnp.dot(a, b, preferred_element_type=F32)


def dot_t(a, b):
    return lax.dot_general(a, b, (((1,), (1,)), ((), ())), preferred_element_type=F32)


def iota(shape, dim):
    return lax.broadcasted_iota(jnp.int32, shape, dim)


class Wires:
    def __init__(self, ssem, rsem, lsem):
        self.ssem, self.rsem, self.lsem = ssem, rsem, lsem
        self.sent, self.groups, self.waited, self.locals_ = [], {}, set(), 0

    def send(self, name, src, dst, dev):
        i = len(self.sent)
        copy = pltpu.make_async_remote_copy(
            src_ref=src, dst_ref=dst, send_sem=self.ssem.at[i], recv_sem=self.rsem.at[i],
            device_id=dev, device_id_type=MESH,
        )
        copy.start()
        self.sent.append(copy)
        self.groups.setdefault(name, []).append(copy.wait_recv)

    def local(self, name, src, dst):
        copy = pltpu.make_async_copy(src, dst, self.lsem.at[self.locals_])
        self.locals_ += 1
        copy.start()
        self.groups.setdefault(name, []).append(copy.wait)

    def need(self, *names):
        for name in names:
            if name not in self.waited:
                self.waited.add(name)
                for wait in self.groups[name]:
                    wait()

    def finish(self):
        self.need(*self.groups)
        for copy in self.sent:
            copy.wait_send()


class Place:
    def __init__(self):
        t, c = lax.axis_index("tm"), lax.axis_index("ctx")
        self.t, self.c = t, c
        self.x, self.z = lax.rem(t, NX), lax.div(t, NX)
        self.core, self.yy = lax.rem(c, 2), lax.div(c, 2)
        self.up = (lax.rem(self.z + 1, NZ) * NX + self.x, c)
        self.dn = (lax.rem(self.z + NZ - 1, NZ) * NX + self.x, c)
        self.nxt = (lax.rem(t + 1, NT), c)
        self.prv = (lax.rem(t + NT - 1, NT), c)
        self.y_up, self.y_dn, self.far = [lax.rem(c + d, NC) for d in (2, 6, 4)]

    def ctx_peer(self, d):
        return (self.t, lax.rem(self.c + d, NC))

    def x_peer(self, d):
        return (self.z * NX + lax.rem(self.x + d, NX), self.c)

    def zat(self, d):
        return lax.rem(self.z + d + NZ, NZ)

    def beside(self, cc):
        return cc + 1 - 2 * self.core

    def mate(self):
        return (self.t, self.beside(self.c))


def al(v, m):
    return pl.multiple_of(v, m)


def signal_to(bar, dev):
    pl.semaphore_signal(bar, inc=1, device_id=dev, device_id_type=MESH)


def head_cols(h):
    return pl.ds(al(h * DH, DH), DH)


def gather_terms(tiles, other, h):
    hs = head_cols(h)
    first, second = pl.ds(0, 256), pl.ds(256, 256)
    top = dot(tiles[0], other[0, first, hs]) + dot(tiles[1][:256], other[0, second, hs])
    top = top + dot(tiles[2][:256], other[1, first, hs])
    bottom = dot(tiles[1][256:], other[0, second, hs])
    bottom = bottom + dot(tiles[2][256:], other[1, first, hs])
    bottom = bottom + dot(tiles[3], other[1, second, hs])
    return top, bottom


SCALE = 1.0 / math.sqrt(DH)


def kernel_a(
    frames, vw, gw, taps, ow, low, adapter, q, k, g,
    enc_o, AD, ks, qs, gs, lown,
    frames_s, vw_s, gw_s, taps_s, ow_s, low_s, ext, glu_s, mixs, mixr, enc_s, stage,
    ssem, rsem, lsem,
):
    me = Place()
    w = Wires(ssem, rsem, lsem)
    t, c = me.t, me.c
    own_rows = pl.ds(al(c * 64, 64), 64)
    own_cols = pl.ds(al(c * HC, HC), HC)
    ad_rows = pl.ds(al(t * 32, 32), 32)

    bar = pltpu.get_barrier_semaphore()
    for dev in (me.up, me.dn, me.nxt, me.prv):
        signal_to(bar, dev)
    for d in range(1, NX):
        signal_to(bar, me.x_peer(d))
    for d in range(1, NC):
        signal_to(bar, me.ctx_peer(d))
    w.local("frames", frames, frames_s)
    w.local("vw", vw, vw_s)
    w.local("gw", gw, gw_s)
    w.local("ad", adapter, AD.at[ad_rows])
    w.local("taps", taps, taps_s)
    w.local("ow", ow, ow_s)
    w.local("q0", q.at[:, own_cols], qs.at[0, own_rows])
    w.local("k0", k.at[:, own_cols], ks.at[own_rows])
    w.local("g0", g.at[:, own_cols], gs.at[own_rows])
    low_s[...] = jnp.broadcast_to(low[...], low_s.shape)
    pl.semaphore_wait(bar, 4 + NX - 1 + NC - 1)
    w.send("fh", frames.at[pl.ds(AUD - 16, 16)], ext.at[pl.ds(0, 16)], me.nxt)
    w.send("fh", frames.at[pl.ds(0, 16)], ext.at[pl.ds(AUD + 16, 16)], me.prv)
    for d in (1, 3, 2):
        w.send("adx", adapter, AD.at[ad_rows], me.x_peer(d))
    w.send("low", low_s, lown, me.prv)

    def d_step(s):
        def rows(zz, at, n):
            return AD.at[pl.ds(al(zz * 128 + at, 64), n)]

        if s < NZ // 2 - 1:
            u, v = rows(me.zat(-s), 0, 128), rows(me.zat(s), 0, 128)
        else:
            u, v = rows(me.zat(-s), 0, 64), rows(me.zat(s), 64, 64)
        w.send(f"d{s}", u, u, me.up)
        w.send(f"d{s}", v, v, me.dn)

    def regroup(name, src, dst, st):
        def piece(peer):
            return src.at[:, pl.ds(al(peer * HC, HC), HC)]

        w.send(name + "s", piece(me.far), st.at[0], (t, me.y_up))
        w.send(name + "s", piece(me.beside(me.far)), st.at[1], (t, me.y_dn))
        for peer in (me.y_up, me.y_dn, me.beside(me.y_up), me.beside(me.y_dn), me.beside(c)):
            w.send(name, piece(peer), dst.at[own_rows], (t, peer))

    def regroup_relay(name, dst, st):
        w.need(name + "s")
        w.send(name + "2", st.at[0], dst.at[pl.ds(al(me.y_dn * 64, 64), 64)], (t, me.y_up))
        w.send(name + "2", st.at[1], dst.at[pl.ds(al(me.y_up * 64, 64), 64)], (t, me.beside(me.y_dn)))

    regroup("q", q, qs.at[0], stage.at[0])
    regroup("k", k, ks, stage.at[1])

    w.need("frames", "vw", "gw")
    ext[pl.ds(16, AUD), :] = frames_s[...]
    w.need("fh")
    rows = ext[...].astype(F32)
    centre = jnp.mean(rows, axis=1, keepdims=True)
    off = rows - centre
    spread = jnp.mean(off * off, axis=1, keepdims=True)
    normed = (off * lax.rsqrt(spread + NORM_EPS)).astype(BF16)
    value_part = dot(normed, vw_s[...])
    gate_part = dot(normed, gw_s[...])
    glu = (value_part * jax.nn.sigmoid(gate_part)).astype(BF16).astype(F32)
    row = iota(glu.shape, 0)
    first = jnp.where(t == 0, 16, 0)
    last = jnp.where(t == NT - 1, AUD + 16, AUD + 32)
    glu_s[...] = jnp.where((row >= first) & (row < last), glu, 0.0)
    w.need("ad", "adx")
    d_step(0)

    w.need("taps", "ow")
    smooth = jnp.zeros((AUD, DH), F32)
    for j in range(taps_s.shape[0]):
        smooth = smooth + taps_s[pl.ds(j, 1), :] * glu_s[pl.ds(1 + j, AUD), :]
    action = (smooth * jax.nn.sigmoid(smooth)).astype(BF16)
    mixs[...] = dot(action, ow_s[...]).astype(BF16)
    for d in (4, 2, 6, 3, 5, 1, 7):
        rows_d = pl.ds(al(lax.rem(c + d, NC) * 16, 16), 16)
        w.send("mix", mixs.at[rows_d], mixr.at[d], me.ctx_peer(d))
    regroup_relay("q", qs.at[0], stage.at[0])
    regroup("g", g, gs, stage.at[2])
    regroup_relay("k", ks, stage.at[1])

    w.need("mix")
    mine = pl.ds(al(c * 16, 16), 16)
    total = frames_s[mine, :].astype(F32) + mixs[mine, :].astype(F32)
    for d in range(1, NC):
        total = total + mixr[d].astype(F32)
    enc_s[...] = total.astype(BF16)
    for d in (4, 2, 6, 3, 5, 1, 7):
        w.send("enc", enc_s, enc_o.at[mine], me.ctx_peer(d))
    w.local("enc0", enc_s, enc_o.at[mine])

    w.need("d0")
    d_step(1)
    w.need("q", "q2", "q0")
    w.send("hq", qs.at[0], qs.at[1], me.prv)
    regroup_relay("g", gs, stage.at[2])
    w.need("d1")
    d_step(2)
    w.need("d2")
    d_step(3)
    w.finish()


def positions(t, aud, slot_s, land_s):
    order = (iota((AUD, AUD), 0) < iota((AUD, AUD), 1)).astype(F32).astype(BF16)
    own = aud[pl.ds(t, 1), :]
    target = own // TOK
    hit = (iota((NT, AUD), 0) == target).astype(F32)
    rank = jnp.sum(dot(hit.astype(BF16), order) * hit, axis=0, keepdims=True)
    slot = target * SLOT + rank.astype(jnp.int32)
    slot_s[...] = jnp.broadcast_to(slot, slot_s.shape)
    table = aud[...]
    landing = table // TOK == t
    landing_rank = dot(landing.astype(F32).astype(BF16), order)
    spot = jnp.where(landing, table - t * TOK + 1, 0)
    n = NT * 16
    grow = (iota((n, NT), 0) // 16 == iota((n, NT), 1)).astype(F32).astype(BF16)
    spot_hi = dot(grow, (spot // 16).astype(F32).astype(BF16))
    spot_lo = dot(grow, (spot % 16).astype(F32).astype(BF16))
    ranks = dot(grow, jnp.where(landing, landing_rank, 64.0).astype(BF16))
    place = spot_hi * 16.0 + spot_lo
    r = (iota((n, AUD), 0) % 16).astype(F32)
    eye = iota((n, n), 0) == iota((n, n), 1)
    for half in range(2):
        col = jnp.sum(jnp.where(ranks == r - 8.0 * half, place, 0.0), axis=1, keepdims=True) - 1.0
        line = jnp.sum(jnp.where(eye, col, 0.0), axis=0, keepdims=True)
        land_s[half] = jnp.broadcast_to(line, (8, n)).astype(jnp.int32)


def kernel_b(
    enc_i, ad_i, ks_i, qs_i, gs_i, lown_i, low, aud, text, first_a, first_b,
    hid_o, pb_o, VG, gs_o,
    enc, AD, ks, qs, gs, low_s, lown, text_s, slot_s, land_s, adp, pick, inc, hid,
    e_ref, pb, vg, st_own, st_nxt, st_fp, st_fn,
    ssem, rsem, lsem, aus, aur,
):
    me = Place()
    w = Wires(ssem, rsem, lsem)
    t, c = me.t, me.c
    bar = pltpu.get_barrier_semaphore()

    def greet(d, carry):
        signal_to(bar, (lax.rem(t + d, NT), c))
        return carry

    lax.fori_loop(1, NT, greet, 0)
    for dev in ((t, me.y_up), (t, me.y_dn), me.mate()):
        signal_to(bar, dev)
    w.local("ad", ad_i, AD)
    w.local("enc", enc_i, enc)
    w.local("ks", ks_i, ks)
    w.local("qs", qs_i, qs)
    w.local("gs", gs_i, gs.at[0])
    w.local("lown", lown_i, lown)
    w.local("text", text, text_s)
    low_s[...] = jnp.broadcast_to(low[...], low_s.shape)
    pl.semaphore_wait(bar, NT - 1 + 3)
    w.send("hg", gs_i, gs.at[1], me.prv)

    positions(t, aud, slot_s, land_s)

    my_slot = pl.ds(al(t * 16, 16), 16)

    def audio_copy(d):
        peer = lax.rem(t + d, NT)
        return pltpu.make_async_remote_copy(
            src_ref=pick.at[pl.ds(al(peer * 16, 16), 16)], dst_ref=inc.at[my_slot],
            send_sem=aus.at[d], recv_sem=aur.at[d], device_id=(peer, c), device_id_type=MESH,
        )

    w.need("ad", "enc")
    for n in range(4):
        cols = pl.ds(256 * n, 256)
        adp[:, cols] = dot(enc[...], AD[:, cols]).astype(BF16)
    slot_row = iota((NT * 16, AUD), 0)
    picker = ((slot_row // 16) * SLOT + slot_row % SLOT == slot_s[pl.ds(0, 1), :]).astype(F32)
    picker = picker.astype(BF16)
    low_half = dot(picker, adp[:, pl.ds(0, 512)])
    high_half = dot(picker, adp[:, pl.ds(512, 512)])
    upper = iota((NT * 16, 512), 0) % 16 < SLOT
    pick[...] = jnp.where(upper, low_half, high_half).astype(BF16)

    def audio_start(d, carry):
        audio_copy(d).start()
        return carry

    lax.fori_loop(1, NT, audio_start, 0)
    inc[my_slot, :] = pick[my_slot, :]

    base = t * TOK
    row8 = iota((8, HALF), 0)

    def score_tiles(block, lows, limit, stats):
        def one_head(h, carry):
            hs = head_cols(h)
            for b, i0, j0, jn in TILES:
                if b != block:
                    continue
                qi = pl.ds(i0, HALF)
                s = dot_t(ks[pl.ds(j0, jn), hs], qs[b, qi, hs]) * SCALE
                jj = iota((jn, HALF), 0) + j0
                ok = jj >= lows[pl.ds(0, 1), qi] - base
                if block == 0:
                    ok = ok & (jj <= iota((jn, HALF), 1) + i0)
                else:
                    ok = ok & (jj < limit)
                s = jnp.where(ok, s, MASK_FILL)
                m = jnp.max(s, axis=0, keepdims=True)
                e = jnp.where(ok, jnp.exp(s - m), 0.0)
                n = jnp.sum(e, axis=0, keepdims=True)
                e_ref[b, h, pl.ds(j0, jn), qi] = e
                stats[h, :, qi] = jnp.where(row8 == 0, m, n)
            return carry

        lax.fori_loop(0, HH, one_head, 0)

    w.need("ks", "qs", "lown")
    score_tiles(1, lown, jnp.where(t == NT - 1, 0, TOK), st_nxt)
    w.send("stb", st_nxt, st_fp, me.nxt)
    score_tiles(0, low_s, TOK, st_own)
    w.send("sta", st_own, st_fn, me.prv)

    def factor(mine_st, other_st, h):
        m1, s1 = mine_st[h, pl.ds(0, 1), :], mine_st[h, pl.ds(1, 1), :]
        m2, s2 = other_st[h, pl.ds(0, 1), :], other_st[h, pl.ds(1, 1), :]
        m = jnp.maximum(m1, m2)
        a1 = jnp.exp(m1 - m)
        return a1 / (s1 * a1 + s2 * jnp.exp(m2 - m))

    w.need("sta", "stb", "gs", "hg")
    blank = jnp.zeros((256, 256), BF16)

    def prob_head(h, carry):
        f = (factor(st_own, st_fp, h), factor(st_nxt, st_fn, h))
        tiles = []
        for b, i0, j0, jn in TILES:
            at = (b, h, pl.ds(j0, jn), pl.ds(i0, HALF))
            p = (e_ref[at] * f[b][:, i0 : i0 + HALF]).astype(BF16)
            pb[at] = p
            tiles.append(p)
        pb[0, h, pl.ds(256, 256), pl.ds(0, 256)] = blank
        pb[1, h, pl.ds(0, 256), pl.ds(256, 256)] = blank
        top, bottom = gather_terms(tiles, gs, h)
        hs = head_cols(h)
        vg[pl.ds(0, 256), hs] = top.astype(BF16)
        vg[pl.ds(256, 256), hs] = bottom.astype(BF16)
        return carry

    lax.fori_loop(0, HH, prob_head, 0)
    w.send("vg1", vg, VG.at[c], (t, me.y_up))
    w.send("vg3", vg, VG.at[c], (t, me.y_dn))
    w.send("vgc", vg, VG.at[c], me.mate())
    w.local("vg0", vg, VG.at[c])
    w.local("pb", pb, pb_o)
    w.local("gso", gs, gs_o)

    def audio_arrived(d, carry):
        audio_copy(d).wait_recv()
        return carry

    lax.fori_loop(1, NT, audio_arrived, 0)
    w.need("text")
    for half in range(2):
        cols = pl.ds(512 * half, 512)
        hits = (iota((TOK, NT * 16), 0) == land_s[half, pl.ds(0, 1), :]).astype(F32)
        there = jnp.sum(hits, axis=1, keepdims=True) > 0.5
        rows_in = dot(hits.astype(BF16), inc[...])
        hid[:, cols] = jnp.where(there, rows_in, text_s[:, cols].astype(F32)).astype(BF16)
    w.local("hid", hid, hid_o)

    w.need("vg1", "vg3")
    one, two = VG.at[me.y_dn, pl.ds(0, 256)], VG.at[me.y_up, pl.ds(256, 256)]
    w.send("vg2", one, one, (t, me.y_up))
    w.send("vg2", two, two, (t, me.y_dn))
    w.send("vgc", VG.at[me.y_dn], VG.at[me.y_dn], me.mate())
    w.send("vgc", VG.at[me.y_up], VG.at[me.y_up], me.mate())
    w.need("vg2")
    w.send("vgc", VG.at[me.far], VG.at[me.far], me.mate())

    def audio_sent(d, carry):
        audio_copy(d).wait_send()
        return carry

    lax.fori_loop(1, NT, audio_sent, 0)
    w.finish()


CHUNKS = ((2, 0), (2, 1), (1, 0), (1, 1), (3, 0), (3, 1), (0, 0), (0, 1))
ORDER = (
    "t0", "t1", "rs0", "t2", "rs1", "t3", "rs2", "t4", "rs3", "ad2", "t5", "rs4", "t6", "rs5",
    "ad5", "t7", "rs6", "rs7", "dh0", "dh1", "dh2", "dh3", "dh4", "dh5", "dh6", "dh7", "delta", "key",
)


def kernel_c(
    hid_i, wa, wb, vg_i, pb_i, gs_i, qs_i,
    dk_out, dh_out,
    hid, W, VG, pb, gs, qs, gv_ref, dl_own, dl_nxt, dl_fp, dl_fn,
    psend, pown, precv, rsend, radd, rrecv, vbuf, acc,
    ssem, rsem, lsem, rss, rsr,
):
    me = Place()
    w = Wires(ssem, rsem, lsem)
    t, c, core, yy = me.t, me.c, me.core, me.yy
    mate = me.mate()
    bar = pltpu.get_barrier_semaphore()
    near = (me.y_up, me.y_dn, me.beside(me.y_up), me.beside(me.y_dn), me.beside(c))
    for dev in [(t, cc) for cc in near] + [me.nxt, me.prv]:
        signal_to(bar, dev)
    w.local("hid", hid_i, hid)

    def chunk_of(i):
        e, kd = CHUNKS[i]
        return lax.rem(yy + e, NC // 2) * 2 + kd

    for i in range(NC):
        cp = chunk_of(i)
        w.local(f"w{i}", wa.at[pl.ds(cp * HH, HH)], W.at[i, :, pl.ds(0, 512)])
        for j in range(HH):
            w.local(f"w{i}", wb.at[j, cp], W.at[i, j, pl.ds(512, 512)])
    w.local("vg", vg_i, VG)
    w.local("gs", gs_i, gs)
    w.local("pb", pb_i, pb)
    w.local("qs", qs_i, qs)
    pl.semaphore_wait(bar, len(near) + 2)

    mate_rows = pl.ds(al((1 - core) * HALF, HALF), HALF)
    my_rows = pl.ds(al(core * HALF, HALF), HALF)

    def terms(i):
        w.need("hid", f"w{i}")
        wide = jnp.concatenate([W[i, j] for j in range(HH)], axis=1)
        psend[i] = dot(hid[mate_rows, :], wide).astype(BF16)
        w.send(f"pair{i}", psend.at[i], precv.at[i], mate)
        wide = jnp.concatenate([W[i, j] for j in range(HH)], axis=1)
        pown[i] = dot(hid[my_rows, :], wide).astype(BF16)

    def owner_copy(i):
        e, kd = CHUNKS[i]
        side = e // 2
        return pltpu.make_async_remote_copy(
            src_ref=rsend.at[i], dst_ref=rrecv.at[1 + side, my_rows],
            send_sem=rss.at[2 * side + kd], recv_sem=rsr.at[2 * side + core],
            device_id=(t, chunk_of(i)), device_id_type=MESH,
        )

    def mate_copy(i):
        return pltpu.make_async_remote_copy(
            src_ref=rsend.at[i], dst_ref=rrecv.at[0, my_rows],
            send_sem=rss.at[4], recv_sem=rsr.at[4], device_id=mate, device_id_type=MESH,
        )

    def chip_sum(i):
        e, kd = CHUNKS[i]
        w.need(f"pair{i}")
        total = pown[i].astype(F32) + precv[i].astype(F32)
        rsend[i] = total.astype(BF16)
        if e == 2:
            w.send(f"add{kd}", rsend.at[i], radd.at[kd], (t, me.y_dn if kd else me.y_up))
        elif (e, kd) in ((1, 1), (3, 0)):
            owner_copy(i).start()
        elif e == 0:
            @pl.when(kd != core)
            def _():
                mate_copy(i).start()

            @pl.when(kd == core)
            def _():
                rrecv[0, my_rows, :] = rsend[i]

    def added_sum(i):
        kd = CHUNKS[i][1]
        w.need(f"add{kd}")
        total = rsend[i].astype(F32) + radd[kd].astype(F32)
        rsend[i] = total.astype(BF16)
        owner_copy(i).start()

    added = []

    def hidden_grad(i):
        w.need("vg", f"w{i}")
        cp = chunk_of(i)
        added.append(i)
        first, last = len(added) == 1, len(added) == NC

        def part(n, carry):
            rows_n = pl.ds(al(n * 256, 256), 256)
            wide = jnp.concatenate([W[i, j, rows_n, :] for j in range(HH)], axis=1)
            term = dot_t(VG[cp], wide)
            if not first:
                term = term + acc[n]
            if last:
                dh_out[:, rows_n] = term.astype(BF16)
            else:
                acc[n] = term
            return carry

        lax.fori_loop(0, COLS // 256, part, 0)

    row8 = iota((8, HALF), 0)

    def delta():
        for n in range(5):
            pltpu.make_async_remote_copy(
                src_ref=rsend.at[0], dst_ref=rrecv.at[0, my_rows], send_sem=rss.at[n],
                recv_sem=rsr.at[n], device_id=mate, device_id_type=MESH,
            ).wait_recv()
        total = rrecv[0].astype(F32) + rrecv[1].astype(F32) + rrecv[2].astype(F32)
        vbuf[...] = total.astype(BF16)
        w.need("gs", "pb")

        def delta_head(h, carry):
            hs = head_cols(h)
            for b, i0, j0, jn in TILES:
                qi = pl.ds(i0, HALF)
                gv = dot_t(vbuf[pl.ds(j0, jn), hs], gs[b, qi, hs])
                gv_ref[b, h, pl.ds(j0, jn), qi] = gv
                p = pb[b, h, pl.ds(j0, jn), qi].astype(F32)
                part = jnp.sum(p * gv, axis=0, keepdims=True)
                table = dl_own if b == 0 else dl_nxt
                table[h, :, qi] = jnp.where(row8 == 0, part, 0.0)
            return carry

        lax.fori_loop(0, HH, delta_head, 0)
        w.send("dl", dl_own, dl_fn, me.prv)
        w.send("dl", dl_nxt, dl_fp, me.nxt)

    def key():
        w.need("dl", "qs")

        def key_head(h, carry):
            deltas = (
                dl_own[h, pl.ds(0, 1), :] + dl_fp[h, pl.ds(0, 1), :],
                dl_nxt[h, pl.ds(0, 1), :] + dl_fn[h, pl.ds(0, 1), :],
            )
            tiles = []
            for b, i0, j0, jn in TILES:
                qi = pl.ds(i0, HALF)
                p = pb[b, h, pl.ds(j0, jn), qi].astype(F32)
                gv = gv_ref[b, h, pl.ds(j0, jn), qi]
                tiles.append((p * (gv - deltas[b][:, i0 : i0 + HALF])).astype(BF16))
            top, bottom = gather_terms(tiles, qs, h)
            hs = head_cols(h)
            dk_out[pl.ds(0, 256), hs] = (top * SCALE).astype(BF16)
            dk_out[pl.ds(256, 256), hs] = (bottom * SCALE).astype(BF16)
            return carry

        lax.fori_loop(0, HH, key_head, 0)

    steps = {"delta": delta, "key": key}
    for i in range(NC):
        steps[f"t{i}"] = lambda i=i: terms(i)
        steps[f"rs{i}"] = lambda i=i: chip_sum(i)
        steps[f"ad{i}"] = lambda i=i: added_sum(i)
        steps[f"dh{i}"] = lambda i=i: hidden_grad(i)
    for name in ORDER:
        steps[name]()
    for n in range(5):
        pltpu.make_async_remote_copy(
            src_ref=rsend.at[0], dst_ref=rrecv.at[0, my_rows], send_sem=rss.at[n],
            recv_sem=rsr.at[n], device_id=mate, device_id_type=MESH,
        ).wait_send()
    w.finish()


def call(kernel, n, out_shape, in_specs, out_specs, scratch, flops, moved):
    return pl.pallas_call(
        kernel,
        out_shape=out_shape,
        in_specs=in_specs,
        out_specs=out_specs,
        scratch_shapes=scratch,
        compiler_params=pltpu.CompilerParams(
            collective_id=n, has_side_effects=True, vmem_limit_bytes=60 * 1024 * 1024
        ),
        cost_estimate=pl.CostEstimate(flops=flops, bytes_accessed=moved, transcendentals=0),
    )


def body(
    frames, value_weight, gate_weight, conv_taps, out_weight, adapter, audio_pos, text_rows,
    value_proj, queries, keys, grad_out, window_low,
):
    along_x = [[NX * zz + xx for xx in range(NX)] for zz in range(NZ)]
    along_z = [[NX * zz + xx for zz in range(NZ)] for xx in range(NX)]
    first_a = lax.all_gather(value_proj[:512], "tm", axis_index_groups=along_x)
    first_b = lax.all_gather(value_proj[512:], "tm", axis_index_groups=along_z)
    low = window_low.reshape(1, TOK)
    vm = pl.BlockSpec(memory_space=pltpu.VMEM)
    hbm = pl.BlockSpec(memory_space=pl.ANY)
    vmem = pltpu.VMEM
    dma = pltpu.SemaphoreType.DMA
    shape = jax.ShapeDtypeStruct
    enc, ad, ks, qs, gs, lown = call(
        kernel_a, 0,
        (
            shape((AUD, DE), BF16), shape((DE, COLS), BF16), shape((TOK, HC), BF16),
            shape((2, TOK, HC), BF16), shape((TOK, HC), BF16), shape((8, TOK), jnp.int32),
        ),
        [hbm] * 5 + [vm] + [hbm] * 4, (hbm,) * 6,
        [
            vmem((AUD, DE), BF16),
            vmem((DE, DH), BF16),
            vmem((DE, DH), BF16),
            vmem(conv_taps.shape, F32),
            vmem((DH, DE), BF16),
            vmem((8, TOK), jnp.int32),
            vmem((AUD + 32, DE), BF16),
            vmem((AUD + 32, DH), F32),
            vmem((AUD, DE), BF16),
            vmem((NC, 16, DE), BF16),
            vmem((16, DE), BF16),
            vmem((3, 2, 64, HC), BF16),
            dma((64,)), dma((64,)), dma((16,)),
        ],
        200_000_000, 20_000_000,
    )(
        frames, value_weight, gate_weight, conv_taps, out_weight, low, adapter,
        queries, keys, grad_out,
    )
    enc, first_a, first_b = lax.optimization_barrier((enc, first_a, first_b))
    weights_a = lax.all_gather(first_a, "tm", axis_index_groups=along_z).reshape(NT, 512, DH)
    weights_b = lax.all_gather(first_b, "tm", axis_index_groups=along_x)
    hid, pb, vg, gs2 = call(
        kernel_b, 1,
        (
            shape((TOK, COLS), BF16), shape((2, HH, TOK, TOK), BF16),
            shape((NC, TOK, HC), BF16), shape((2, TOK, HC), BF16),
        ),
        [hbm] * 6 + [vm] * 2 + [hbm] * 3, (hbm,) * 4,
        [
            vmem((AUD, DE), BF16),
            vmem((DE, COLS), BF16),
            vmem((TOK, HC), BF16),
            vmem((2, TOK, HC), BF16),
            vmem((2, TOK, HC), BF16),
            vmem((8, TOK), jnp.int32),
            vmem((8, TOK), jnp.int32),
            vmem((TOK, COLS), BF16),
            vmem((8, AUD), jnp.int32),
            vmem((2, 8, NT * 16), jnp.int32),
            vmem((AUD, COLS), BF16),
            vmem((NT * 16, 512), BF16),
            vmem((NT * 16, 512), BF16),
            vmem((TOK, COLS), BF16),
            vmem((2, HH, TOK, TOK), F32),
            vmem((2, HH, TOK, TOK), BF16),
            vmem((TOK, HC), BF16),
        ]
        + [vmem((HH, 8, TOK), F32)] * 4
        + [dma((16,)), dma((16,)), dma((16,)), dma((NT,)), dma((NT,))],
        3_000_000_000, 60_000_000,
    )(
        enc, ad, ks, qs, gs, lown, low, audio_pos.reshape(NT, AUD), text_rows, first_a, first_b,
    )
    return call(
        kernel_c, 2,
        (shape((TOK, HC), BF16), shape((TOK, COLS), BF16)),
        [hbm] * 7, (vm, vm),
        [
            vmem((TOK, COLS), BF16),
            vmem((NC, HH, COLS, DH), BF16),
            vmem((NC, TOK, HC), BF16),
            vmem((2, HH, TOK, TOK), BF16),
            vmem((2, TOK, HC), BF16),
            vmem((2, TOK, HC), BF16),
            vmem((2, HH, TOK, TOK), F32),
        ]
        + [vmem((HH, 8, TOK), F32)] * 4
        + [
            vmem((NC, HALF, HC), BF16),
            vmem((NC, HALF, HC), BF16),
            vmem((NC, HALF, HC), BF16),
            vmem((NC, HALF, HC), BF16),
            vmem((2, HALF, HC), BF16),
            vmem((3, TOK, HC), BF16),
            vmem((TOK, HC), BF16),
            vmem((COLS // 256, TOK, 256), F32),
            dma((16,)), dma((16,)), dma((64,)), dma((8,)), dma((8,)),
        ],
        10_000_000_000, 30_000_000,
    )(hid, weights_a, weights_b, vg, pb, gs2, qs)


def solution(mesh):
    return jax.shard_map(
        body,
        mesh=mesh,
        in_specs=(
            P("tm", None),
            P(None, "ctx"),
            P(None, "ctx"),
            P(None, "ctx"),
            P("ctx", None),
            P("tm", "ctx"),
            P(),
            P("tm", "ctx"),
            P("ctx", "tm"),
            P(("tm", "ctx"), None),
            P(("tm", "ctx"), None),
            P(("tm", "ctx"), None),
            P("tm"),
        ),
        out_specs=(P("tm", "ctx"), P("tm", "ctx")),
        check_vma=False,
    )
```

time: 384 us -> 248 us (0.65); the launches traced: 376 us -> 245 us
  waiting for transfers between devices: 252 us -> 57.6 us
  Pallas kernels: 0 us -> 156 us
  matrix products: 38.4 us -> 0 us
  starting transfers between devices: 37.8 us -> 0.12 us
  other arithmetic: 17.7 us -> 0 us
  blocking collectives: 0 us -> 12 us
  local copies, waits for them, and re-layouts: 14.5 us -> 5.77 us
    pallas_call x0 -> x3, Pallas kernels: none -> 156 us  [the longest x1 60.6 us: body(): call(kernel_a, 0, (shape((AUD, DE), BF16), shape((DE, COLS), BF16), shape...]
    psum x1 -> x0, waiting for transfers between devices: 67.4 us -> none  [encode_frames(): mixed_sum = lax.psum(partial_mix, 'ctx')]
    all_gather x3, waiting for transfers between devices: 104 us -> 56.9 us  [the longest x1 54.4 us: body(): lax.all_gather(first_a, 'tm', axis_index_groups=along_z)]
    ppermute x6 -> x0, waiting for transfers between devices: 44.4 us -> none  [the longest x4 43.3 us: passed_along(): return lax.ppermute(value, axis, pairs)]
    dot_general x10 -> x0, matrix products: 38.4 us -> none  [the longest x1 10.2 us: body(): lax.dot_general(lax.all_gather(value_grad, 'ctx', axis=1, tiled=True), fu...]
    all_to_all x4 -> x0, waiting for transfers between devices: 35.8 us -> none  [the longest x1 11.5 us: body(): lax.all_to_all(outgoing, 'tm', split_axis=0, concat_axis=0, tiled=True)]
    all_to_all x4 -> x0, starting transfers between devices: 25.7 us -> none  [the longest x1 8.36 us: body(): lax.all_to_all(keys, 'ctx', split_axis=1, concat_axis=0, tiled=True)]
    all_gather x0 -> x1, blocking collectives: none -> 12 us  [body(): first_a = lax.all_gather(value_proj[:512], 'tm', axis_index_groups=along_x)]
  transfers between devices with their start and end apart: 15 -> 3, of which waited for: 12 -> 2; matrix products, arithmetic and copies ran while one was open for 13% -> 0% of each run, Pallas kernels for 0% -> 48%
where the time goes in v4:
time: 248 us; the launch traced here: 245 us
  Pallas kernels  156 us (63%)
  waiting for transfers between devices  57.6 us (23%)
  between operations  13.8 us (6%)
  blocking collectives  12 us (5%)
  local copies, waits for them, and re-layouts  5.77 us (2%)
    pallas_call x1, Pallas kernels, body(): call(kernel_a, 0, (shape((AUD, DE), BF16), shape((DE, COLS), BF16), shape...  60.6 us
    pallas_call x1, Pallas kernels, body(): call(kernel_b, 1, (shape((TOK, COLS), BF16), shape((2, HH, TOK, TOK), BF1...  56.9 us
    all_gather x1, waiting for transfers between devices, body(): lax.all_gather(first_a, 'tm', axis_index_groups=along_z)  54.4 us
    pallas_call x1, Pallas kernels, body(): call(kernel_c, 2, (shape((TOK, HC), BF16), shape((TOK, COLS), BF16)), [hb...  38.3 us
    all_gather x1, blocking collectives, body(): first_a = lax.all_gather(value_proj[:512], 'tm', axis_index_groups=along_x)  12 us
  transfers between devices with their start and end apart: 3, of which 2 were waited for; matrix products, arithmetic and copies ran while one was open for 0% of the time, Pallas kernels for 48%

profile of v4, /device:TPU:9, one launch (start us, length us, event | category | flops | bytes accessed | tf_op | source)
XLA Modules:
  0.0 245.1 jit_solution(17412167216547061828)
XLA Ops:
  7.2 0.0 all-gather.8.cloned.1.call-start
  7.2 1.6 fusion
  8.9 0.0 all-gather.8.cloned.1.call-update
  8.9 0.0 all-gather.12.cloned.1.call-start
  8.9 60.6 %shard_map.140 = (bf16[128,1024]{1,0:T(8,128)(2,1)}, bf16[1024,1024]{1,0:T(8,128)(2,1)}, bf16[512,512]{1,0:T(8,128)(2,1)}, bf16[2,512,512]{2,1,0:T(8,128)(2,1)},...) custom-call(bf16[128,1024]{1,0:T(8,128)(2,1)} %frames.1, bf16[1024,128]{1,0:T(8,128)(2,1)} %vw.1, bf16[1024,128]{1,0:T(8,128)(2,1)} %gw.1, ...), custom_call_target="tpu_custom_call" | custom-call | flops 200000000 | bytes 20000000 | tf_op jit(solution)/shard_map/pallas_call | solution.py:640
  69.6 12.0 %all-gather = bf16[2048,128]{1,0:T(8,128)(2,1)} all-gather(bf16[512,128]{1,0:T(8,128)(2,1)S(1)} %get-tuple-element.29), channel_id=2, replica_groups={{0,8,16,24},{32,40,48,56},{64,72,80,88},{96,104,112,120},{128,136,144,1..., dimensions={0}, use_global_device_ids=true | all-gather | bytes 655360 | tf_op jit(solution)/shard_map/all_gather | solution.py:632
  81.6 0.0 all-gather.8.cloned.1.call-done
  81.6 0.0 all-gather.12.cloned.1.call-update
  81.6 0.0 all-gather.10.cloned.1.call-start
  81.7 0.7 all-gather.10.cloned.1.call-update
  82.3 56.9 %shard_map.141 = (bf16[512,1024]{1,0:T(8,128)(2,1)}, bf16[2,4,512,512]{3,2,1,0:T(8,128)(2,1)}, bf16[8,512,512]{2,1,0:T(8,128)(2,1)}, bf16[2,512,512]{2,1,0:T(8,128)(2,1)}) custom-call(bf16[128,1024]{1,0:T(8,128)(2,1)} %get-tuple-element.16.enc_i, bf16[1024,1024]{1,0:T(8,128)(2,1)} %get-tuple-element.17.ad_i, bf16[512,512]{1,0:T(8,128)(2,1)} %get-tuple-element.18.ks_i, ...), custom_call_target="tpu_custom_call" | custom-call | flops 3000000000 | bytes 60000000 | tf_op jit(solution)/shard_map/pallas_call | solution.py:670
  139.2 2.6 %all-gather.12.cloned.1.call-done = bf16[32,512,128]{2,1,0:T(8,128)(2,1)} async-done(((bf16[8,512,128]{2,1,0:T(8,128)(2,1)}), bf16[32,512,128]{2,1,0:T(8,128)(2,1)}) %all-gather.12.cloned.1.call-update) | async-done | bytes 4194320 | tf_op jit(solution)/shard_map/all_gather | solution.py:669
  141.8 54.4 %all-gather.10.cloned.1.call-done.wa = bf16[32,512,128]{2,1,0:T(8,128)(2,1)} async-done(((bf16[4,512,128]{2,1,0:T(8,128)(2,1)}), bf16[32,512,128]{2,1,0:T(8,128)(2,1)}) %all-gather.10.cloned.1.call-update) | async-done | bytes 4194320 | tf_op jit(solution)/shard_map/all_gather | solution.py:668
  196.1 38.3 %shard_map.142 = (bf16[512,512]{1,0:T(8,128)(2,1)}, bf16[512,1024]{1,0:T(8,128)(2,1)}) custom-call(bf16[512,1024]{1,0:T(8,128)(2,1)} %get-tuple-element.24.hid_i, bf16[32,512,128]{2,1,0:T(8,128)(2,1)} %all-gather.10.cloned.1.call-done.wa, bf16[4,8,512,128]{3,2,1,0:T(8,128)(2,1)} %bitcast.11, bf16[8,512,512]{2,1,0:T(8,128)(2,1)} %get-tuple-element.25.vg_i, ...), custom_call_target="tpu_custom_call" | custom-call | flops 10000000000 | bytes 30000000 | tf_op jit(solution)/shard_map/pallas_call | solution.py:702
  234.5 1.9 copy.17
  236.3 2.3 copy.18
Async XLA Ops:
  7.2 74.4 %all-gather.8.cloned.1.call-start = ((), (), s32[]{:S(2)}) async-start(), calls=%async_computation | async-start | bytes 1179648 | tf_op jit(solution)/shard_map/all_gather | solution.py:633
  8.9 132.9 %all-gather.12.cloned.1.call-start = ((), (), s32[]{:S(2)}) async-start(), calls=%async_computation.2 | async-start | bytes 5242880 | tf_op jit(solution)/shard_map/all_gather | solution.py:669
  81.6 114.5 %all-gather.10.cloned.1.call-start = ((), (), s32[]{:S(2)}) async-start(), calls=%async_computation.1 | async-start | bytes 4718592 | tf_op jit(solution)/shard_map/all_gather | solution.py:668
Sparse Core Ops, SparseCore 0:
  10.4 40.6 all-gather.7
  81.7 59.9 all-gather.11
  143.6 52.5 all-gather.9

commit v5 on v3

--- a/solution.py
+++ b/solution.py
@@ -28,17 +28,18 @@
 SLOT = 8
 TILES = ((0, 0, 0, 256), (0, 256, 0, 512), (1, 0, 0, 512), (1, 256, 256, 256))
 N_SEMS = 160
-ROWS_A = 352
+QUART = COLS // NX
+ROWS_A = 576
 ROWS_B = COLS - ROWS_A
 OFFSETS = (0, -1, 1, -2, 2, -3, 3, 4)
 ORDER = (
-    "issue", "i_b0", "i_k", "i_q", "i_ax", "mm", "b_s1", "p0", "m0", "LN", "fk", "fq", "conv",
-    "i_g", "d_s0", "b_s2", "i_bm", "rm", "hq", "sc0", "b_s3", "pos", "enc", "fg", "d_s1", "r0",
-    "p3", "hg", "d_s2", "d_s3", "a_s0", "p1", "sc1", "adapt", "m1", "p2", "m2", "m3", "prob",
-    "r1", "a_s1", "r3", "vgr", "place", "t0", "t1", "r2", "vgf", "t2", "rs0", "a_s2", "t3",
-    "rs1", "t4", "rs2", "ad0", "dh0", "rs3", "dh1", "ad1", "rs4", "dh2", "dh3", "dh4", "ad2",
-    "a_s3", "t5", "ad3", "t6", "ad4", "dh5", "rs5", "dh6", "rs6", "t7", "dh7", "ad5", "ad6",
-    "rs7", "ad7", "delta", "key",
+    "issue", "i_b0", "i_q", "mm", "i_ax", "LN", "b_s1", "m0", "fq", "conv", "i_g", "d_s0", "p0",
+    "b_s2", "rm", "hq", "d_s1", "a_s0", "p1", "enc", "b_s3", "fg", "r0", "encx", "hg", "i_k",
+    "pos", "d_s2", "a_s1", "fk", "p3", "r1", "er", "sc1", "sc0", "m2", "d_s3", "p2", "i_bm",
+    "m1", "a_s2", "m3", "adapt", "r2", "prob", "r3", "vgr", "place", "t3", "t0", "t2", "a_s3",
+    "rs3", "t4", "rs0", "t5", "ad3", "rs2", "rs4", "t6", "ad0", "t1", "rs5", "ad2", "t7", "ad4",
+    "rs6", "vgf", "rs7", "ad6", "dh0", "dh2", "dh3", "dh7", "ad5", "rs1", "dh1", "ad7", "dh5",
+    "dh6", "ad1", "delta", "dh4", "key",
 )
 
 
@@ -139,7 +140,7 @@
         local("vw", vw, vw_s)
         local("gw", gw, gw_s)
         local("vp", vp, W.at[t])
-        local("ad", adapter, AD.at[ad_rows])
+        local("ad", adapter.at[:, pl.ds(al(x * QUART, QUART), QUART)], AD.at[ad_rows])
         local("taps", taps, taps_s)
         local("ow", ow, ow_s)
         local("k0", k.at[:, own_cols], ks.at[own_rows])
@@ -151,7 +152,8 @@
         send("fh", frames.at[pl.ds(AUD - 16, 16)], ext.at[pl.ds(0, 16)], nxt)
         send("fh", frames.at[pl.ds(0, 16)], ext.at[pl.ds(AUD + 16, 16)], prv)
         for d in (1, 3, 2):
-            send("adx", adapter, AD.at[ad_rows], x_peer(d))
+            quarter = pl.ds(al(lax.rem(x + d, NX) * QUART, QUART), QUART)
+            send("adx", adapter.at[:, quarter], AD.at[ad_rows], x_peer(d))
         send("low", low_s, lown, prv)
 
     def b_ref(zz, xx=x):
@@ -233,28 +235,27 @@
 
     def positions():
         order = (iota((AUD, AUD), 0) < iota((AUD, AUD), 1)).astype(F32).astype(BF16)
-        own = aud[pl.ds(t, 1), :]
-        target = own // TOK
-        hit = (iota((NT, AUD), 0) == target).astype(F32)
-        rank = jnp.sum(dot(hit.astype(BF16), order) * hit, axis=0, keepdims=True)
-        slot = target * SLOT + rank.astype(jnp.int32)
-        slot_s[...] = jnp.broadcast_to(slot, slot_s.shape)
+        for b in range(NX):
+            target = aud[pl.ds(z * NX + b, 1), :] // TOK
+            hit = (iota((NT, AUD), 0) == target).astype(F32)
+            rank = jnp.sum(dot(hit.astype(BF16), order) * hit, axis=0, keepdims=True)
+            slot = target * (NX * SLOT) + b * SLOT + rank.astype(jnp.int32)
+            slot_s[:, pl.ds(b * AUD, AUD)] = jnp.broadcast_to(slot, (8, AUD))
         table = aud[...]
         landing = table // TOK == t
         landing_rank = dot(landing.astype(F32).astype(BF16), order)
         spot = jnp.where(landing, table - t * TOK + 1, 0)
-        n = NT * 16
-        grow = (iota((n, NT), 0) // 16 == iota((n, NT), 1)).astype(F32).astype(BF16)
+        n = NT * SLOT
+        grow = (iota((n, NT), 0) // SLOT == iota((n, NT), 1)).astype(F32).astype(BF16)
         spot_hi = dot(grow, (spot // 16).astype(F32).astype(BF16))
         spot_lo = dot(grow, (spot % 16).astype(F32).astype(BF16))
         ranks = dot(grow, jnp.where(landing, landing_rank, 64.0).astype(BF16))
-        place = spot_hi * 16.0 + spot_lo
-        r = (iota((n, AUD), 0) % 16).astype(F32)
+        spots = spot_hi * 16.0 + spot_lo
+        r = (iota((n, AUD), 0) % SLOT).astype(F32)
+        col = jnp.sum(jnp.where(ranks == r, spots, 0.0), axis=1, keepdims=True) - 1.0
         eye = iota((n, n), 0) == iota((n, n), 1)
-        for half in range(2):
-            col = jnp.sum(jnp.where(ranks == r - 8.0 * half, place, 0.0), axis=1, keepdims=True) - 1.0
-            line = jnp.sum(jnp.where(eye, col, 0.0), axis=0, keepdims=True)
-            land_s[half] = jnp.broadcast_to(line, (8, n)).astype(jnp.int32)
+        line = jnp.sum(jnp.where(eye, col, 0.0), axis=0, keepdims=True)
+        land_s[...] = jnp.broadcast_to(line, (8, n)).astype(jnp.int32)
 
     def norm_glu():
         need("frames", "vw", "gw")
@@ -290,9 +291,20 @@
         total = frames_s[mine, :].astype(F32) + mixs[mine, :].astype(F32)
         for d in range(1, NC):
             total = total + mixr[d].astype(F32)
-        enc[mine, :] = total.astype(BF16)
+        enc[x, mine, :] = total.astype(BF16)
         for d in (4, 2, 6, 3, 5, 1, 7):
-            send("enc", enc.at[mine], enc.at[mine], ctx_peer(d))
+            send("enc", enc.at[x, mine], enc.at[x, mine], ctx_peer(d))
+
+    def encode_x():
+        need("enc")
+        for d in (1, 3):
+            send("ex", enc.at[x], enc.at[x], x_peer(d))
+
+    def encode_relay():
+        need("ex")
+        for d, at in ((1, 0), (3, AUD // 2)):
+            part = enc.at[lax.rem(x + NX - d, NX), pl.ds(at, AUD // 2)]
+            send("ex2", part, part, x_peer(d))
 
     def halo(name):
         part = qs if name == "q" else gs
@@ -340,34 +352,33 @@
         score_tiles(1, lown, jnp.where(t == NT - 1, 0, TOK), st_nxt)
         send("stb", st_nxt, st_fp, nxt)
 
-    my_slot = pl.ds(al(t * 16, 16), 16)
+    group_rows = NX * SLOT
+    my_slot = pl.ds(al(z * group_rows, group_rows), group_rows)
+
+    def slot_rows(tm):
+        return pl.ds(al(tm * group_rows, group_rows), group_rows)
 
     def audio_copy(d):
         peer = lax.rem(t + d, NT)
         return pltpu.make_async_remote_copy(
-            src_ref=pick.at[pl.ds(al(peer * 16, 16), 16)], dst_ref=inc.at[my_slot],
+            src_ref=pick.at[slot_rows(peer)], dst_ref=inc.at[x, my_slot],
             send_sem=aus.at[d], recv_sem=aur.at[d], device_id=(peer, c), device_id_type=MESH,
         )
 
     def adapt():
-        need("d3", "enc")
+        need("d3", "ex", "ex2")
+        adp[...] = dot(enc[...].reshape(NX * AUD, DE), AD[...]).astype(BF16)
         for n in range(4):
-            cols = pl.ds(256 * n, 256)
-            adp[:, cols] = dot(enc[...], AD[:, cols]).astype(BF16)
-        slot_row = iota((NT * 16, AUD), 0)
-        picker = ((slot_row // 16) * SLOT + slot_row % SLOT == slot_s[pl.ds(0, 1), :]).astype(F32)
-        picker = picker.astype(BF16)
-        low_half = dot(picker, adp[:, pl.ds(0, 512)])
-        high_half = dot(picker, adp[:, pl.ds(512, 512)])
-        upper = iota((NT * 16, 512), 0) % 16 < SLOT
-        pick[...] = jnp.where(upper, low_half, high_half).astype(BF16)
+            slot_row = iota((256, NX * AUD), 0) + 256 * n
+            picker = (slot_row == slot_s[pl.ds(0, 1), :]).astype(F32).astype(BF16)
+            pick[pl.ds(256 * n, 256), :] = dot(picker, adp[...]).astype(BF16)
 
         def audio_start(d, carry):
             audio_copy(d).start()
             return carry
 
         lax.fori_loop(1, NT, audio_start, 0)
-        inc[my_slot, :] = pick[my_slot, :]
+        inc[x, my_slot, :] = pick[slot_rows(t), :]
 
     def factor(mine_st, other_st, h):
         m1, s1 = mine_st[h, pl.ds(0, 1), :], mine_st[h, pl.ds(1, 1), :]
@@ -429,11 +440,12 @@
             return carry
 
         lax.fori_loop(1, NT, audio_arrived, 0)
-        for half in range(2):
-            cols = pl.ds(512 * half, 512)
-            hits = (iota((TOK, NT * 16), 0) == land_s[half, pl.ds(0, 1), :]).astype(F32)
-            there = jnp.sum(hits, axis=1, keepdims=True) > 0.5
-            rows_in = dot(hits.astype(BF16), inc[...])
+        hits = (iota((TOK, NT * SLOT), 0) == land_s[pl.ds(0, 1), :]).astype(F32)
+        there = jnp.sum(hits, axis=1, keepdims=True) > 0.5
+        hits = hits.astype(BF16)
+        for n in range(NX):
+            cols = pl.ds(QUART * n, QUART)
+            rows_in = dot(hits, inc[n])
             hid[:, cols] = jnp.where(there, rows_in, text_s[:, cols].astype(F32)).astype(BF16)
 
     mate_rows = pl.ds(al((1 - core) * HALF, HALF), HALF)
@@ -589,7 +601,7 @@
         "fk": lambda: regroup_relay("k", ks, stage.at[0]),
         "fq": lambda: regroup_relay("q", qs.at[0], stage.at[1]),
         "fg": lambda: regroup_relay("g", gs.at[0], stage.at[2]),
-        "pos": positions, "LN": norm_glu, "conv": conv, "enc": encode, "adapt": adapt, "place": place,
+        "pos": positions, "LN": norm_glu, "conv": conv, "enc": encode, "encx": encode_x, "er": encode_relay, "adapt": adapt, "place": place,
         "hq": lambda: halo("q"), "hg": lambda: halo("g"),
         "sc0": score_own, "sc1": score_next, "prob": prob, "vgr": vg_relay, "vgf": vg_last,
         "rm": lambda: relay(-1), "delta": delta, "key": key,
@@ -643,7 +655,7 @@
         out_specs=(vm, vm),
         scratch_shapes=[
             vmem((NT, COLS, DH), BF16),
-            vmem((DE, COLS), BF16),
+            vmem((DE, QUART), BF16),
             vmem((2, TOK, HC), BF16),
             vmem((2, TOK, HC), BF16),
             vmem((TOK, HC), BF16),
@@ -655,16 +667,16 @@
             vmem(conv_taps.shape, F32),
             vmem((DH, DE), BF16),
             vmem((TOK, COLS), BF16),
-            vmem((8, AUD), jnp.int32),
-            vmem((2, 8, NT * 16), jnp.int32),
+            vmem((8, NX * AUD), jnp.int32),
+            vmem((8, NT * SLOT), jnp.int32),
             vmem((AUD + 32, DE), BF16),
             vmem((AUD + 32, DH), F32),
             vmem((AUD, DE), BF16),
             vmem((NC, 16, DE), BF16),
-            vmem((AUD, DE), BF16),
-            vmem((AUD, COLS), BF16),
-            vmem((NT * 16, 512), BF16),
-            vmem((NT * 16, 512), BF16),
+            vmem((NX, AUD, DE), BF16),
+            vmem((NX * AUD, QUART), BF16),
+            vmem((NT * NX * SLOT, QUART), BF16),
+            vmem((NX, NT * SLOT, QUART), BF16),
             vmem((TOK, COLS), BF16),
             vmem((2, HH, TOK, TOK), F32),
             vmem((2, HH, TOK, TOK), F32),

time: 158 us -> 156 us (0.987)
  Pallas kernels: 154 us -> 152 us
    pallas_call x1, Pallas kernels: 154 us -> 152 us  [body(): pl.pallas_call(kernel, out_shape=(jax.ShapeDtypeStruct((TOK, HC), BF16),...]
where the time goes in v5:
time: 156 us; the launch traced here: 155 us
  Pallas kernels  152 us (97%)
  local copies, waits for them, and re-layouts  2.93 us (2%)
    pallas_call x1, Pallas kernels, body(): pl.pallas_call(kernel, out_shape=(jax.ShapeDtypeStruct((TOK, HC), BF16),...  152 us

profile of v5, /device:TPU:9, one launch (start us, length us, event | category | flops | bytes accessed | tf_op | source)
XLA Modules:
  0.0 155.4 jit_solution(468888509249984607)
XLA Ops:
  0.6 151.8 %shard_map.140 = (bf16[512,512]{1,0:T(8,128)(2,1)}, bf16[512,1024]{1,0:T(8,128)(2,1)}) custom-call(bf16[128,1024]{1,0:T(8,128)(2,1)} %frames.1, bf16[1024,128]{1,0:T(8,128)(2,1)} %vw.1, bf16[1024,128]{1,0:T(8,128)(2,1)} %gw.1, f32[31,128]{1,0:T(8,128)} %taps.1, bf16[128,1024]{1,0:T(8,128)(2,1)} %ow.1, bf16[512,1024]{1,0:T(8,128)(2,1)} %text.1, ...), custom_call_target="tpu_custom_call" | custom-call | flops 12999999488 | bytes 8000000 | tf_op jit(solution)/shard_map/pallas_call | solution.py:648
  152.5 0.0 copy-start
  152.5 2.0 %copy.17 = bf16[512,512]{1,0:T(8,128)(2,1)} copy(bf16[512,512]{1,0:T(8,128)(2,1)} %get-tuple-element.4) | data formatting | bytes 1048576
  154.5 0.0 copy-done
  154.5 1.0 copy.18
Async XLA Ops:
  152.5 2.0 %copy-start = (bf16[512,1024]{1,0:T(8,128)(2,1)S(1)}, bf16[512,1024]{1,0:T(8,128)(2,1)}, u32[]{:S(2)}) copy-start(bf16[512,1024]{1,0:T(8,128)(2,1)} %get-tuple-element.5) | copy-start | bytes 3145732

commit v6 on v5

--- a/solution.py
+++ b/solution.py
@@ -29,17 +29,17 @@
 TILES = ((0, 0, 0, 256), (0, 256, 0, 512), (1, 0, 0, 512), (1, 256, 256, 256))
 N_SEMS = 160
 QUART = COLS // NX
-ROWS_A = 576
+ROWS_A = 512
 ROWS_B = COLS - ROWS_A
 OFFSETS = (0, -1, 1, -2, 2, -3, 3, 4)
 ORDER = (
-    "issue", "i_b0", "i_q", "mm", "i_ax", "LN", "b_s1", "m0", "fq", "conv", "i_g", "d_s0", "p0",
-    "b_s2", "rm", "hq", "d_s1", "a_s0", "p1", "enc", "b_s3", "fg", "r0", "encx", "hg", "i_k",
-    "pos", "d_s2", "a_s1", "fk", "p3", "r1", "er", "sc1", "sc0", "m2", "d_s3", "p2", "i_bm",
-    "m1", "a_s2", "m3", "adapt", "r2", "prob", "r3", "vgr", "place", "t3", "t0", "t2", "a_s3",
-    "rs3", "t4", "rs0", "t5", "ad3", "rs2", "rs4", "t6", "ad0", "t1", "rs5", "ad2", "t7", "ad4",
-    "rs6", "vgf", "rs7", "ad6", "dh0", "dh2", "dh3", "dh7", "ad5", "rs1", "dh1", "ad7", "dh5",
-    "dh6", "ad1", "delta", "dh4", "key",
+    "issue", "i_q", "i_ax", "b_s0", "i_bm", "mm", "LN", "d_s0", "conv", "b_s1", "m0", "p0",
+    "d_s1", "i_k", "a0_s0", "rm", "enc", "hq", "b_s2", "p1", "r0", "a1_s0", "pos", "i_g",
+    "encx", "b_s3", "d_s2", "sc0", "a0_s1", "sc1", "er", "d_s3", "p2", "a1_s1", "a0_s2", "hg",
+    "adapt", "r1", "m1", "prob", "m3", "r2", "a1_s2", "place", "t0", "m2", "t1", "t2", "rs0",
+    "r3", "a0_s3", "p3", "rs1", "vgr", "rs2", "t3", "t4", "t6", "t5", "ad0", "a1_s3", "rs3",
+    "ad1", "ad2", "rs4", "vgf", "rs5", "ad3", "t7", "rs6", "ad4", "dh0", "ad5", "rs7", "dh1",
+    "dh4", "ad6", "dh2", "ad7", "dh6", "dh5", "dh7", "delta", "dh3", "key",
 )
 
 
@@ -61,7 +61,7 @@
     W, AD, qs, gs, ks, low_s, lown, frames_s, vw_s, gw_s, taps_s, ow_s, text_s,
     slot_s, land_s, ext, glu_s, mixs, mixr, enc, adp, pick, inc, hid,
     e_ref, gv_ref, st_own, st_nxt, st_fp, st_fn, dl_own, dl_nxt, dl_fp, dl_fn,
-    VG, psend, pown, precv, rsend, radd, rrecv, vbuf, acc, stage,
+    VG, psend, pown, precv, rsend, radd, rrecv, vbuf, acc,
     ssem, rsem, lsem, aus, aur, rss, rsr,
 ):
     t = lax.axis_index("tm")
@@ -162,11 +162,11 @@
     def b_part(zz, p):
         return W.at[zz * NX + x, pl.ds(ROWS_A + ROWS_B // 2 * p, ROWS_B // 2)]
 
-    def a_ref(zz):
-        return W.at[pl.ds(zz * NX, NX), rows_a]
-
-    def a_part(zz, p):
-        return W.at[pl.ds(zz * NX + 2 * p, 2), rows_a]
+    def a_ref(zz, pair):
+        return W.at[pl.ds(zz * NX + 2 * pair, 2), rows_a]
+
+    def a_part(zz, pair, p):
+        return W.at[zz * NX + 2 * pair + p, rows_a]
 
     def d_ref(zz):
         return AD.at[pl.ds(al(zz * 128, 128), 128)]
@@ -182,9 +182,9 @@
         send(f"{name}{s}", u, u, up)
         send(f"{name}{s}", v, v, dn)
 
-    def a_step(s):
-        need(*([f"a{s - 1}"] if s else ["ax", "vp"]))
-        ring("a", s, a_ref, a_part)
+    def a_step(pair, s):
+        need(*([f"a{pair}_{s - 1}"] if s else ["ax", "vp"]))
+        ring(f"a{pair}_", s, lambda zz: a_ref(zz, pair), lambda zz, p: a_part(zz, pair, p))
 
     def b_step(s):
         need(*([f"b{s - 1}"] if s else ["vp"]))
@@ -213,25 +213,10 @@
         for d in (1, 3, 2):
             send("ax", vp.at[rows_a], W.at[t, rows_a], x_peer(d))
 
-    def beside(cc):
-        return cc + 1 - 2 * core
-
-    def regroup(name, src, dst, stage):
-        y_up, y_dn, far = [lax.rem(c + d, NC) for d in (2, 6, 4)]
-
-        def piece(peer):
-            return src.at[:, pl.ds(al(peer * HC, HC), HC)]
-
-        send(name + "s", piece(far), stage.at[0], (t, y_up))
-        send(name + "s", piece(beside(far)), stage.at[1], (t, y_dn))
-        for peer in (y_up, y_dn, beside(y_up), beside(y_dn), beside(c)):
-            send(name, piece(peer), dst.at[own_rows], (t, peer))
-
-    def regroup_relay(name, dst, stage):
-        need(name + "s")
-        y_up, y_dn = [lax.rem(c + d, NC) for d in (2, 6)]
-        send(name + "2", stage.at[0], dst.at[pl.ds(al(y_dn * 64, 64), 64)], (t, y_up))
-        send(name + "2", stage.at[1], dst.at[pl.ds(al(y_up * 64, 64), 64)], (t, beside(y_dn)))
+    def regroup(name, src, dst):
+        for d in (4, 1, 7, 2, 6, 3, 5):
+            peer = lax.rem(c + d, NC)
+            send(name, src.at[:, pl.ds(al(peer * HC, HC), HC)], dst.at[own_rows], (t, peer))
 
     def positions():
         order = (iota((AUD, AUD), 0) < iota((AUD, AUD), 1)).astype(F32).astype(BF16)
@@ -308,7 +293,7 @@
 
     def halo(name):
         part = qs if name == "q" else gs
-        need(name, name + "2", name + "0")
+        need(name, name + "0")
         send("h" + name, part.at[0], part.at[1], prv)
 
     scale = 1.0 / math.sqrt(DH)
@@ -343,12 +328,12 @@
         lax.fori_loop(0, HH, one_head, 0)
 
     def score_own():
-        need("k", "k2", "k0", "q", "q2", "q0")
+        need("k", "k0", "q", "q0")
         score_tiles(0, low_s, TOK, st_own)
         send("sta", st_own, st_fn, prv)
 
     def score_next():
-        need("k", "k2", "k0", "hq", "low")
+        need("k", "k0", "hq", "low")
         score_tiles(1, lown, jnp.where(t == NT - 1, 0, TOK), st_nxt)
         send("stb", st_nxt, st_fp, nxt)
 
@@ -398,7 +383,7 @@
         return top, bottom
 
     def prob():
-        need("sta", "stb", "g", "g2", "g0", "hg")
+        need("sta", "stb", "g", "g0", "hg")
 
         def prob_head(h, carry):
             f = (factor(st_own, st_fp, h), factor(st_nxt, st_fn, h))
@@ -454,7 +439,7 @@
     def weights_ready(i):
         s = (i - 1) // 2
         need(f"m{s}", f"p{s}", f"r{s}")
-        need(*([f"a{s}", f"b{s}"] if i else ["ax", "vp"]))
+        need(*([f"a0_{s}", f"a1_{s}", f"b{s}"] if i else ["ax", "vp"]))
 
     def terms(i):
         weights_ready(i)
@@ -594,20 +579,18 @@
 
     steps = {
         "issue": issue, "i_ax": issue_ax,
-        "i_b0": lambda: b_step(0), "i_bm": lambda: spread(-1, 1, "p"), "mm": lambda: spread(-1, 3, "m"),
-        "i_k": lambda: regroup("k", k, ks, stage.at[0]),
-        "i_q": lambda: regroup("q", q, qs.at[0], stage.at[1]),
-        "i_g": lambda: regroup("g", g, gs.at[0], stage.at[2]),
-        "fk": lambda: regroup_relay("k", ks, stage.at[0]),
-        "fq": lambda: regroup_relay("q", qs.at[0], stage.at[1]),
-        "fg": lambda: regroup_relay("g", gs.at[0], stage.at[2]),
+        "i_bm": lambda: spread(-1, 1, "p"), "mm": lambda: spread(-1, 3, "m"),
+        "i_k": lambda: regroup("k", k, ks),
+        "i_q": lambda: regroup("q", q, qs.at[0]),
+        "i_g": lambda: regroup("g", g, gs.at[0]),
         "pos": positions, "LN": norm_glu, "conv": conv, "enc": encode, "encx": encode_x, "er": encode_relay, "adapt": adapt, "place": place,
         "hq": lambda: halo("q"), "hg": lambda: halo("g"),
         "sc0": score_own, "sc1": score_next, "prob": prob, "vgr": vg_relay, "vgf": vg_last,
         "rm": lambda: relay(-1), "delta": delta, "key": key,
     }
     for s in range(4):
-        steps[f"a_s{s}"] = lambda s=s: a_step(s)
+        steps[f"a0_s{s}"] = lambda s=s: a_step(0, s)
+        steps[f"a1_s{s}"] = lambda s=s: a_step(1, s)
         steps[f"b_s{s}"] = lambda s=s: b_step(s)
         steps[f"d_s{s}"] = lambda s=s: d_step(s)
         steps[f"p{s}"] = lambda s=s: spread(s, 1, "p")
@@ -692,7 +675,6 @@
             vmem((3, TOK, HC), BF16),
             vmem((TOK, HC), BF16),
             vmem((COLS // 256, TOK, 256), F32),
-            vmem((3, 2, 64, HC), BF16),
             dma((N_SEMS,)),
             dma((N_SEMS,)),
             dma((16,)),

time: 156 us -> 156 us (level)
  no operation moved by 1% of the time
where the time goes in v6:
time: 156 us; the launch traced here: 154 us
  Pallas kernels  151 us (97%)
  local copies, waits for them, and re-layouts  2.93 us (2%)
    pallas_call x1, Pallas kernels, body(): pl.pallas_call(kernel, out_shape=(jax.ShapeDtypeStruct((TOK, HC), BF16),...  151 us

profile of v6, /device:TPU:9, one launch (start us, length us, event | category | flops | bytes accessed | tf_op | source)
XLA Modules:
  0.0 154.5 jit_solution(5913380720276612929)
XLA Ops:
  0.6 150.9 %shard_map.140 = (bf16[512,512]{1,0:T(8,128)(2,1)}, bf16[512,1024]{1,0:T(8,128)(2,1)}) custom-call(bf16[128,1024]{1,0:T(8,128)(2,1)} %frames.1, bf16[1024,128]{1,0:T(8,128)(2,1)} %vw.1, bf16[1024,128]{1,0:T(8,128)(2,1)} %gw.1, f32[31,128]{1,0:T(8,128)} %taps.1, bf16[128,1024]{1,0:T(8,128)(2,1)} %ow.1, bf16[512,1024]{1,0:T(8,128)(2,1)} %text.1, ...), custom_call_target="tpu_custom_call" | custom-call | flops 12999999488 | bytes 8000000 | tf_op jit(solution)/shard_map/pallas_call | solution.py:631
  151.5 0.0 copy-start
  151.5 2.0 %copy.17 = bf16[512,512]{1,0:T(8,128)(2,1)} copy(bf16[512,512]{1,0:T(8,128)(2,1)} %get-tuple-element.4) | data formatting | bytes 1048576
  153.5 0.0 copy-done
  153.5 1.0 copy.18
Async XLA Ops:
  151.5 2.0 %copy-start = (bf16[512,1024]{1,0:T(8,128)(2,1)S(1)}, bf16[512,1024]{1,0:T(8,128)(2,1)}, u32[]{:S(2)}) copy-start(bf16[512,1024]{1,0:T(8,128)(2,1)} %get-tuple-element.5) | copy-start | bytes 3145732

commit v7 on v6

--- a/solution.py
+++ b/solution.py
@@ -33,13 +33,13 @@
 ROWS_B = COLS - ROWS_A
 OFFSETS = (0, -1, 1, -2, 2, -3, 3, 4)
 ORDER = (
-    "issue", "i_q", "i_ax", "b_s0", "i_bm", "mm", "LN", "d_s0", "conv", "b_s1", "m0", "p0",
-    "d_s1", "i_k", "a0_s0", "rm", "enc", "hq", "b_s2", "p1", "r0", "a1_s0", "pos", "i_g",
-    "encx", "b_s3", "d_s2", "sc0", "a0_s1", "sc1", "er", "d_s3", "p2", "a1_s1", "a0_s2", "hg",
-    "adapt", "r1", "m1", "prob", "m3", "r2", "a1_s2", "place", "t0", "m2", "t1", "t2", "rs0",
-    "r3", "a0_s3", "p3", "rs1", "vgr", "rs2", "t3", "t4", "t6", "t5", "ad0", "a1_s3", "rs3",
-    "ad1", "ad2", "rs4", "vgf", "rs5", "ad3", "t7", "rs6", "ad4", "dh0", "ad5", "rs7", "dh1",
-    "dh4", "ad6", "dh2", "ad7", "dh6", "dh5", "dh7", "delta", "dh3", "key",
+    "issue", "i_q", "b_s0", "i_ax", "LN", "mm", "d_s0", "b_s1", "i_bm", "conv", "m0", "p0",
+    "d_s1", "i_k", "b_s2", "hq", "a0_s0", "d_s2", "enc", "r0", "pos", "a1_s0", "i_g", "encx",
+    "a0_s1", "b_s3", "sc0", "a1_s1", "d_s3", "er", "hg", "p3", "a0_s2", "p1", "sc1", "adapt",
+    "p2", "prob", "m1", "rm", "m3", "a1_s2", "r1", "place", "r2", "m2", "t0", "vgr", "r3", "t1",
+    "a0_s3", "a1_s3", "rs0", "t2", "t4", "rs2", "rs1", "t3", "t6", "ad0", "t7", "rs4", "rs3",
+    "t5", "ad1", "ad4", "vgf", "rs5", "dh0", "dh1", "dh4", "rs6", "rs7", "dh2", "dh3", "dh5",
+    "ad3", "ad2", "ad5", "dh6", "ad6", "ad7", "delta", "dh7", "key",
 )
 
 

time: 156 us -> 154 us (0.987)
  Pallas kernels: 151 us -> 149 us
    pallas_call x1, Pallas kernels: 151 us -> 149 us  [body(): pl.pallas_call(kernel, out_shape=(jax.ShapeDtypeStruct((TOK, HC), BF16),...]
where the time goes in v7:
time: 154 us; the launch traced here: 153 us
  Pallas kernels  149 us (97%)
  local copies, waits for them, and re-layouts  2.93 us (2%)
    pallas_call x1, Pallas kernels, body(): pl.pallas_call(kernel, out_shape=(jax.ShapeDtypeStruct((TOK, HC), BF16),...  149 us

profile of v7, /device:TPU:9, one launch (start us, length us, event | category | flops | bytes accessed | tf_op | source)
XLA Modules:
  0.0 152.9 jit_solution(1984738417781216933)
XLA Ops:
  0.6 149.3 %shard_map.140 = (bf16[512,512]{1,0:T(8,128)(2,1)}, bf16[512,1024]{1,0:T(8,128)(2,1)}) custom-call(bf16[128,1024]{1,0:T(8,128)(2,1)} %frames.1, bf16[1024,128]{1,0:T(8,128)(2,1)} %vw.1, bf16[1024,128]{1,0:T(8,128)(2,1)} %gw.1, f32[31,128]{1,0:T(8,128)} %taps.1, bf16[128,1024]{1,0:T(8,128)(2,1)} %ow.1, bf16[512,1024]{1,0:T(8,128)(2,1)} %text.1, ...), custom_call_target="tpu_custom_call" | custom-call | flops 12999999488 | bytes 8000000 | tf_op jit(solution)/shard_map/pallas_call | solution.py:631
  150.0 0.0 copy-start
  150.0 2.0 %copy.17 = bf16[512,512]{1,0:T(8,128)(2,1)} copy(bf16[512,512]{1,0:T(8,128)(2,1)} %get-tuple-element.4) | data formatting | bytes 1048576
  151.9 0.0 copy-done
  151.9 1.0 copy.18
Async XLA Ops:
  150.0 2.0 %copy-start = (bf16[512,1024]{1,0:T(8,128)(2,1)S(1)}, bf16[512,1024]{1,0:T(8,128)(2,1)}, u32[]{:S(2)}) copy-start(bf16[512,1024]{1,0:T(8,128)(2,1)} %get-tuple-element.5) | copy-start | bytes 3145732

commit v8 on v3

--- a/solution.py
+++ b/solution.py
@@ -28,17 +28,17 @@
 SLOT = 8
 TILES = ((0, 0, 0, 256), (0, 256, 0, 512), (1, 0, 0, 512), (1, 256, 256, 256))
 N_SEMS = 160
-ROWS_A = 352
+ROWS_A = 384
 ROWS_B = COLS - ROWS_A
 OFFSETS = (0, -1, 1, -2, 2, -3, 3, 4)
 ORDER = (
-    "issue", "i_b0", "i_k", "i_q", "i_ax", "mm", "b_s1", "p0", "m0", "LN", "fk", "fq", "conv",
-    "i_g", "d_s0", "b_s2", "i_bm", "rm", "hq", "sc0", "b_s3", "pos", "enc", "fg", "d_s1", "r0",
-    "p3", "hg", "d_s2", "d_s3", "a_s0", "p1", "sc1", "adapt", "m1", "p2", "m2", "m3", "prob",
-    "r1", "a_s1", "r3", "vgr", "place", "t0", "t1", "r2", "vgf", "t2", "rs0", "a_s2", "t3",
-    "rs1", "t4", "rs2", "ad0", "dh0", "rs3", "dh1", "ad1", "rs4", "dh2", "dh3", "dh4", "ad2",
-    "a_s3", "t5", "ad3", "t6", "ad4", "dh5", "rs5", "dh6", "rs6", "t7", "dh7", "ad5", "ad6",
-    "rs7", "ad7", "delta", "key",
+    "issue", "b_s0", "i_k", "i_bm", "mm", "d_s0", "m0", "p0", "LN", "i_q", "conv", "b_s1",
+    "d_s1", "i_ax", "p1", "r0", "pos", "hq", "b_s2", "i_g", "d_s2", "sc0", "a1_s0", "hg", "rm",
+    "p2", "d_s3", "enc", "b_s3", "a0_s0", "sc1", "a1_s1", "adapt", "m1", "r1", "prob", "vgr",
+    "a0_s1", "p3", "m3", "m2", "r2", "place", "t0", "t1", "t2", "rs0", "a1_s2", "t3", "a0_s2",
+    "rs1", "vgf", "rs2", "t4", "ad1", "r3", "rs3", "dh3", "rs4", "dh1", "ad0", "dh2", "a1_s3",
+    "ad3", "ad2", "t5", "a0_s3", "t6", "ad4", "rs5", "rs6", "t7", "ad5", "ad6", "rs7", "dh4",
+    "dh0", "dh5", "ad7", "delta", "dh7", "dh6", "key",
 )
 
 
@@ -60,7 +60,7 @@
     W, AD, qs, gs, ks, low_s, lown, frames_s, vw_s, gw_s, taps_s, ow_s, text_s,
     slot_s, land_s, ext, glu_s, mixs, mixr, enc, adp, pick, inc, hid,
     e_ref, gv_ref, st_own, st_nxt, st_fp, st_fn, dl_own, dl_nxt, dl_fp, dl_fn,
-    VG, psend, pown, precv, rsend, radd, rrecv, vbuf, acc, stage,
+    VG, psend, pown, precv, rsend, radd, rrecv, vbuf, acc,
     ssem, rsem, lsem, aus, aur, rss, rsr,
 ):
     t = lax.axis_index("tm")
@@ -160,11 +160,11 @@
     def b_part(zz, p):
         return W.at[zz * NX + x, pl.ds(ROWS_A + ROWS_B // 2 * p, ROWS_B // 2)]
 
-    def a_ref(zz):
-        return W.at[pl.ds(zz * NX, NX), rows_a]
-
-    def a_part(zz, p):
-        return W.at[pl.ds(zz * NX + 2 * p, 2), rows_a]
+    def a_ref(zz, pair):
+        return W.at[pl.ds(zz * NX + 2 * pair, 2), rows_a]
+
+    def a_part(zz, pair, p):
+        return W.at[zz * NX + 2 * pair + p, rows_a]
 
     def d_ref(zz):
         return AD.at[pl.ds(al(zz * 128, 128), 128)]
@@ -180,9 +180,9 @@
         send(f"{name}{s}", u, u, up)
         send(f"{name}{s}", v, v, dn)
 
-    def a_step(s):
-        need(*([f"a{s - 1}"] if s else ["ax", "vp"]))
-        ring("a", s, a_ref, a_part)
+    def a_step(pair, s):
+        need(*([f"a{pair}_{s - 1}"] if s else ["ax", "vp"]))
+        ring(f"a{pair}_", s, lambda zz: a_ref(zz, pair), lambda zz, p: a_part(zz, pair, p))
 
     def b_step(s):
         need(*([f"b{s - 1}"] if s else ["vp"]))
@@ -211,25 +211,10 @@
         for d in (1, 3, 2):
             send("ax", vp.at[rows_a], W.at[t, rows_a], x_peer(d))
 
-    def beside(cc):
-        return cc + 1 - 2 * core
-
-    def regroup(name, src, dst, stage):
-        y_up, y_dn, far = [lax.rem(c + d, NC) for d in (2, 6, 4)]
-
-        def piece(peer):
-            return src.at[:, pl.ds(al(peer * HC, HC), HC)]
-
-        send(name + "s", piece(far), stage.at[0], (t, y_up))
-        send(name + "s", piece(beside(far)), stage.at[1], (t, y_dn))
-        for peer in (y_up, y_dn, beside(y_up), beside(y_dn), beside(c)):
-            send(name, piece(peer), dst.at[own_rows], (t, peer))
-
-    def regroup_relay(name, dst, stage):
-        need(name + "s")
-        y_up, y_dn = [lax.rem(c + d, NC) for d in (2, 6)]
-        send(name + "2", stage.at[0], dst.at[pl.ds(al(y_dn * 64, 64), 64)], (t, y_up))
-        send(name + "2", stage.at[1], dst.at[pl.ds(al(y_up * 64, 64), 64)], (t, beside(y_dn)))
+    def regroup(name, src, dst):
+        for d in (4, 1, 7, 2, 6, 3, 5):
+            peer = lax.rem(c + d, NC)
+            send(name, src.at[:, pl.ds(al(peer * HC, HC), HC)], dst.at[own_rows], (t, peer))
 
     def positions():
         order = (iota((AUD, AUD), 0) < iota((AUD, AUD), 1)).astype(F32).astype(BF16)
@@ -296,7 +281,7 @@
 
     def halo(name):
         part = qs if name == "q" else gs
-        need(name, name + "2", name + "0")
+        need(name, name + "0")
         send("h" + name, part.at[0], part.at[1], prv)
 
     scale = 1.0 / math.sqrt(DH)
@@ -331,12 +316,12 @@
         lax.fori_loop(0, HH, one_head, 0)
 
     def score_own():
-        need("k", "k2", "k0", "q", "q2", "q0")
+        need("k", "k0", "q", "q0")
         score_tiles(0, low_s, TOK, st_own)
         send("sta", st_own, st_fn, prv)
 
     def score_next():
-        need("k", "k2", "k0", "hq", "low")
+        need("k", "k0", "hq", "low")
         score_tiles(1, lown, jnp.where(t == NT - 1, 0, TOK), st_nxt)
         send("stb", st_nxt, st_fp, nxt)
 
@@ -387,7 +372,7 @@
         return top, bottom
 
     def prob():
-        need("sta", "stb", "g", "g2", "g0", "hg")
+        need("sta", "stb", "g", "g0", "hg")
 
         def prob_head(h, carry):
             f = (factor(st_own, st_fp, h), factor(st_nxt, st_fn, h))
@@ -442,7 +427,7 @@
     def weights_ready(i):
         s = (i - 1) // 2
         need(f"m{s}", f"p{s}", f"r{s}")
-        need(*([f"a{s}", f"b{s}"] if i else ["ax", "vp"]))
+        need(*([f"a0_{s}", f"a1_{s}", f"b{s}"] if i else ["ax", "vp"]))
 
     def terms(i):
         weights_ready(i)
@@ -582,20 +567,18 @@
 
     steps = {
         "issue": issue, "i_ax": issue_ax,
-        "i_b0": lambda: b_step(0), "i_bm": lambda: spread(-1, 1, "p"), "mm": lambda: spread(-1, 3, "m"),
-        "i_k": lambda: regroup("k", k, ks, stage.at[0]),
-        "i_q": lambda: regroup("q", q, qs.at[0], stage.at[1]),
-        "i_g": lambda: regroup("g", g, gs.at[0], stage.at[2]),
-        "fk": lambda: regroup_relay("k", ks, stage.at[0]),
-        "fq": lambda: regroup_relay("q", qs.at[0], stage.at[1]),
-        "fg": lambda: regroup_relay("g", gs.at[0], stage.at[2]),
+        "i_bm": lambda: spread(-1, 1, "p"), "mm": lambda: spread(-1, 3, "m"),
+        "i_k": lambda: regroup("k", k, ks),
+        "i_q": lambda: regroup("q", q, qs.at[0]),
+        "i_g": lambda: regroup("g", g, gs.at[0]),
         "pos": positions, "LN": norm_glu, "conv": conv, "enc": encode, "adapt": adapt, "place": place,
         "hq": lambda: halo("q"), "hg": lambda: halo("g"),
         "sc0": score_own, "sc1": score_next, "prob": prob, "vgr": vg_relay, "vgf": vg_last,
         "rm": lambda: relay(-1), "delta": delta, "key": key,
     }
     for s in range(4):
-        steps[f"a_s{s}"] = lambda s=s: a_step(s)
+        steps[f"a0_s{s}"] = lambda s=s: a_step(0, s)
+        steps[f"a1_s{s}"] = lambda s=s: a_step(1, s)
         steps[f"b_s{s}"] = lambda s=s: b_step(s)
         steps[f"d_s{s}"] = lambda s=s: d_step(s)
         steps[f"p{s}"] = lambda s=s: spread(s, 1, "p")
@@ -680,7 +663,6 @@
             vmem((3, TOK, HC), BF16),
             vmem((TOK, HC), BF16),
             vmem((COLS // 256, TOK, 256), F32),
-            vmem((3, 2, 64, HC), BF16),
             dma((N_SEMS,)),
             dma((N_SEMS,)),
             dma((16,)),

time: 158 us -> 157 us (level)
  no operation moved by 1% of the time
where the time goes in v8:
time: 157 us; the launch traced here: 156 us
  Pallas kernels  153 us (97%)
  local copies, waits for them, and re-layouts  2.93 us (2%)
    pallas_call x1, Pallas kernels, body(): pl.pallas_call(kernel, out_shape=(jax.ShapeDtypeStruct((TOK, HC), BF16),...  153 us

profile of v8, /device:TPU:9, one launch (start us, length us, event | category | flops | bytes accessed | tf_op | source)
XLA Modules:
  0.0 156.4 jit_solution(17213705200666925766)
XLA Ops:
  0.6 152.8 %shard_map.140 = (bf16[512,512]{1,0:T(8,128)(2,1)}, bf16[512,1024]{1,0:T(8,128)(2,1)}) custom-call(bf16[128,1024]{1,0:T(8,128)(2,1)} %frames.1, bf16[1024,128]{1,0:T(8,128)(2,1)} %vw.1, bf16[1024,128]{1,0:T(8,128)(2,1)} %gw.1, f32[31,128]{1,0:T(8,128)} %taps.1, bf16[128,1024]{1,0:T(8,128)(2,1)} %ow.1, bf16[512,1024]{1,0:T(8,128)(2,1)} %text.1, ...), custom_call_target="tpu_custom_call" | custom-call | flops 12999999488 | bytes 8000000 | tf_op jit(solution)/shard_map/pallas_call | solution.py:619
  153.4 0.0 copy-start
  153.4 2.0 %copy.17 = bf16[512,512]{1,0:T(8,128)(2,1)} copy(bf16[512,512]{1,0:T(8,128)(2,1)} %get-tuple-element.4) | data formatting | bytes 1048576
  155.4 0.0 copy-done
  155.4 1.0 copy.18
Async XLA Ops:
  153.4 2.0 %copy-start = (bf16[512,1024]{1,0:T(8,128)(2,1)S(1)}, bf16[512,1024]{1,0:T(8,128)(2,1)}, u32[]{:S(2)}) copy-start(bf16[512,1024]{1,0:T(8,128)(2,1)} %get-tuple-element.5) | copy-start | bytes 3145732

commit v9 on v7

--- a/solution.py
+++ b/solution.py
@@ -27,19 +27,19 @@
 HALF = TOK // 2
 SLOT = 8
 TILES = ((0, 0, 0, 256), (0, 256, 0, 512), (1, 0, 0, 512), (1, 256, 256, 256))
-N_SEMS = 160
+N_SEMS = 176
 QUART = COLS // NX
 ROWS_A = 512
 ROWS_B = COLS - ROWS_A
 OFFSETS = (0, -1, 1, -2, 2, -3, 3, 4)
 ORDER = (
-    "issue", "i_q", "b_s0", "i_ax", "LN", "mm", "d_s0", "b_s1", "i_bm", "conv", "m0", "p0",
-    "d_s1", "i_k", "b_s2", "hq", "a0_s0", "d_s2", "enc", "r0", "pos", "a1_s0", "i_g", "encx",
-    "a0_s1", "b_s3", "sc0", "a1_s1", "d_s3", "er", "hg", "p3", "a0_s2", "p1", "sc1", "adapt",
-    "p2", "prob", "m1", "rm", "m3", "a1_s2", "r1", "place", "r2", "m2", "t0", "vgr", "r3", "t1",
-    "a0_s3", "a1_s3", "rs0", "t2", "t4", "rs2", "rs1", "t3", "t6", "ad0", "t7", "rs4", "rs3",
-    "t5", "ad1", "ad4", "vgf", "rs5", "dh0", "dh1", "dh4", "rs6", "rs7", "dh2", "dh3", "dh5",
-    "ad3", "ad2", "ad5", "dh6", "ad6", "ad7", "delta", "dh7", "key",
+    "issue", "i_q", "i_ax", "hq", "b_s0", "d_s0", "hg", "b_s1", "p0", "LN", "conv", "a0_s0",
+    "d_s1", "pos", "r0", "enc", "d_s2", "a1_s0", "d_s3", "i_bm", "i_k", "encx", "a0_s1", "i_g",
+    "b_s2", "er", "a0_s2", "p1", "sc0", "a1_s1", "sc1", "m2", "adapt", "mm", "m0", "p2", "prob",
+    "rm", "m1", "b_s3", "r1", "vgr", "a1_s2", "place", "t0", "m3", "t1", "r2", "t2", "rs0",
+    "t3", "rs1", "t4", "vgf", "r3", "rs2", "a1_s3", "p3", "rs3", "rs4", "a0_s3", "ad0", "t5",
+    "t6", "ad3", "dh0", "ad1", "ad4", "dh1", "ad2", "rs5", "dh3", "rs6", "t7", "dh4", "dh6",
+    "ad5", "ad6", "rs7", "dh5", "ad7", "dh2", "dh7", "delta", "key",
 )
 
 
@@ -136,6 +136,9 @@
         lax.fori_loop(1, NT, greet, 0)
         for d in range(1, NC):
             pl.semaphore_signal(bar, inc=1, device_id=ctx_peer(d), device_id_type=MESH)
+            for beside in (lax.rem(t + 1, NT), lax.rem(t + NT - 1, NT)):
+                peer = (beside, lax.rem(c + d, NC))
+                pl.semaphore_signal(bar, inc=1, device_id=peer, device_id_type=MESH)
         local("frames", frames, frames_s)
         local("vw", vw, vw_s)
         local("gw", gw, gw_s)
@@ -148,7 +151,7 @@
         local("g0", g.at[:, own_cols], gs.at[0, own_rows])
         local("text", text, text_s)
         low_s[...] = jnp.broadcast_to(low[...], low_s.shape)
-        pl.semaphore_wait(bar, NT - 1 + NC - 1)
+        pl.semaphore_wait(bar, NT - 1 + 3 * (NC - 1))
         send("fh", frames.at[pl.ds(AUD - 16, 16)], ext.at[pl.ds(0, 16)], nxt)
         send("fh", frames.at[pl.ds(0, 16)], ext.at[pl.ds(AUD + 16, 16)], prv)
         for d in (1, 3, 2):
@@ -291,10 +294,11 @@
             part = enc.at[lax.rem(x + NX - d, NX), pl.ds(at, AUD // 2)]
             send("ex2", part, part, x_peer(d))
 
-    def halo(name):
-        part = qs if name == "q" else gs
-        need(name, name + "0")
-        send("h" + name, part.at[0], part.at[1], prv)
+    def halo(name, src, dst):
+        before = lax.rem(t + NT - 1, NT)
+        for d in (4, 1, 7, 2, 6, 3, 5, 0):
+            peer = lax.rem(c + d, NC)
+            send("h" + name, src.at[:, pl.ds(al(peer * HC, HC), HC)], dst.at[own_rows], (before, peer))
 
     scale = 1.0 / math.sqrt(DH)
     base = t * TOK
@@ -584,7 +588,7 @@
         "i_q": lambda: regroup("q", q, qs.at[0]),
         "i_g": lambda: regroup("g", g, gs.at[0]),
         "pos": positions, "LN": norm_glu, "conv": conv, "enc": encode, "encx": encode_x, "er": encode_relay, "adapt": adapt, "place": place,
-        "hq": lambda: halo("q"), "hg": lambda: halo("g"),
+        "hq": lambda: halo("q", q, qs.at[1]), "hg": lambda: halo("g", g, gs.at[1]),
         "sc0": score_own, "sc1": score_next, "prob": prob, "vgr": vg_relay, "vgf": vg_last,
         "rm": lambda: relay(-1), "delta": delta, "key": key,
     }

time: 154 us -> 155 us (level)
  no operation moved by 1% of the time
where the time goes in v9:
time: 155 us; the launch traced here: 153 us
  Pallas kernels  149 us (96%)
  local copies, waits for them, and re-layouts  2.93 us (2%)
    pallas_call x1, Pallas kernels, body(): pl.pallas_call(kernel, out_shape=(jax.ShapeDtypeStruct((TOK, HC), BF16),...  149 us

profile of v9, /device:TPU:9, one launch (start us, length us, event | category | flops | bytes accessed | tf_op | source)
XLA Modules:
  0.0 152.9 jit_solution(9125749061439292073)
XLA Ops:
  0.6 149.3 %shard_map.140 = (bf16[512,512]{1,0:T(8,128)(2,1)}, bf16[512,1024]{1,0:T(8,128)(2,1)}) custom-call(bf16[128,1024]{1,0:T(8,128)(2,1)} %frames.1, bf16[1024,128]{1,0:T(8,128)(2,1)} %vw.1, bf16[1024,128]{1,0:T(8,128)(2,1)} %gw.1, f32[31,128]{1,0:T(8,128)} %taps.1, bf16[128,1024]{1,0:T(8,128)(2,1)} %ow.1, bf16[512,1024]{1,0:T(8,128)(2,1)} %text.1, ...), custom_call_target="tpu_custom_call" | custom-call | flops 12999999488 | bytes 8000000 | tf_op jit(solution)/shard_map/pallas_call | solution.py:635
  149.9 0.0 copy-start
  149.9 2.0 %copy.17 = bf16[512,512]{1,0:T(8,128)(2,1)} copy(bf16[512,512]{1,0:T(8,128)(2,1)} %get-tuple-element.4) | data formatting | bytes 1048576
  151.9 0.0 copy-done
  151.9 1.0 copy.18
Async XLA Ops:
  149.9 2.0 %copy-start = (bf16[512,1024]{1,0:T(8,128)(2,1)S(1)}, bf16[512,1024]{1,0:T(8,128)(2,1)}, u32[]{:S(2)}) copy-start(bf16[512,1024]{1,0:T(8,128)(2,1)} %get-tuple-element.5) | copy-start | bytes 3145732

commit v10 on v7

--- a/solution.py
+++ b/solution.py
@@ -61,7 +61,7 @@
     W, AD, qs, gs, ks, low_s, lown, frames_s, vw_s, gw_s, taps_s, ow_s, text_s,
     slot_s, land_s, ext, glu_s, mixs, mixr, enc, adp, pick, inc, hid,
     e_ref, gv_ref, st_own, st_nxt, st_fp, st_fn, dl_own, dl_nxt, dl_fp, dl_fn,
-    VG, psend, pown, precv, rsend, radd, rrecv, vbuf, acc,
+    VG, pfull, precv, rsend, radd, rrecv, vbuf, acc,
     ssem, rsem, lsem, aus, aur, rss, rsr,
 ):
     t = lax.axis_index("tm")
@@ -303,7 +303,7 @@
     def head_cols(h):
         return pl.ds(al(h * DH, DH), DH)
 
-    def score_tiles(block, lows, limit, stats):
+    def score_tiles(block, lows, floor, stats):
         def one_head(h, carry):
             hs = head_cols(h)
             for b, i0, j0, jn in TILES:
@@ -312,14 +312,12 @@
                 qi = pl.ds(i0, HALF)
                 s = dot_t(ks[pl.ds(j0, jn), hs], qs[b, qi, hs]) * scale
                 jj = iota((jn, HALF), 0) + j0
-                ok = jj >= lows[pl.ds(0, 1), qi] - base
+                ok = jj >= jnp.maximum(lows[pl.ds(0, 1), qi] - base, floor)
                 if block == 0:
                     ok = ok & (jj <= iota((jn, HALF), 1) + i0)
-                else:
-                    ok = ok & (jj < limit)
                 s = jnp.where(ok, s, MASK_FILL)
-                m = jnp.max(s, axis=0, keepdims=True)
-                e = jnp.where(ok, jnp.exp(s - m), 0.0)
+                m = jnp.maximum(jnp.max(s, axis=0, keepdims=True), MASK_FILL / 10)
+                e = jnp.exp(s - m)
                 n = jnp.sum(e, axis=0, keepdims=True)
                 e_ref[b, h, pl.ds(j0, jn), qi] = e
                 stats[h, :, qi] = jnp.where(row8 == 0, m, n)
@@ -329,12 +327,12 @@
 
     def score_own():
         need("k", "k0", "q", "q0")
-        score_tiles(0, low_s, TOK, st_own)
+        score_tiles(0, low_s, 0, st_own)
         send("sta", st_own, st_fn, prv)
 
     def score_next():
         need("k", "k0", "hq", "low")
-        score_tiles(1, lown, jnp.where(t == NT - 1, 0, TOK), st_nxt)
+        score_tiles(1, lown, jnp.where(t == NT - 1, TOK, 0), st_nxt)
         send("stb", st_nxt, st_fp, nxt)
 
     group_rows = NX * SLOT
@@ -444,11 +442,10 @@
     def terms(i):
         weights_ready(i)
         cp = zat(OFFSETS[i])
-        w = jnp.concatenate([W[cp * HH + j] for j in range(HH)], axis=1)
-        psend[i] = dot(hid[mate_rows, :], w).astype(BF16)
-        send(f"pair{i}", psend.at[i], precv.at[i], mate)
-        w = jnp.concatenate([W[cp * HH + j] for j in range(HH)], axis=1)
-        pown[i] = dot(hid[my_rows, :], w).astype(BF16)
+        for j in range(0, HH, 2):
+            w = jnp.concatenate([W[cp * HH + j], W[cp * HH + j + 1]], axis=1)
+            pfull[i, :, pl.ds(j * DH, 2 * DH)] = dot(hid[...], w).astype(BF16)
+        send(f"pair{i}", pfull.at[i, mate_rows], precv.at[i], mate)
 
     def owner_copy(side, kd, i):
         owner = lax.rem(yy + 1 + 2 * side, NC // 2) * 2 + kd
@@ -478,7 +475,7 @@
     def chip_sum(i):
         e, kd = owner_of(i)
         need(f"pair{i}")
-        total = pown[i].astype(F32) + precv[i].astype(F32)
+        total = pfull[i, my_rows, :].astype(F32) + precv[i].astype(F32)
         rsend[i] = total.astype(BF16)
 
         @pl.when(e == 2)
@@ -667,8 +664,7 @@
         + [vmem((HH, 8, TOK), F32)] * 8
         + [
             vmem((NC, TOK, HC), BF16),
-            vmem((NC, HALF, HC), BF16),
-            vmem((NC, HALF, HC), BF16),
+            vmem((NC, TOK, HC), BF16),
             vmem((NC, HALF, HC), BF16),
             vmem((NC, HALF, HC), BF16),
             vmem((2, HALF, HC), BF16),

time: 154 us -> 154 us (level)
  no operation moved by 1% of the time
where the time goes in v10:
time: 154 us; the launch traced here: 153 us
  Pallas kernels  149 us (97%)
  local copies, waits for them, and re-layouts  2.93 us (2%)
    pallas_call x1, Pallas kernels, body(): pl.pallas_call(kernel, out_shape=(jax.ShapeDtypeStruct((TOK, HC), BF16),...  149 us

profile of v10, /device:TPU:9, one launch (start us, length us, event | category | flops | bytes accessed | tf_op | source)
XLA Modules:
  0.0 152.8 jit_solution(13065620807005819721)
XLA Ops:
  0.6 149.2 %shard_map.140 = (bf16[512,512]{1,0:T(8,128)(2,1)}, bf16[512,1024]{1,0:T(8,128)(2,1)}) custom-call(bf16[128,1024]{1,0:T(8,128)(2,1)} %frames.1, bf16[1024,128]{1,0:T(8,128)(2,1)} %vw.1, bf16[1024,128]{1,0:T(8,128)(2,1)} %gw.1, f32[31,128]{1,0:T(8,128)} %taps.1, bf16[128,1024]{1,0:T(8,128)(2,1)} %ow.1, bf16[512,1024]{1,0:T(8,128)(2,1)} %text.1, ...), custom_call_target="tpu_custom_call" | custom-call | flops 12999999488 | bytes 8000000 | tf_op jit(solution)/shard_map/pallas_call | solution.py:628
  149.8 0.0 copy-start
  149.8 2.0 %copy.17 = bf16[512,512]{1,0:T(8,128)(2,1)} copy(bf16[512,512]{1,0:T(8,128)(2,1)} %get-tuple-element.4) | data formatting | bytes 1048576
  151.8 0.0 copy-done
  151.8 1.0 copy.18
Async XLA Ops:
  149.8 2.0 %copy-start = (bf16[512,1024]{1,0:T(8,128)(2,1)S(1)}, bf16[512,1024]{1,0:T(8,128)(2,1)}, u32[]{:S(2)}) copy-start(bf16[512,1024]{1,0:T(8,128)(2,1)} %get-tuple-element.5) | copy-start | bytes 3145732

commit v11 on v8

--- a/solution.py
+++ b/solution.py
@@ -32,13 +32,13 @@
 ROWS_B = COLS - ROWS_A
 OFFSETS = (0, -1, 1, -2, 2, -3, 3, 4)
 ORDER = (
-    "issue", "b_s0", "i_k", "i_bm", "mm", "d_s0", "m0", "p0", "LN", "i_q", "conv", "b_s1",
-    "d_s1", "i_ax", "p1", "r0", "pos", "hq", "b_s2", "i_g", "d_s2", "sc0", "a1_s0", "hg", "rm",
-    "p2", "d_s3", "enc", "b_s3", "a0_s0", "sc1", "a1_s1", "adapt", "m1", "r1", "prob", "vgr",
-    "a0_s1", "p3", "m3", "m2", "r2", "place", "t0", "t1", "t2", "rs0", "a1_s2", "t3", "a0_s2",
-    "rs1", "vgf", "rs2", "t4", "ad1", "r3", "rs3", "dh3", "rs4", "dh1", "ad0", "dh2", "a1_s3",
-    "ad3", "ad2", "t5", "a0_s3", "t6", "ad4", "rs5", "rs6", "t7", "ad5", "ad6", "rs7", "dh4",
-    "dh0", "dh5", "ad7", "delta", "dh7", "dh6", "key",
+    "issue", "i_b0", "i_k", "i_q", "mm", "pos", "LN", "d_s0", "i_bm", "p0", "m0", "conv",
+    "d_s1", "b_s1", "i_ax", "hq", "rm", "sc0", "i_g", "enc", "b_s2", "p1", "d_s2", "r0", "hg",
+    "p2", "d_s3", "b_s3", "a_s0", "sc1", "m3", "adapt", "r1", "m1", "m2", "prob", "a_s1", "r2",
+    "vgr", "place", "t0", "t1", "t2", "rs0", "rs1", "a_s2", "t3", "vgf", "p3", "rs2", "t4",
+    "rs3", "dh0", "ad0", "rs4", "dh1", "ad1", "r3", "dh2", "ad2", "dh3", "dh4", "a_s3", "ad3",
+    "ad4", "t5", "t6", "dh5", "dh6", "rs5", "rs6", "t7", "dh7", "rs7", "ad5", "ad6", "ad7",
+    "delta", "key",
 )
 
 
@@ -160,11 +160,11 @@
     def b_part(zz, p):
         return W.at[zz * NX + x, pl.ds(ROWS_A + ROWS_B // 2 * p, ROWS_B // 2)]
 
-    def a_ref(zz, pair):
-        return W.at[pl.ds(zz * NX + 2 * pair, 2), rows_a]
-
-    def a_part(zz, pair, p):
-        return W.at[zz * NX + 2 * pair + p, rows_a]
+    def a_ref(zz):
+        return W.at[pl.ds(zz * NX, NX), rows_a]
+
+    def a_part(zz, p):
+        return W.at[pl.ds(zz * NX + 2 * p, 2), rows_a]
 
     def d_ref(zz):
         return AD.at[pl.ds(al(zz * 128, 128), 128)]
@@ -180,9 +180,9 @@
         send(f"{name}{s}", u, u, up)
         send(f"{name}{s}", v, v, dn)
 
-    def a_step(pair, s):
-        need(*([f"a{pair}_{s - 1}"] if s else ["ax", "vp"]))
-        ring(f"a{pair}_", s, lambda zz: a_ref(zz, pair), lambda zz, p: a_part(zz, pair, p))
+    def a_step(s):
+        need(*([f"a{s - 1}"] if s else ["ax", "vp"]))
+        ring("a", s, a_ref, a_part)
 
     def b_step(s):
         need(*([f"b{s - 1}"] if s else ["vp"]))
@@ -201,18 +201,17 @@
             send(f"{kind}{s}", b_ref(zat(o)), b_ref(zat(o)), x_peer(d))
 
     def relay(s):
-        turn = 3 if s in (-1, 3) else 1
-        need(f"p{s}" if turn == 1 else f"m{s}")
-        origin = lax.rem(x + NX - turn, NX)
+        need(f"p{s}")
+        behind = lax.rem(x + NX - 1, NX)
         for o in reached(s):
-            send(f"r{s}", b_ref(zat(o), origin), b_ref(zat(o), origin), x_peer(turn))
+            send(f"r{s}", b_ref(zat(o), behind), b_ref(zat(o), behind), x_peer(1))
 
     def issue_ax():
         for d in (1, 3, 2):
             send("ax", vp.at[rows_a], W.at[t, rows_a], x_peer(d))
 
     def regroup(name, src, dst):
-        for d in (4, 1, 7, 2, 6, 3, 5):
+        for d in (1, 7, 2, 6, 3, 5, 4):
             peer = lax.rem(c + d, NC)
             send(name, src.at[:, pl.ds(al(peer * HC, HC), HC)], dst.at[own_rows], (t, peer))
 
@@ -427,7 +426,7 @@
     def weights_ready(i):
         s = (i - 1) // 2
         need(f"m{s}", f"p{s}", f"r{s}")
-        need(*([f"a0_{s}", f"a1_{s}", f"b{s}"] if i else ["ax", "vp"]))
+        need(*([f"a{s}", f"b{s}"] if i else ["ax", "vp"]))
 
     def terms(i):
         weights_ready(i)
@@ -567,7 +566,7 @@
 
     steps = {
         "issue": issue, "i_ax": issue_ax,
-        "i_bm": lambda: spread(-1, 1, "p"), "mm": lambda: spread(-1, 3, "m"),
+        "i_b0": lambda: b_step(0), "i_bm": lambda: spread(-1, 1, "p"), "mm": lambda: spread(-1, 3, "m"),
         "i_k": lambda: regroup("k", k, ks),
         "i_q": lambda: regroup("q", q, qs.at[0]),
         "i_g": lambda: regroup("g", g, gs.at[0]),
@@ -577,8 +576,7 @@
         "rm": lambda: relay(-1), "delta": delta, "key": key,
     }
     for s in range(4):
-        steps[f"a0_s{s}"] = lambda s=s: a_step(0, s)
-        steps[f"a1_s{s}"] = lambda s=s: a_step(1, s)
+        steps[f"a_s{s}"] = lambda s=s: a_step(s)
         steps[f"b_s{s}"] = lambda s=s: b_step(s)
         steps[f"d_s{s}"] = lambda s=s: d_step(s)
         steps[f"p{s}"] = lambda s=s: spread(s, 1, "p")

time: 157 us -> 149 us (0.949)
  Pallas kernels: 153 us -> 145 us
    pallas_call x1, Pallas kernels: 153 us -> 145 us  [body(): pl.pallas_call(kernel, out_shape=(jax.ShapeDtypeStruct((TOK, HC), BF16),...]
where the time goes in v11:
time: 149 us
  Pallas kernels  145 us (97%)
  local copies, waits for them, and re-layouts  2.93 us (2%)
    pallas_call x1, Pallas kernels, body(): pl.pallas_call(kernel, out_shape=(jax.ShapeDtypeStruct((TOK, HC), BF16),...  145 us

profile of v11, /device:TPU:9, one launch (start us, length us, event | category | flops | bytes accessed | tf_op | source)
XLA Modules:
  0.0 148.9 jit_solution(5419015879381653630)
XLA Ops:
  0.6 145.3 %shard_map.140 = (bf16[512,512]{1,0:T(8,128)(2,1)}, bf16[512,1024]{1,0:T(8,128)(2,1)}) custom-call(bf16[128,1024]{1,0:T(8,128)(2,1)} %frames.1, bf16[1024,128]{1,0:T(8,128)(2,1)} %vw.1, bf16[1024,128]{1,0:T(8,128)(2,1)} %gw.1, f32[31,128]{1,0:T(8,128)} %taps.1, bf16[128,1024]{1,0:T(8,128)(2,1)} %ow.1, bf16[512,1024]{1,0:T(8,128)(2,1)} %text.1, ...), custom_call_target="tpu_custom_call" | custom-call | flops 12999999488 | bytes 8000000 | tf_op jit(solution)/shard_map/pallas_call | solution.py:617
  145.9 0.0 copy-start
  145.9 2.0 %copy.17 = bf16[512,512]{1,0:T(8,128)(2,1)} copy(bf16[512,512]{1,0:T(8,128)(2,1)} %get-tuple-element.4) | data formatting | bytes 1048576
  147.9 0.0 copy-done
  147.9 1.0 copy.18
Async XLA Ops:
  145.9 2.0 %copy-start = (bf16[512,1024]{1,0:T(8,128)(2,1)S(1)}, bf16[512,1024]{1,0:T(8,128)(2,1)}, u32[]{:S(2)}) copy-start(bf16[512,1024]{1,0:T(8,128)(2,1)} %get-tuple-element.5) | copy-start | bytes 3145732
